TPU v7x, 32 devices: a whole 2x2x4 slice. The times are simulated.
32 devices in a mesh: groups: 2 (over y), blk: 4 (over x, core), branch: 4 (over z).
Axes of the slice: x: 2, y: 2, z: 4, core: 2. Of those that a mesh axis runs over, the one named last changes fastest.
Arguments:
- queries: bfloat16 [128, 64, 128], P(('groups', 'blk', 'branch')), parts along dimension 0, may hold values from -128 to 128
- new_keys: bfloat16 [128, 8, 128], P(('groups', 'blk', 'branch')), parts along dimension 0, may hold values from -8 to 8
- fresh_token_values: bfloat16 [128, 8, 128], P(('groups', 'blk', 'branch')), parts along dimension 0, may hold values from -6 to 6
- prefix_keys: bfloat16 [16384, 8, 128], P(('groups', 'blk'), 'branch'), parts along dimension 0, may hold values from -4 to 4
- prefix_values: bfloat16 [16384, 8, 128], P(('groups', 'blk'), 'branch'), parts along dimension 0, may hold values from -6 to 6
- suffix_keys: bfloat16 [128, 512, 8, 128], P(('groups', 'blk'), None, 'branch'), parts along dimension 0, may hold values from -8 to 8
- suffix_values: bfloat16 [128, 512, 8, 128], P(('groups', 'blk'), None, 'branch'), parts along dimension 0, may hold values from -6 to 6
- suffix_lengths: int32 [128], P('groups'), parts along dimension 0, may hold values from 1 to 512, 20480 in all
- slot_branch: int32 [128], P('groups'), parts along dimension 0, may hold values from 0 to 63, as said below
Outputs:
- attended: bfloat16 [128, 64, 128], P(('groups', 'blk', 'branch')), parts along dimension 0
There are 2 independent parts, one for each index of `groups`. A program takes and returns all parts, laid end to end along the dimension named above; each array names one. Nothing has to cross between parts.
Inputs may be any that keep to these rules, and one draw needn't show every extreme that they name: slot_branch is a permutation that maps each aligned block of 16 slots onto the branches of the same block of 16 branches.
All inputs are finite; a program needn't handle non-finite values.
Results may differ from a plain program's by a relative error of at most 0.0045.
Values may be sent and summed in bfloat16 or wider, within the bound.
No kernel may reach another device: no remote copies, remote signals or barrier semaphores. Data moves between devices by JAX's collectives and lax.ppermute only.
A program may use at most 128 MiB of HBM per device.

v0:
```python
import math

import jax
import jax.numpy as jnp
from jax import lax
from jax.sharding import PartitionSpec as P

neg_large = -1e30


def advance(carried, scores, apply_values):
    out_sum, top_score, weight_sum = carried
    new_top = jnp.maximum(top_score, jnp.max(scores, axis=-1))
    rescale = jnp.exp(top_score - new_top)
    weights = jnp.exp(scores - new_top[..., None])
    weight_sum = weight_sum * rescale + jnp.sum(weights, axis=-1)
    out_sum = out_sum * rescale[..., None] + apply_values(weights.astype(jnp.bfloat16))
    return (out_sum, new_top, weight_sum)


def combine(first, second):
    top_score = jnp.maximum(first[1], second[1])
    scale_one = jnp.exp(first[1] - top_score)
    scale_two = jnp.exp(second[1] - top_score)
    out_sum = first[0] * scale_one[..., None] + second[0] * scale_two[..., None]
    weight_sum = first[2] * scale_one + second[2] * scale_two
    return (out_sum, top_score, weight_sum)


def empty_state(rows, kv_heads, group, head_dim):
    return (
        jnp.zeros((rows, kv_heads, group, head_dim), jnp.float32),
        jnp.full((rows, kv_heads, group), neg_large, jnp.float32),
        jnp.zeros((rows, kv_heads, group), jnp.float32),
    )


def attend_prefix(carried, query_rows, key_rows, value_rows):
    total = key_rows.shape[0]
    kv_heads, head_dim = (key_rows.shape[1], key_rows.shape[2])
    width = math.gcd(total, 512)
    count = total // width
    score_scale = 1.0 / math.sqrt(head_dim)
    key_blocks = key_rows.reshape(count, width, kv_heads, head_dim)
    value_blocks = value_rows.reshape(count, width, kv_heads, head_dim)

    def step(state, blocks):
        key_block, value_block = blocks
        scores = (
            jnp.einsum("rkgd,nkd->rkgn", query_rows, key_block, preferred_element_type=jnp.float32)
            * score_scale
        )

        def apply_values(weights):
            return jnp.einsum(
                "rkgn,nkd->rkgd", weights, value_block, preferred_element_type=jnp.float32
            )

        return (advance(state, scores, apply_values), None)

    final_output, _ = lax.scan(step, carried, (key_blocks, value_blocks))
    return final_output


def attend_suffix(
    slot_queries, slot_new_keys, slot_new_values, suffix_keys, suffix_values, slot_lengths
):
    head_dim = slot_queries.shape[3]
    score_scale = 1.0 / math.sqrt(head_dim)
    own_score = (
        jnp.einsum("skgd,skd->skg", slot_queries, slot_new_keys, preferred_element_type=jnp.float32)
        * score_scale
    )
    own_value = jnp.broadcast_to(
        slot_new_values.astype(jnp.float32)[:, :, None, :], slot_queries.shape
    )
    carried = (own_value, own_score, jnp.ones_like(own_score))
    scores = (
        jnp.einsum("skgd,snkd->skgn", slot_queries, suffix_keys, preferred_element_type=jnp.float32)
        * score_scale
    )
    positions = jnp.arange(suffix_keys.shape[1], dtype=jnp.int32)
    valid_mask = positions[None, :] < slot_lengths[:, None]
    scores = jnp.where(valid_mask[:, None, None, :], scores, neg_large)

    def apply_values(weights):
        return jnp.einsum(
            "skgn,snkd->skgd", weights, suffix_values, preferred_element_type=jnp.float32
        )

    return advance(carried, scores, apply_values)


def per_device(
    queries,
    new_keys,
    fresh_token_values,
    prefix_keys,
    prefix_values,
    suffix_keys,
    suffix_values,
    suffix_lengths,
    slot_branch,
):
    head_rows, nearby_keys, nearby_values = (
        lax.all_to_all(queries, "branch", split_axis=1, concat_axis=0, tiled=True),
        lax.all_to_all(new_keys, "branch", split_axis=1, concat_axis=0, tiled=True),
        lax.all_to_all(fresh_token_values, "branch", split_axis=1, concat_axis=0, tiled=True),
    )
    rows = head_rows.shape[0]
    local_key_value = nearby_keys.shape[1]
    head_dim = nearby_keys.shape[2]
    group = head_rows.shape[1] // local_key_value
    query_rows = head_rows.reshape(rows, local_key_value, group, head_dim)
    block_index = lax.axis_index("blk")
    first_row = block_index * rows
    pieces = lax.all_gather(head_rows, "blk", axis=0, tiled=True)
    count = pieces.shape[0]
    fresh = attend_prefix(
        empty_state(count, local_key_value, group, head_dim),
        pieces.reshape(count, local_key_value, group, head_dim),
        prefix_keys,
        prefix_values,
    )
    full_state = tuple((member for member in fresh))
    out_parts, top_parts, sum_parts = (
        lax.all_to_all(full_state[0][None], "blk", split_axis=1, concat_axis=0, tiled=True),
        lax.all_to_all(full_state[1][None], "blk", split_axis=1, concat_axis=0, tiled=True),
        lax.all_to_all(full_state[2][None], "blk", split_axis=1, concat_axis=0, tiled=True),
    )
    top_score = jnp.max(top_parts, axis=0)
    rescale = jnp.exp(top_parts - top_score[None])
    prefix_state = (
        jnp.sum(out_parts * rescale[..., None], axis=0),
        top_score,
        jnp.sum(sum_parts * rescale, axis=0),
    )
    local_slot_index = lax.dynamic_slice_in_dim(slot_branch, first_row, rows) - first_row
    length_block = lax.dynamic_slice_in_dim(suffix_lengths, first_row, rows)
    picker = local_slot_index[:, None] == jnp.arange(rows, dtype=jnp.int32)[None, :]
    select_halfway = picker.astype(jnp.bfloat16)
    slot_queries = jnp.einsum(
        "sb,bkgd->skgd", select_halfway, query_rows, preferred_element_type=jnp.float32
    ).astype(jnp.bfloat16)
    slot_new_keys = jnp.einsum(
        "qx,xuy->quy", select_halfway, nearby_keys, preferred_element_type=jnp.float32
    ).astype(jnp.bfloat16)
    slot_new_values = jnp.einsum(
        "qx,xuy->quy", select_halfway, nearby_values, preferred_element_type=jnp.float32
    ).astype(jnp.bfloat16)
    slot_lengths = jnp.sum(jnp.where(picker, length_block[None, :], 0), axis=1)
    slot_state = attend_suffix(
        slot_queries, slot_new_keys, slot_new_values, suffix_keys, suffix_values, slot_lengths
    )
    pick_wide = picker.astype(jnp.float32)
    suffix_state = (
        jnp.einsum("sb,skgd->bkgd", pick_wide, slot_state[0], precision=lax.Precision.HIGHEST),
        jnp.einsum("sb,skg->bkg", pick_wide, slot_state[1], precision=lax.Precision.HIGHEST),
        jnp.einsum("sb,skg->bkg", pick_wide, slot_state[2], precision=lax.Precision.HIGHEST),
    )
    out_sum, top_score, weight_sum = combine(prefix_state, suffix_state)
    final_output = (out_sum / weight_sum[..., None]).astype(jnp.bfloat16)
    final_output = final_output.reshape(rows, local_key_value * group, head_dim)
    return lax.all_to_all(final_output, "branch", split_axis=0, concat_axis=1, tiled=True)


def solution(mesh):
    return jax.shard_map(
        per_device,
        mesh=mesh,
        in_specs=(
            P(("groups", "blk", "branch"), None, None),
            P(("groups", "blk", "branch"), None, None),
            P(("groups", "blk", "branch"), None, None),
            P(("groups", "blk"), "branch", None),
            P(("groups", "blk"), "branch", None),
            P(("groups", "blk"), None, "branch", None),
            P(("groups", "blk"), None, "branch", None),
            P("groups"),
            P("groups"),
        ),
        out_specs=P(("groups", "blk", "branch"), None, None),
        check_vma=False,
    )
```

profile of v0, /device:TPU:0, one launch (start us, length us, event | category | flops | bytes accessed | tf_op | source)
XLA Modules:
  0.0 90.6 jit_solution(9462983046000429940)
XLA Ops:
  0.0 1.3 %copy.68 = bf16[4,8,128]{2,0,1:T(4,128)(2,1)} copy(bf16[4,8,128]{2,1,0:T(8,128)(2,1)} %param.13) | data formatting | bytes 16384 | tf_op args[2]
  1.3 6.3 %all-to-all-start.4 = ((bf16[4,8,128]{2,0,1:T(4,128)(2,1)}), bf16[4,8,128]{2,0,1:T(4,128)(2,1)S(1)}, u32[]{:S(2)}, u32[]{:S(2)}) async-start(bf16[4,8,128]{2,0,1:T(4,128)(2,1)} %copy.68), calls=%async_computation.4 | async-start | bytes 16384 | tf_op jit(solution)/shard_map/all_to_all | solution.py:108
  7.6 0.7 dynamic-slice_subtract_fusion
  8.3 0.7 dynamic_slice.14
  9.3 1.3 %copy.60 = bf16[4,8,128]{2,0,1:T(4,128)(2,1)} copy(bf16[4,8,128]{2,1,0:T(8,128)(2,1)} %param.12) | data formatting | bytes 16384 | tf_op args[1]
  10.6 1.5 %copy.53 = bf16[4,64,128]{2,0,1:T(4,128)(2,1)} copy(bf16[4,64,128]{2,1,0:T(8,128)(2,1)} %param.11) | data formatting | bytes 131072 | tf_op args[0]
  12.2 1.1 %all-to-all-done.4 = bf16[4,8,128]{2,0,1:T(4,128)(2,1)S(1)} async-done(((bf16[4,8,128]{2,0,1:T(4,128)(2,1)}), bf16[4,8,128]{2,0,1:T(4,128)(2,1)S(1)}, u32[]{:S(2)}, u32[]{:S(2)}) %all-to-all-start.4) | async-done | bytes 8224 | tf_op jit(solution)/shard_map/all_to_all | solution.py:108
  13.2 4.0 %all-to-all-start.3 = ((bf16[4,8,128]{2,0,1:T(4,128)(2,1)}), bf16[4,8,128]{2,0,1:T(4,128)(2,1)S(1)}, u32[]{:S(2)}, u32[]{:S(2)}) async-start(bf16[4,8,128]{2,0,1:T(4,128)(2,1)} %copy.60), calls=%async_computation.3 | async-start | bytes 16384 | tf_op jit(solution)/shard_map/all_to_all | solution.py:107
  17.5 5.4 %all-to-all-done.3 = bf16[4,8,128]{2,0,1:T(4,128)(2,1)S(1)} async-done(((bf16[4,8,128]{2,0,1:T(4,128)(2,1)}), bf16[4,8,128]{2,0,1:T(4,128)(2,1)S(1)}, u32[]{:S(2)}, u32[]{:S(2)}) %all-to-all-start.3) | async-done | bytes 8224 | tf_op jit(solution)/shard_map/all_to_all | solution.py:107
  22.8 3.3 %all-to-all-start = ((bf16[4,64,128]{2,0,1:T(4,128)(2,1)}), bf16[4,64,128]{2,0,1:T(4,128)(2,1)S(1)}, u32[]{:S(2)}, u32[]{:S(2)}) async-start(bf16[4,64,128]{2,0,1:T(4,128)(2,1)} %copy.53), calls=%async_computation | async-start | bytes 131072 | tf_op jit(solution)/shard_map/all_to_all | solution.py:106
  26.3 5.5 %all-to-all-done = bf16[4,64,128]{2,0,1:T(4,128)(2,1)S(1)} async-done(((bf16[4,64,128]{2,0,1:T(4,128)(2,1)}), bf16[4,64,128]{2,0,1:T(4,128)(2,1)S(1)}, u32[]{:S(2)}, u32[]{:S(2)}) %all-to-all-start) | async-done | bytes 65568 | tf_op jit(solution)/shard_map/all_to_all | solution.py:106
  31.9 0.2 convolution_convert_fusion
  32.1 5.8 %all_gather.3 = bf16[64,16,128]{2,0,1:T(8,128)(2,1)S(1)} all-gather(bf16[16,16,128]{2,0,1:T(8,128)(2,1)S(1)} %bitcast.122), channel_id=1, replica_groups=mesh['groups'=2,'blk'=4,'branch'=4] {'blk'}, dimensions={0}, use_global_device_ids=true | all-gather | bytes 327680 | tf_op jit(solution)/shard_map/all_gather | solution.py:117
  37.9 13.4 %while.15 = (s32[]{:T(128)}, f32[64,2,8,128]{3,0,2,1:T(8,128)S(1)}, f32[64,2,8]{0,2,1:T(8,128)S(1)}, f32[64,2,8]{0,2,1:T(8,128)S(1)}, bf16[4,512,2,128]{3,2,1,0:...) while((s32[]{:T(128)}, f32[64,2,8,128]{3,0,2,1:T(8,128)S(1)}, ...), condition=%wide.region_3.4_spmd.clone, body=%wide.region_0.3_spmd.clone.sunk | while | flops 273028096 | bytes 9240693 | solution.py:61
  37.9 1.4 %constant_dynamic-slice_fusion.3 = (bf16[1,512,2,128]{3,2,1,0:T(2,128)(2,1)S(1)}, bf16[1,512,2,128]{3,2,1,0:T(2,128)(2,1)S(1)}) fusion(bf16[4,512,2,128]{3,2,1,0:T(2,128)(2,1)} %get-tuple-element.199, s32[]{:T(128)S(6)} %copy.133, bf16[4,512,2,128]{3,2,1,0:T(2,128)(2,1)} %get-tuple-element.197), kind=kLoop, calls=%fused_computation.17.clone.1 | loop fusion | bytes 1048580 | tf_op jit(solution)/shard_map/while/body/jit(dynamic_index_in_dim)/dynamic_slice | solution.py:61
  39.3 0.5 bitcast_reduce_fusion.2
  39.8 0.6 fusion.68
  40.4 0.8 fusion.70
  41.2 1.4 %constant_dynamic-slice_fusion.3 = (bf16[1,512,2,128]{3,2,1,0:T(2,128)(2,1)S(1)}, bf16[1,512,2,128]{3,2,1,0:T(2,128)(2,1)S(1)}) fusion(bf16[4,512,2,128]{3,2,1,0:T(2,128)(2,1)} %get-tuple-element.199, s32[]{:T(128)S(6)} %copy.133, bf16[4,512,2,128]{3,2,1,0:T(2,128)(2,1)} %get-tuple-element.197), kind=kLoop, calls=%fused_computation.17.clone.1 | loop fusion | bytes 1048580 | tf_op jit(solution)/shard_map/while/body/jit(dynamic_index_in_dim)/dynamic_slice | solution.py:61
  42.6 0.5 bitcast_reduce_fusion.2
  43.1 0.6 fusion.68
  43.7 0.8 fusion.70
  44.5 1.4 %constant_dynamic-slice_fusion.3 = (bf16[1,512,2,128]{3,2,1,0:T(2,128)(2,1)S(1)}, bf16[1,512,2,128]{3,2,1,0:T(2,128)(2,1)S(1)}) fusion(bf16[4,512,2,128]{3,2,1,0:T(2,128)(2,1)} %get-tuple-element.199, s32[]{:T(128)S(6)} %copy.133, bf16[4,512,2,128]{3,2,1,0:T(2,128)(2,1)} %get-tuple-element.197), kind=kLoop, calls=%fused_computation.17.clone.1 | loop fusion | bytes 1048580 | tf_op jit(solution)/shard_map/while/body/jit(dynamic_index_in_dim)/dynamic_slice | solution.py:61
  45.9 0.5 bitcast_reduce_fusion.2
  46.5 0.6 fusion.68
  47.1 0.8 fusion.70
  47.9 1.4 %constant_dynamic-slice_fusion.3 = (bf16[1,512,2,128]{3,2,1,0:T(2,128)(2,1)S(1)}, bf16[1,512,2,128]{3,2,1,0:T(2,128)(2,1)S(1)}) fusion(bf16[4,512,2,128]{3,2,1,0:T(2,128)(2,1)} %get-tuple-element.199, s32[]{:T(128)S(6)} %copy.133, bf16[4,512,2,128]{3,2,1,0:T(2,128)(2,1)} %get-tuple-element.197), kind=kLoop, calls=%fused_computation.17.clone.1 | loop fusion | bytes 1048580 | tf_op jit(solution)/shard_map/while/body/jit(dynamic_index_in_dim)/dynamic_slice | solution.py:61
  49.3 0.5 bitcast_reduce_fusion.2
  49.8 0.6 fusion.68
  50.4 0.8 fusion.70
  51.3 0.7 reshape.83
  52.1 3.2 %all-to-all-start.5 = ((f32[4,1,256]{2,1,0:T(1,128)}), f32[4,1,256]{2,1,0:T(1,128)S(1)}, u32[]{:S(2)}, u32[]{:S(2)}) async-start(f32[4,1,256]{2,1,0:T(1,128)} %reshape.83), calls=%async_computation.5 | async-start | bytes 8192 | tf_op jit(solution)/shard_map/all_to_all | solution.py:129
  55.6 3.5 %fusion.56 = (f32[16,2,8]{2,1,0:T(2,128)S(1)}, f32[16,2,8,512]{3,2,1,0:T(8,128)S(1)}) fusion(bf16[16,512,2,128]{3,2,1,0:T(2,128)(2,1)} %param.16, bf16[16,2,8,128]{3,0,2,1:T(8,128)(2,1)S(1)} %convolution_convert_fusion, pred[16,512]{1,0:T(8,128)(4,1)S(1)} %iota_compare_fusion), kind=kOutput, calls=%fused_computation.75 | convolution fusion | flops 33947392 | bytes 4793344 | tf_op jit(solution)/shard_map/skgd,snkd->skgn/dot_general | solution.py:79
  59.1 0.2 fusion.30
  59.4 0.7 reshape.81
  60.1 3.3 %all-to-all-start.2 = ((f32[4,1,256]{2,1,0:T(1,128)}), f32[4,1,256]{2,1,0:T(1,128)S(1)}, u32[]{:S(2)}, u32[]{:S(2)}) async-start(f32[4,1,256]{2,1,0:T(1,128)} %reshape.81), calls=%async_computation.2 | async-start | bytes 8192 | tf_op jit(solution)/shard_map/all_to_all | solution.py:128
  63.4 2.9 %fusion.20 = f32[16,2,8,128]{3,2,1,0:T(8,128)S(1)} fusion(bf16[16,512,2,128]{3,2,1,0:T(2,128)(2,1)} %param.17, f32[16,2,8,512]{3,2,1,0:T(8,128)S(1)} %get-tuple-element.119, f32[16,2,8]{2,1,0:T(2,128)S(1)} %multiply_maximum_fusion, f32[16,2,8]{2,1,0:T(2,128)S(1)} %get-tuple-element.111, f32[16,2,128]{2,1,0:T(2,128)S(1)} %copy.70), kind=kOutput, calls=%fused_computation.26 | convolution fusion | flops 33882112 | bytes 4868096 | tf_op jit(solution)/shard_map/skgn,snkd->skgd/dot_general | solution.py:87
  66.5 1.1 %copy.124 = f32[64,2,8,128]{3,2,1,0:T(8,128)} copy(f32[64,2,8,128]{3,0,2,1:T(8,128)S(1)} %get-tuple-element.44) | data formatting | bytes 1048576 | tf_op jit(solution)/shard_map/while | solution.py:61
  67.6 0.5 broadcast.67
  68.1 0.7 reduce
  68.9 3.5 %all-to-all-start.1 = ((f32[1,64,2,8,128]{4,3,2,0,1:T(8,128)}), f32[1,64,2,8,128]{4,3,2,0,1:T(8,128)S(1)}, u32[]{:S(2)}, u32[]{:S(2)}) async-start(f32[1,64,2,8,128]{4,3,2,0,1:T(8,128)} %bitcast.100), calls=%async_computation.1 | async-start | bytes 1048576 | tf_op jit(solution)/shard_map/all_to_all | solution.py:127
  72.4 0.7 reduce.1
  73.5 0.2 fusion.39
  73.9 7.3 %all-to-all-done.1 = f32[1,64,2,8,128]{4,3,2,0,1:T(8,128)S(1)} async-done(((f32[1,64,2,8,128]{4,3,2,0,1:T(8,128)}), f32[1,64,2,8,128]{4,3,2,0,1:T(8,128)S(1)}, u32[]{:S(2)}, u32[]{:S(2)}) %all-to-all-start.1) | async-done | bytes 524320 | tf_op jit(solution)/shard_map/all_to_all | solution.py:127
  81.2 0.2 multiply_reduce_fusion
  81.4 0.3 fusion.25
  81.8 8.1 %all_to_all.108 = bf16[16,16,128]{2,1,0:T(8,128)(2,1)S(1)} all-to-all(bf16[16,16,128]{2,1,0:T(8,128)(2,1)S(1)} %copy.77), channel_id=1, replica_groups=mesh['groups'=2,'blk'=4,'branch'=4] {'branch'}, dimensions={0} | all-to-all | bytes 131072 | tf_op jit(solution)/shard_map/all_to_all | solution.py:164
  89.9 0.6 copy.78
  (42 shorter events, 2.1 us)
Async XLA Ops:
  1.3 11.9 %all-to-all-start.4 = ((bf16[4,8,128]{2,0,1:T(4,128)(2,1)}), bf16[4,8,128]{2,0,1:T(4,128)(2,1)S(1)}, u32[]{:S(2)}, u32[]{:S(2)}) async-start(bf16[4,8,128]{2,0,1:T(4,128)(2,1)} %copy.68), calls=%async_computation.4 | async-start | bytes 16384 | tf_op jit(solution)/shard_map/all_to_all | solution.py:108
  13.2 9.6 %all-to-all-start.3 = ((bf16[4,8,128]{2,0,1:T(4,128)(2,1)}), bf16[4,8,128]{2,0,1:T(4,128)(2,1)S(1)}, u32[]{:S(2)}, u32[]{:S(2)}) async-start(bf16[4,8,128]{2,0,1:T(4,128)(2,1)} %copy.60), calls=%async_computation.3 | async-start | bytes 16384 | tf_op jit(solution)/shard_map/all_to_all | solution.py:107
  22.8 9.0 %all-to-all-start = ((bf16[4,64,128]{2,0,1:T(4,128)(2,1)}), bf16[4,64,128]{2,0,1:T(4,128)(2,1)S(1)}, u32[]{:S(2)}, u32[]{:S(2)}) async-start(bf16[4,64,128]{2,0,1:T(4,128)(2,1)} %copy.53), calls=%async_computation | async-start | bytes 131072 | tf_op jit(solution)/shard_map/all_to_all | solution.py:106
  52.1 8.1 %all-to-all-start.5 = ((f32[4,1,256]{2,1,0:T(1,128)}), f32[4,1,256]{2,1,0:T(1,128)S(1)}, u32[]{:S(2)}, u32[]{:S(2)}) async-start(f32[4,1,256]{2,1,0:T(1,128)} %reshape.83), calls=%async_computation.5 | async-start | bytes 8192 | tf_op jit(solution)/shard_map/all_to_all | solution.py:129
  60.1 8.8 %all-to-all-start.2 = ((f32[4,1,256]{2,1,0:T(1,128)}), f32[4,1,256]{2,1,0:T(1,128)S(1)}, u32[]{:S(2)}, u32[]{:S(2)}) async-start(f32[4,1,256]{2,1,0:T(1,128)} %reshape.81), calls=%async_computation.2 | async-start | bytes 8192 | tf_op jit(solution)/shard_map/all_to_all | solution.py:128
  68.9 12.3 %all-to-all-start.1 = ((f32[1,64,2,8,128]{4,3,2,0,1:T(8,128)}), f32[1,64,2,8,128]{4,3,2,0,1:T(8,128)S(1)}, u32[]{:S(2)}, u32[]{:S(2)}) async-start(f32[1,64,2,8,128]{4,3,2,0,1:T(8,128)} %bitcast.100), calls=%async_computation.1 | async-start | bytes 1048576 | tf_op jit(solution)/shard_map/all_to_all | solution.py:127
where the time goes:
time: 91.4 us; the launch traced here: 90.6 us
  starting transfers between devices  23.6 us (26%)
  waiting for transfers between devices  19.2 us (21%)
  local copies, waits for them, and re-layouts  15 us (16%)
  blocking collectives  13.9 us (15%)
  matrix products  13 us (14%)
  other arithmetic  5.34 us (6%)
    all_to_all x1, blocking collectives, per_device(): lax.all_to_all(final_output, 'branch', split_axis=0, concat_axis=1, tiled...  8.11 us
    all_to_all x1, waiting for transfers between devices, per_device(): lax.all_to_all(full_state[0][None], 'blk', split_axis=1, concat_axis=0, t...  7.31 us
    all_to_all x1, starting transfers between devices, per_device(): lax.all_to_all(fresh_token_values, 'branch', split_axis=1, concat_axis=0,...  6.32 us
    unnamed x9, local copies, waits for them, and re-layouts  5.89 us
    all_gather x1, blocking collectives, per_device(): pieces = lax.all_gather(head_rows, 'blk', axis=0, tiled=True)  5.79 us
    dynamic_slice x4, local copies, waits for them, and re-layouts, attend_prefix(): final_output, _ = lax.scan(step, carried, (key_blocks, value_blocks))  5.58 us
    all_to_all x1, waiting for transfers between devices, per_device(): lax.all_to_all(queries, 'branch', split_axis=1, concat_axis=0, tiled=True)  5.51 us
    all_to_all x1, waiting for transfers between devices, per_device(): lax.all_to_all(new_keys, 'branch', split_axis=1, concat_axis=0, tiled=True)  5.38 us
  transfers between devices with their start and end apart: 6, of which 4 were waited for; matrix products, arithmetic and copies ran while one was open for 18% of the time, Pallas kernels for 0%

commit v1 on v0

v1 whole, which is shorter than its diff:
```python
import functools
import math

import jax
import jax.numpy as jnp
from jax import lax
from jax.experimental import pallas as pl
from jax.experimental.pallas import tpu as pltpu
from jax.sharding import PartitionSpec as P

NEG = -1e30
LOG2E = 1.4426950408889634
F32 = jnp.float32
BF16 = jnp.bfloat16
VM = pl.BlockSpec(memory_space=pltpu.VMEM)
SM = pl.BlockSpec(memory_space=pltpu.SMEM)
ANY = pl.BlockSpec(memory_space=pl.ANY)
NT = (((1,), (1,)), ((), ()))


def ceil_to(value, unit):
    return -(-value // unit) * unit


def partner(index, step, count):
    if count & (count - 1) == 0:
        return index ^ step
    return (index + step) % count


def back(step, count):
    return step if count & (count - 1) == 0 else (count - step) % count


def step_to(me, other, count):
    if count & (count - 1) == 0:
        return me ^ other
    return lax.rem(me - other + count, count)


def call(kernel, name, out_shape, inputs, in_specs, scratch=(), vmem=16 << 20, flops=0, moved=0, out_specs=None):
    many = isinstance(out_shape, (list, tuple))
    return pl.pallas_call(
        kernel,
        name=name,
        out_shape=out_shape,
        in_specs=in_specs,
        out_specs=out_specs if out_specs is not None else ([VM] * len(out_shape) if many else VM),
        scratch_shapes=list(scratch),
        compiler_params=pltpu.CompilerParams(vmem_limit_bytes=vmem),
        cost_estimate=pl.CostEstimate(flops=flops, bytes_accessed=moved, transcendentals=0),
    )(*inputs)


def pack_kernel(nz, local, group, pad, q_ref, k_ref, v_ref, *out_refs):
    me = lax.axis_index("branch")
    nb = q_ref.shape[0]
    head_dim = q_ref.shape[-1]
    new_k = k_ref[...].astype(F32)
    new_v = v_ref[...].astype(F32)
    for step in range(nz):
        peer = partner(me, step, nz)
        q = q_ref[:, peer].astype(F32)
        parts = [
            q[:, kl * group : (kl + 1) * group].reshape(nb * group, head_dim) for kl in range(local)
        ]
        rows_k, rows_v = new_k[:, :local], new_v[:, :local]
        for z in range(1, nz):
            here = peer == z
            rows_k = jnp.where(here, new_k[:, z * local : (z + 1) * local], rows_k)
            rows_v = jnp.where(here, new_v[:, z * local : (z + 1) * local], rows_v)
        for rows in (rows_k, rows_v):
            for kl in range(local):
                parts += [rows[b, kl : kl + 1] for b in range(nb)]
        if pad:
            parts.append(jnp.zeros((pad, head_dim), F32))
        out_refs[step][...] = jnp.concatenate(parts, axis=0).astype(BF16)


def join_kernel(*refs):
    for step, ref in enumerate(refs[:-1]):
        refs[-1][step] = ref[...]


def split_kernel(local, k_ref, v_ref, ko_ref, vo_ref, wide):
    chunk = wide.shape[0]
    rows = chunk // local
    for src, dst in ((k_ref, ko_ref), (v_ref, vo_ref)):
        for at in range(src.shape[0] // chunk):
            wide[...] = src[at * chunk : (at + 1) * chunk].astype(F32)
            for kl in range(local):
                dst[kl, at * rows : (at + 1) * rows] = wide[pl.ds(kl, rows, stride=local)].astype(BF16)


def suffix_kernel(
    nz, local, group, scale, joined_ref, slot_ref, len_ref, keys, values, out_ref, lse_ref,
    kbuf, vbuf, qwide, scores, probs, ksem, vsem
):
    slots, width, head_dim = kbuf.shape
    block = lax.axis_index("blk")
    me = lax.axis_index("branch")
    copies_k = [pltpu.make_async_copy(keys.at[c], kbuf.at[c], ksem.at[c]) for c in range(slots)]
    copies_v = [pltpu.make_async_copy(values.at[c], vbuf.at[c], vsem.at[c]) for c in range(slots)]
    for copy in copies_k + copies_v:
        copy.start()
    nb = slots // nz
    qrows = local * nb * group
    for step in range(nz):
        qwide[step * qrows : (step + 1) * qrows] = joined_ref[step, :qrows].astype(F32)
    heads = local * group
    column = lax.broadcasted_iota(jnp.int32, (heads, width), 1)
    row = lax.broadcasted_iota(jnp.int32, (heads, width), 0)
    own_head = lax.rem(column, local) == row // group

    def places(c):
        branch = slot_ref[block * slots + c]
        length = len_ref[branch]
        branch = branch - block * slots
        step = step_to(me, branch // nb, nz)
        at = step * qrows + lax.rem(branch, nb) * group
        return [pl.multiple_of(at + kl * nb * group, 8) for kl in range(local)], length

    for c in range(slots):
        at, length = places(c)
        q = jnp.concatenate([qwide[pl.ds(a, group)] for a in at], axis=0).astype(BF16)
        copies_k[c].wait()
        s = lax.dot_general(q, kbuf[c], NT, preferred_element_type=F32)
        scores[c * heads : (c + 1) * heads] = jnp.where(
            own_head & (column < length * local), s, NEG
        )
    s = scores[...]
    top = jnp.max(s, axis=-1, keepdims=True)
    weights = jnp.exp2((s - top) * (scale * LOG2E))
    total = jnp.sum(weights, axis=-1, keepdims=True)
    probs[...] = weights.astype(BF16)
    lse = top * scale + jnp.log(total)
    inverse = 1.0 / total
    for c in range(slots):
        at, _ = places(c)
        copies_v[c].wait()
        o = jnp.dot(probs[c * heads : (c + 1) * heads], vbuf[c], preferred_element_type=F32)
        o = o * inverse[c * heads : (c + 1) * heads]
        for kl in range(local):
            lo, hi = kl * group, (kl + 1) * group
            out_ref[pl.ds(at[kl], group)] = o[lo:hi]
            lse_ref[pl.ds(at[kl], group)] = jnp.broadcast_to(
                lse[c * heads + lo : c * heads + hi], (group, head_dim)
            )


def column_to_rows(column, lanes):
    count = column.shape[0] // lanes
    eye = lax.broadcasted_iota(jnp.int32, (lanes, lanes), 0) == lax.broadcasted_iota(
        jnp.int32, (lanes, lanes), 1
    )
    rows = [
        jnp.sum(jnp.where(eye, column[i * lanes : (i + 1) * lanes], 0.0), axis=0, keepdims=True)
        for i in range(count)
    ]
    return jnp.concatenate(rows, axis=0)


def rows_to_column(rows):
    lanes = rows.shape[1]
    eye = lax.broadcasted_iota(jnp.int32, (lanes, lanes), 0) == lax.broadcasted_iota(
        jnp.int32, (lanes, lanes), 1
    )
    parts = [
        jnp.sum(jnp.where(eye, rows[i : i + 1], 0.0), axis=1, keepdims=True)
        for i in range(rows.shape[0])
    ]
    return jnp.concatenate(parts, axis=0)


def encode(out, lse):
    lanes = out.shape[1]
    rows = column_to_rows(lse, lanes)
    high = rows.astype(BF16).astype(F32)
    middle = (rows - high).astype(BF16).astype(F32)
    low = rows - high - middle
    tail = [high, middle, low]
    used = 3 * rows.shape[0]
    tail.append(jnp.zeros((ceil_to(used, 16) - used, lanes), F32))
    return jnp.concatenate([out] + tail, axis=0).astype(BF16)


def decode(payload, count):
    wide = payload.astype(F32)
    lanes = wide.shape[1]
    n = count // lanes
    rows = wide[count : count + n] + wide[count + n : count + 2 * n] + wide[count + 2 * n : count + 3 * n]
    return wide[:count], rows_to_column(rows)


def merge(parts):
    top = parts[0][1]
    for _, lse in parts[1:]:
        top = jnp.maximum(top, lse)
    weights = [jnp.exp2((lse - top) * LOG2E) for _, lse in parts]
    total = sum(weights[1:], weights[0])
    out = parts[0][0] * weights[0]
    for (o, _), w in zip(parts[1:], weights[1:]):
        out = out + o * w
    return out * (1.0 / total), top + jnp.log(total)


def prefix_partial(q_refs, k_ref, v_ref, local, qrows, scale):
    part = qrows // local
    steps = q_refs[0].shape[0]
    outs, lses = [], []
    for kl in range(local):
        q = jnp.concatenate(
            [ref[z, kl * part : (kl + 1) * part] for ref in q_refs for z in range(steps)], axis=0
        )
        s = lax.dot_general(q, k_ref[kl], NT, preferred_element_type=F32)
        top = jnp.max(s, axis=-1, keepdims=True)
        weights = jnp.exp2((s - top) * (scale * LOG2E))
        total = jnp.sum(weights, axis=-1, keepdims=True)
        o = jnp.dot(weights.astype(BF16), v_ref[kl], preferred_element_type=F32)
        outs.append(o * (1.0 / total))
        lses.append(top * scale + jnp.log(total))
    results = []
    for i in range(len(q_refs)):
        pieces = [(i * steps + z) * part for z in range(steps)]
        results.append(
            tuple(
                jnp.concatenate([a[p : p + part] for p in pieces for a in arrays], axis=0)
                for arrays in (outs, lses)
            )
        )
    return results


def prefix_kernel(count, merged, local, qrows, scale, *refs):
    q_refs, (k_ref, v_ref) = refs[:count], refs[count : count + 2]
    others = refs[count + 2 : count + 2 + (count if merged else 0)]
    outs = refs[-count:]
    results = prefix_partial(q_refs, k_ref, v_ref, local, qrows, scale)
    for i, (o, lse) in enumerate(results):
        if merged:
            o, lse = merge([(o, lse), decode(others[i][...], o.shape[0])])
        outs[i][...] = encode(o, lse)


def prefix_own_kernel(local, qrows, scale, q_ref, k_ref, v_ref, o_ref, lse_ref):
    ((o, lse),) = prefix_partial([q_ref], k_ref, v_ref, local, qrows, scale)
    o_ref[...] = o
    lse_ref[...] = jnp.broadcast_to(lse, o.shape)


def final_kernel(count, local, group, scale, joined_ref, so_ref, sl_ref, po_ref, pl_ref, *refs):
    others, outs = refs[:count], refs[count:]
    nz = joined_ref.shape[0]
    rows, head_dim = po_ref.shape
    qrows = rows // nz
    nb = qrows // (local * group)
    part = nb * local
    own_score, own_value = [], []
    for step in range(nz):
        q = joined_ref[step, :qrows].astype(F32)
        tail = joined_ref[step, qrows:].astype(F32)
        k = jnp.concatenate(
            [jnp.broadcast_to(tail[i : i + 1], (group, head_dim)) for i in range(part)], axis=0
        )
        own_value += [
            jnp.broadcast_to(tail[i : i + 1], (group, head_dim)) for i in range(part, 2 * part)
        ]
        own_score.append(jnp.sum(q * k, axis=1, keepdims=True) * scale)
    parts = [
        (jnp.concatenate(own_value, axis=0), jnp.concatenate(own_score, axis=0)),
        (so_ref[...], sl_ref[:, :1]),
        (po_ref[...], pl_ref[:, :1]),
    ]
    parts += [decode(ref[...], rows) for ref in others]
    out, _ = merge(parts)
    for step in range(nz):
        outs[step][...] = out[step * qrows : (step + 1) * qrows].astype(BF16)


def unpack_kernel(nz, local, group, *refs):
    pieces, out_ref = refs[:nz], refs[nz]
    me = lax.axis_index("branch")
    nb = out_ref.shape[0]
    for step in range(nz):
        peer = partner(me, step, nz)
        wide = pieces[step][...].astype(F32)
        for b in range(nb):
            rows = [wide[(kl * nb + b) * group : (kl * nb + b + 1) * group] for kl in range(local)]
            out_ref[b, peer] = jnp.concatenate(rows, axis=0).astype(BF16)


def per_device(
    nz, nblk, queries, new_keys, fresh_token_values, prefix_keys, prefix_values, suffix_keys,
    suffix_values, suffix_lengths, slot_branch
):
    nb, heads, head_dim = queries.shape
    positions, local = prefix_keys.shape[:2]
    group = heads // new_keys.shape[1]
    slots, suffix = suffix_keys.shape[:2]
    scale = 1.0 / math.sqrt(head_dim)
    qrows = local * nb * group
    used = qrows + 2 * nb * local
    padded = ceil_to(used, 16)
    rows = nz * qrows
    nc = 2 if nblk % 2 == 0 else 1
    nx = nblk // nc

    def shift(x, axis, step, count, unit=1, size=None):
        size = count * unit if size is None else size
        pairs = []
        for i in range(size):
            inner, outer = i % unit, i // unit
            low = outer % count
            other = outer - low + partner(low, step, count)
            pairs.append((i, other * unit + inner))
        return lax.ppermute(x, axis, pairs)

    def along_core(x):
        return shift(x, "blk", 1, 2, 1, nblk)

    def along_x(x, step):
        return shift(x, "blk", step, nx, nc, nblk)

    payloads = call(
        functools.partial(pack_kernel, nz, local, group, padded - used),
        "pack",
        [jax.ShapeDtypeStruct((padded, head_dim), BF16)] * nz,
        (queries.reshape(nb, nz, heads // nz, head_dim), new_keys, fresh_token_values),
        [VM] * 3,
        moved=queries.size * 4,
    )
    arrived = [payloads[0]] + [
        shift(payloads[step], "branch", step, nz) for step in range(nz - 1, 0, -1)
    ][::-1]
    if local > 1:
        chunk = math.gcd(positions * local, 1024)
        flat = (positions * local, head_dim)
        keys, values = call(
            functools.partial(split_kernel, local),
            "split",
            [jax.ShapeDtypeStruct((local, positions, head_dim), BF16)] * 2,
            (prefix_keys.reshape(flat), prefix_values.reshape(flat)),
            [VM] * 2,
            scratch=[pltpu.VMEM((chunk, head_dim), F32)],
            moved=prefix_keys.size * 8,
        )
    else:
        keys = prefix_keys.reshape(1, positions, head_dim)
        values = prefix_values.reshape(1, positions, head_dim)
    joined = call(
        join_kernel,
        "join",
        jax.ShapeDtypeStruct((nz, padded, head_dim), BF16),
        arrived,
        [VM] * nz,
        moved=nz * padded * head_dim * 4,
    )

    def prefix(name, arrays, others=()):
        count = len(arrays)
        return call(
            functools.partial(prefix_kernel, count, bool(others), local, qrows, scale),
            name,
            [jax.ShapeDtypeStruct((rows + ceil_to(3 * (rows // head_dim), 16), head_dim), BF16)] * count,
            (*arrays, keys, values, *others),
            [VM] * (count + 2 + len(others)),
            vmem=48 << 20,
            flops=4 * count * rows * positions * head_dim,
            moved=keys.size * 4,
        )

    far = {step: along_x(joined, step) for step in range(1, nx)}
    near = along_core(joined) if nc > 1 else None
    far_near = {step: along_core(far[step]) for step in far} if nc > 1 else {}

    width = suffix * local
    suffix_out, suffix_lse = call(
        functools.partial(suffix_kernel, nz, local, group, scale),
        "suffix",
        [jax.ShapeDtypeStruct((rows, head_dim), F32)] * 2,
        (
            joined, slot_branch, suffix_lengths,
            suffix_keys.reshape(slots, width, head_dim), suffix_values.reshape(slots, width, head_dim),
        ),
        [VM, SM, SM, ANY, ANY],
        scratch=[
            pltpu.VMEM((slots, width, head_dim), BF16),
            pltpu.VMEM((slots, width, head_dim), BF16),
            pltpu.VMEM((rows, head_dim), F32),
            pltpu.VMEM((slots * local * group, width), F32),
            pltpu.VMEM((slots * local * group, width), BF16),
            pltpu.SemaphoreType.DMA((slots,)),
            pltpu.SemaphoreType.DMA((slots,)),
        ],
        vmem=32 << 20,
        flops=4 * rows * width * head_dim,
        moved=suffix_keys.size * 4,
    )
    received = []
    merged = {}
    if nc > 1:
        sent = prefix("prefix_sibling", [near] + [far_near[step] for step in far])
        got = [along_core(x) for x in sent]
        received.append(got[0])
        merged = dict(zip(far, got[1:]))
    own_out, own_lse = call(
        functools.partial(prefix_own_kernel, local, qrows, scale),
        "prefix_own",
        [jax.ShapeDtypeStruct((rows, head_dim), F32)] * 2,
        (joined, keys, values),
        [VM] * 3,
        vmem=48 << 20,
        flops=4 * rows * positions * head_dim,
        moved=keys.size * 4,
    )
    if far:
        sent = prefix("prefix_far", list(far.values()), [merged[step] for step in far] if nc > 1 else ())
        received += [along_x(x, back(step, nx)) for x, step in zip(sent, far)]
    pieces = call(
        functools.partial(final_kernel, len(received), local, group, scale),
        "final",
        [jax.ShapeDtypeStruct((qrows, head_dim), BF16)] * nz,
        (joined, suffix_out, suffix_lse, own_out, own_lse, *received),
        [VM] * (5 + len(received)),
        moved=rows * head_dim * 20,
    )
    landed = [pieces[0]] + [
        shift(pieces[step], "branch", back(step, nz), nz) for step in range(nz - 1, 0, -1)
    ][::-1]
    out = call(
        functools.partial(unpack_kernel, nz, local, group),
        "unpack",
        jax.ShapeDtypeStruct((nb, nz, heads // nz, head_dim), BF16),
        landed,
        [VM] * nz,
        moved=queries.size * 4,
    )
    return out.reshape(nb, heads, head_dim)


def solution(mesh):
    lanes = P(("groups", "blk", "branch"), None, None)
    return jax.shard_map(
        functools.partial(per_device, mesh.shape["branch"], mesh.shape["blk"]),
        mesh=mesh,
        in_specs=(
            lanes,
            lanes,
            lanes,
            P(("groups", "blk"), "branch", None),
            P(("groups", "blk"), "branch", None),
            P(("groups", "blk"), None, "branch", None),
            P(("groups", "blk"), None, "branch", None),
            P("groups"),
            P("groups"),
        ),
        out_specs=lanes,
        check_vma=False,
    )
```

time: 91.4 us -> 45.3 us (0.50)
  blocking collectives: 13.9 us -> 0 us
  Pallas kernels: 0 us -> 13.2 us
  matrix products: 13 us -> 0 us
  starting transfers between devices: 23.6 us -> 12.9 us
  local copies, waits for them, and re-layouts: 15 us -> 7.27 us
  waiting for transfers between devices: 19.2 us -> 11.5 us
  other arithmetic: 5.34 us -> 0 us
    all_to_all x6 -> x0, starting transfers between devices: 23.6 us -> none  [the longest x1 6.32 us: per_device(): lax.all_to_all(fresh_token_values, 'branch', split_axis=1, concat_axis=0,...]
    all_to_all x6 -> x0, waiting for transfers between devices: 19.2 us -> none  [the longest x1 7.31 us: per_device(): lax.all_to_all(full_state[0][None], 'blk', split_axis=1, concat_axis=0, t...]
    pallas_call x0 -> x9, Pallas kernels: none -> 13.2 us  [call(): pl.pallas_call(kernel, name=name, out_shape=out_shape, in_specs=in_specs,...]
    ppermute x0 -> x12, starting transfers between devices: none -> 12.9 us  [shift(): return lax.ppermute(x, axis, pairs)]
    dot_general x15 -> x0, matrix products: 12.6 us -> none  [the longest x1 3.47 us: attend_suffix(): jnp.einsum('skgd,snkd->skgn', slot_queries, suffix_keys, preferred_elemen...]
    ppermute x0 -> x12, waiting for transfers between devices: none -> 11.5 us  [shift(): return lax.ppermute(x, axis, pairs)]
    all_to_all x1 -> x0, blocking collectives: 8.11 us -> none  [per_device(): lax.all_to_all(final_output, 'branch', split_axis=0, concat_axis=1, tiled...]
    dynamic_slice x5 -> x0, local copies, waits for them, and re-layouts: 6.31 us -> none  [the longest x4 5.58 us: attend_prefix(): final_output, _ = lax.scan(step, carried, (key_blocks, value_blocks))]
  transfers between devices with their start and end apart: 6 -> 12, of which waited for: 4 -> 6; matrix products, arithmetic and copies ran while one was open for 18% -> 0% of each run, Pallas kernels for 0% -> 23%
where the time goes in v1:
time: 45.3 us; the launch traced here: 45 us
  Pallas kernels  13.2 us (29%)
  starting transfers between devices  12.9 us (28%)
  waiting for transfers between devices  11.5 us (25%)
  local copies, waits for them, and re-layouts  7.27 us (16%)
    pallas_call x9, Pallas kernels, call(): pl.pallas_call(kernel, name=name, out_shape=out_shape, in_specs=in_specs,...  13.2 us
    ppermute x12, starting transfers between devices, shift(): return lax.ppermute(x, axis, pairs)  12.9 us
    ppermute x12, waiting for transfers between devices, shift(): return lax.ppermute(x, axis, pairs)  11.5 us
    unnamed x18, local copies, waits for them, and re-layouts  7.27 us
  transfers between devices with their start and end apart: 12, of which 6 were waited for; matrix products, arithmetic and copies ran while one was open for 0% of the time, Pallas kernels for 23%

profile of v1, /device:TPU:0, one launch (start us, length us, event | category | flops | bytes accessed | tf_op | source)
XLA Modules:
  0.0 45.0 jit_solution(14493919442083608856)
XLA Ops:
  0.0 0.0 copy-start
  0.0 0.0 copy-start.4
  0.0 1.0 %copy-done.4 = bf16[4,64,128]{2,1,0:T(8,128)(2,1)S(1)} copy-done((bf16[4,64,128]{2,1,0:T(8,128)(2,1)S(1)}, bf16[4,64,128]{2,1,0:T(8,128)(2,1)}, u32[]{:S(2)}) %copy-start.4) | copy-done | bytes 65560
  1.0 0.0 copy-start.5
  1.0 0.9 %copy-done.5 = bf16[4,8,128]{2,1,0:T(8,128)(2,1)S(1)} copy-done((bf16[4,8,128]{2,1,0:T(8,128)(2,1)S(1)}, bf16[4,8,128]{2,1,0:T(8,128)(2,1)}, u32[]{:S(2)}) %copy-start.5) | copy-done | bytes 8216
  1.9 0.0 copy-start.6
  1.9 0.7 %copy-done.6 = bf16[4,8,128]{2,1,0:T(8,128)(2,1)S(1)} copy-done((bf16[4,8,128]{2,1,0:T(8,128)(2,1)S(1)}, bf16[4,8,128]{2,1,0:T(8,128)(2,1)}, u32[]{:S(2)}) %copy-start.6) | copy-done | bytes 8216
  2.7 3.1 %collective-permute-start = (bf16[80,128]{1,0:T(8,128)(2,1)S(1)}, bf16[80,128]{1,0:T(8,128)(2,1)S(1)}, u32[]{:S(2)}, u32[]{:S(2)}) collective-permute-start(bf16[80,128]{1,0:T(8,128)(2,1)S(1)} %get-tuple-element.22), channel_id=1, source_target_pairs={{0,1},{1,0},{2,3},{3,2},{4,5},{5,4},{6,7},{7,6},{8,9},{9,8},{10,11... | collective-permute-start | bytes 61448 | tf_op jit(solution)/shard_map/ppermute | solution.py:316
  5.8 2.6 %collective-permute-start.1 = (bf16[80,128]{1,0:T(8,128)(2,1)S(1)}, bf16[80,128]{1,0:T(8,128)(2,1)S(1)}, u32[]{:S(2)}, u32[]{:S(2)}) collective-permute-start(bf16[80,128]{1,0:T(8,128)(2,1)S(1)} %get-tuple-element.23), channel_id=1, source_target_pairs={{0,2},{1,3},{2,0},{3,1},{4,6},{5,7},{6,4},{7,5},{8,10},{9,11},{10,... | collective-permute-start | bytes 61448 | tf_op jit(solution)/shard_map/ppermute | solution.py:316
  8.4 0.0 collective-permute-start.2
  8.4 0.0 collective-permute-done.refs_1_
  8.4 2.3 %collective-permute-done.1.refs_2_ = bf16[80,128]{1,0:T(8,128)(2,1)S(1)} collective-permute-done((bf16[80,128]{1,0:T(8,128)(2,1)S(1)}, bf16[80,128]{1,0:T(8,128)(2,1)S(1)}, u32[]{:S(2)}, u32[]{:S(2)}) %collective-permute-start.1) | collective-permute-done | bytes 20512 | tf_op jit(solution)/shard_map/ppermute | solution.py:316
  10.7 3.3 %collective-permute-done.2.refs_3_ = bf16[80,128]{1,0:T(8,128)(2,1)S(1)} collective-permute-done((bf16[80,128]{1,0:T(8,128)(2,1)S(1)}, bf16[80,128]{1,0:T(8,128)(2,1)S(1)}, u32[]{:S(2)}, u32[]{:S(2)}) %collective-permute-start.2) | collective-permute-done | bytes 20512 | tf_op jit(solution)/shard_map/ppermute | solution.py:316
  14.0 1.5 %collective-permute-start.4 = (bf16[4,80,128]{2,1,0:T(8,128)(2,1)S(1)}, bf16[4,80,128]{2,1,0:T(8,128)(2,1)S(1)}, u32[]{:S(2)}, u32[]{:S(2)}) collective-permute-start(bf16[4,80,128]{2,1,0:T(8,128)(2,1)S(1)} %join.1.joined_ref.q_ref), channel_id=1, source_target_pairs={{0,8},{4,12},{8,0},{12,4},{1,9},{5,13},{9,1},{13,5},{2,10},{6,14},... | collective-permute-start | bytes 245768 | tf_op jit(solution)/shard_map/ppermute | solution.py:316
  15.4 0.0 collective-permute-start.3
  15.4 2.9 %collective-permute-done.4.refs_0_ = bf16[4,80,128]{2,1,0:T(8,128)(2,1)S(1)} collective-permute-done((bf16[4,80,128]{2,1,0:T(8,128)(2,1)S(1)}, bf16[4,80,128]{2,1,0:T(8,128)(2,1)S(1)}, u32[]{:S(2)}, u32[]{:S(2)}) %collective-permute-start.4) | collective-permute-done | bytes 81952 | tf_op jit(solution)/shard_map/ppermute | solution.py:316
  18.4 0.0 collective-permute-start.5
  18.4 0.0 copy-start.2
  18.4 1.2 %copy-done.2 = bf16[2048,2,128]{2,1,0:T(2,128)(2,1)S(1)} copy-done((bf16[2048,2,128]{2,1,0:T(2,128)(2,1)S(1)}, bf16[2048,2,128]{2,1,0:T(2,128)(2,1)}, u32[]{:S(2)}) %copy-start.2) | copy-done | bytes 1048600
  19.6 0.0 copy-start.3
  19.6 1.2 %copy-done.3 = bf16[2048,2,128]{2,1,0:T(2,128)(2,1)S(1)} copy-done((bf16[2048,2,128]{2,1,0:T(2,128)(2,1)S(1)}, bf16[2048,2,128]{2,1,0:T(2,128)(2,1)}, u32[]{:S(2)}) %copy-start.3) | copy-done | bytes 1048600
  20.9 0.0 copy-start.7
  20.9 0.0 copy-start.8
  20.9 0.5 %split.1 = (bf16[2,2048,128]{2,1,0:T(8,128)(2,1)S(1)}, bf16[2,2048,128]{2,1,0:T(8,128)(2,1)S(1)}) custom-call(bf16[4096,128]{1,0:T(8,128)(2,1)S(1)} %bitcast.8, bf16[4096,128]{1,0:T(8,128)(2,1)S(1)} %bitcast.9), custom_call_target="tpu_custom_call" | custom-call | bytes 4194304 | tf_op jit(solution)/shard_map/split/pallas_call | solution.py:43
  21.3 0.0 collective-permute-done.3.refs_0_
  21.4 0.0 collective-permute-done.5.refs_1_
  21.4 1.8 %prefix_sibling.1 = (bf16[272,128]{1,0:T(8,128)(2,1)S(1)}, bf16[272,128]{1,0:T(8,128)(2,1)S(1)}) custom-call(bf16[4,80,128]{2,1,0:T(8,128)(2,1)S(1)} %collective-permute-done.3.refs_0_, bf16[4,80,128]{2,1,0:T(8,128)(2,1)S(1)} %collective-permute-done.5.refs_1_, bf16[2,2048,128]{2,1,0:T(8,128)(2,1)S(1)} %get-tuple-element.27.k_ref.refs_2_.refs_1_, ...), custom_call_target="tpu_custom_call" | custom-call | flops 536870912 | bytes 2097152 | tf_op jit(solution)/shard_map/prefix_sibling/pallas_call | solution.py:43
  23.1 0.6 %collective-permute-start.7 = (bf16[272,128]{1,0:T(8,128)(2,1)S(1)}, bf16[272,128]{1,0:T(8,128)(2,1)S(1)}, u32[]{:S(2)}, u32[]{:S(2)}) collective-permute-start(bf16[272,128]{1,0:T(8,128)(2,1)S(1)} %get-tuple-element.32), channel_id=1, source_target_pairs={{0,4},{4,0},{8,12},{12,8},{1,5},{5,1},{9,13},{13,9},{2,6},{6,2},{1... | collective-permute-start | bytes 208904 | tf_op jit(solution)/shard_map/ppermute | solution.py:316
  23.7 0.1 collective-permute-start.6
  23.8 0.8 %collective-permute-done.7.refs_3_ = bf16[272,128]{1,0:T(8,128)(2,1)S(1)} collective-permute-done((bf16[272,128]{1,0:T(8,128)(2,1)S(1)}, bf16[272,128]{1,0:T(8,128)(2,1)S(1)}, u32[]{:S(2)}, u32[]{:S(2)}) %collective-permute-start.7) | collective-permute-done | bytes 69664 | tf_op jit(solution)/shard_map/ppermute | solution.py:316
  24.6 1.4 %prefix_far.1 = bf16[272,128]{1,0:T(8,128)(2,1)S(1)} custom-call(bf16[4,80,128]{2,1,0:T(8,128)(2,1)S(1)} %collective-permute-done.4.refs_0_, bf16[2,2048,128]{2,1,0:T(8,128)(2,1)S(1)} %get-tuple-element.27.k_ref.refs_2_.refs_1_, bf16[2,2048,128]{2,1,0:T(8,128)(2,1)S(1)} %get-tuple-element.28.v_ref.refs_3_.refs_2_, ...), custom_call_target="tpu_custom_call" | custom-call | flops 268435456 | bytes 2097152 | tf_op jit(solution)/shard_map/prefix_far/pallas_call | solution.py:43
  26.0 1.6 %collective-permute-start.8 = (bf16[272,128]{1,0:T(8,128)(2,1)S(1)}, bf16[272,128]{1,0:T(8,128)(2,1)S(1)}, u32[]{:S(2)}, u32[]{:S(2)}) collective-permute-start(bf16[272,128]{1,0:T(8,128)(2,1)S(1)} %prefix_far.1), channel_id=1, source_target_pairs={{0,8},{4,12},{8,0},{12,4},{1,9},{5,13},{9,1},{13,5},{2,10},{6,14},... | collective-permute-start | bytes 208904 | tf_op jit(solution)/shard_map/ppermute | solution.py:316
  27.6 0.0 copy-done
  27.6 0.0 copy-done.7
  27.6 0.0 copy-done.8
  27.6 2.2 %copy-done.1 = bf16[16,512,2,128]{3,2,1,0:T(2,128)(2,1)S(1)} copy-done((bf16[16,512,2,128]{3,2,1,0:T(2,128)(2,1)S(1)}, bf16[16,512,2,128]{3,2,1,0:T(2,128)(2,1)}, u32[]{:S(2)}) %copy-start.1) | copy-done | bytes 4194328
  29.8 7.1 %suffix.1 = (f32[256,128]{1,0:T(8,128)S(1)}, f32[256,128]{1,0:T(8,128)S(1)}) custom-call(bf16[4,80,128]{2,1,0:T(8,128)(2,1)S(1)} %join.1.joined_ref.q_ref, s32[64]{0:T(128)S(1)} %copy-done.7, s32[64]{0:T(128)S(1)} %copy-done.8, bf16[16,1024,128]{2,1,0:T(8,128)(2,1)S(1)} %bitcast.6, bf16[16,1024,128]{2,1,0:T(8,128)(2,1)S(1)} %bitcast.7), custom_call_target="tpu_custom_call" | custom-call | flops 134217728 | bytes 8388608 | tf_op jit(solution)/shard_map/suffix/pallas_call | solution.py:43
  36.9 1.2 %prefix_own.1 = (f32[256,128]{1,0:T(8,128)S(1)}, f32[256,128]{1,0:T(8,128)S(1)}) custom-call(bf16[4,80,128]{2,1,0:T(8,128)(2,1)S(1)} %join.1.joined_ref.q_ref, bf16[2,2048,128]{2,1,0:T(8,128)(2,1)S(1)} %get-tuple-element.27.k_ref.refs_2_.refs_1_, bf16[2,2048,128]{2,1,0:T(8,128)(2,1)S(1)} %get-tuple-element.28.v_ref.refs_3_.refs_2_), custom_call_target="tpu_custom_call" | custom-call | flops 268435456 | bytes 2097152 | tf_op jit(solution)/shard_map/prefix_own/pallas_call | solution.py:43
  38.2 0.0 collective-permute-done.6.refs_0_
  38.2 0.0 collective-permute-done.8.refs_1_
  38.2 0.5 %final.1 = (bf16[64,128]{1,0:T(8,128)(2,1)S(1)}, bf16[64,128]{1,0:T(8,128)(2,1)S(1)}, bf16[64,128]{1,0:T(8,128)(2,1)S(1)}, bf16[64,128]{1,0:T(8,128)(2,1)S(1)}) custom-call(bf16[4,80,128]{2,1,0:T(8,128)(2,1)S(1)} %join.1.joined_ref.q_ref, f32[256,128]{1,0:T(8,128)S(1)} %get-tuple-element.25.so_ref, f32[256,128]{1,0:T(8,128)S(1)} %get-tuple-element.26.sl_ref, ...), custom_call_target="tpu_custom_call" | custom-call | bytes 655360 | tf_op jit(solution)/shard_map/final/pallas_call | solution.py:43
  38.7 0.1 collective-permute-start.10
  38.8 1.0 %collective-permute-start.11 = (bf16[64,128]{1,0:T(8,128)(2,1)S(1)}, bf16[64,128]{1,0:T(8,128)(2,1)S(1)}, u32[]{:S(2)}, u32[]{:S(2)}) collective-permute-start(bf16[64,128]{1,0:T(8,128)(2,1)S(1)} %get-tuple-element.36), channel_id=1, source_target_pairs={{0,3},{1,2},{2,1},{3,0},{4,7},{5,6},{6,5},{7,4},{8,11},{9,10},{10,... | collective-permute-start | bytes 49160 | tf_op jit(solution)/shard_map/ppermute | solution.py:316
  39.8 2.5 %collective-permute-start.9 = (bf16[64,128]{1,0:T(8,128)(2,1)S(1)}, bf16[64,128]{1,0:T(8,128)(2,1)S(1)}, u32[]{:S(2)}, u32[]{:S(2)}) collective-permute-start(bf16[64,128]{1,0:T(8,128)(2,1)S(1)} %get-tuple-element.34), channel_id=1, source_target_pairs={{0,1},{1,0},{2,3},{3,2},{4,5},{5,4},{6,7},{7,6},{8,9},{9,8},{10,11... | collective-permute-start | bytes 49160 | tf_op jit(solution)/shard_map/ppermute | solution.py:316
  42.3 1.2 %collective-permute-done.10.refs_2_ = bf16[64,128]{1,0:T(8,128)(2,1)S(1)} collective-permute-done((bf16[64,128]{1,0:T(8,128)(2,1)S(1)}, bf16[64,128]{1,0:T(8,128)(2,1)S(1)}, u32[]{:S(2)}, u32[]{:S(2)}) %collective-permute-start.10) | collective-permute-done | bytes 16416 | tf_op jit(solution)/shard_map/ppermute | solution.py:316
  43.4 1.0 %collective-permute-done.11.refs_3_ = bf16[64,128]{1,0:T(8,128)(2,1)S(1)} collective-permute-done((bf16[64,128]{1,0:T(8,128)(2,1)S(1)}, bf16[64,128]{1,0:T(8,128)(2,1)S(1)}, u32[]{:S(2)}, u32[]{:S(2)}) %collective-permute-start.11) | collective-permute-done | bytes 16416 | tf_op jit(solution)/shard_map/ppermute | solution.py:316
  44.4 0.0 collective-permute-done.9.refs_1_
  44.4 0.6 %unpack.1 = bf16[4,4,16,128]{3,2,1,0:T(8,128)(2,1)} custom-call(bf16[64,128]{1,0:T(8,128)(2,1)S(1)} %get-tuple-element.33.refs_0_, bf16[64,128]{1,0:T(8,128)(2,1)S(1)} %collective-permute-done.9.refs_1_, bf16[64,128]{1,0:T(8,128)(2,1)S(1)} %collective-permute-done.10.refs_2_, bf16[64,128]{1,0:T(8,128)(2,1)S(1)} %collective-permute-done.11.refs_3_), custom_call_target="tpu_custom_call" | custom-call | bytes 131072 | tf_op jit(solution)/shard_map/unpack/pallas_call | solution.py:43
  (3 shorter events, 0.1 us)
Async XLA Ops:
  0.0 27.6 %copy-start = (bf16[16,512,2,128]{3,2,1,0:T(2,128)(2,1)S(1)}, bf16[16,512,2,128]{3,2,1,0:T(2,128)(2,1)}, u32[]{:S(2)}) copy-start(bf16[16,512,2,128]{3,2,1,0:T(2,128)(2,1)} %param.14) | copy-start | bytes 12582916
  0.0 1.0 %copy-start.4 = (bf16[4,64,128]{2,1,0:T(8,128)(2,1)S(1)}, bf16[4,64,128]{2,1,0:T(8,128)(2,1)}, u32[]{:S(2)}) copy-start(bf16[4,64,128]{2,1,0:T(8,128)(2,1)} %param.9) | copy-start | bytes 196612
  1.0 0.9 %copy-start.5 = (bf16[4,8,128]{2,1,0:T(8,128)(2,1)S(1)}, bf16[4,8,128]{2,1,0:T(8,128)(2,1)}, u32[]{:S(2)}) copy-start(bf16[4,8,128]{2,1,0:T(8,128)(2,1)} %k_ref.1) | copy-start | bytes 24580
  1.9 0.7 %copy-start.6 = (bf16[4,8,128]{2,1,0:T(8,128)(2,1)S(1)}, bf16[4,8,128]{2,1,0:T(8,128)(2,1)}, u32[]{:S(2)}) copy-start(bf16[4,8,128]{2,1,0:T(8,128)(2,1)} %v_ref.1) | copy-start | bytes 24580
  2.7 5.7 %collective-permute-start = (bf16[80,128]{1,0:T(8,128)(2,1)S(1)}, bf16[80,128]{1,0:T(8,128)(2,1)S(1)}, u32[]{:S(2)}, u32[]{:S(2)}) collective-permute-start(bf16[80,128]{1,0:T(8,128)(2,1)S(1)} %get-tuple-element.22), channel_id=1, source_target_pairs={{0,1},{1,0},{2,3},{3,2},{4,5},{5,4},{6,7},{7,6},{8,9},{9,8},{10,11... | collective-permute-start | bytes 61448 | tf_op jit(solution)/shard_map/ppermute | solution.py:316
  5.8 4.9 %collective-permute-start.1 = (bf16[80,128]{1,0:T(8,128)(2,1)S(1)}, bf16[80,128]{1,0:T(8,128)(2,1)S(1)}, u32[]{:S(2)}, u32[]{:S(2)}) collective-permute-start(bf16[80,128]{1,0:T(8,128)(2,1)S(1)} %get-tuple-element.23), channel_id=1, source_target_pairs={{0,2},{1,3},{2,0},{3,1},{4,6},{5,7},{6,4},{7,5},{8,10},{9,11},{10,... | collective-permute-start | bytes 61448 | tf_op jit(solution)/shard_map/ppermute | solution.py:316
  8.4 5.6 %collective-permute-start.2 = (bf16[80,128]{1,0:T(8,128)(2,1)S(1)}, bf16[80,128]{1,0:T(8,128)(2,1)S(1)}, u32[]{:S(2)}, u32[]{:S(2)}) collective-permute-start(bf16[80,128]{1,0:T(8,128)(2,1)S(1)} %get-tuple-element.24), channel_id=1, source_target_pairs={{0,3},{1,2},{2,1},{3,0},{4,7},{5,6},{6,5},{7,4},{8,11},{9,10},{10,... | collective-permute-start | bytes 61448 | tf_op jit(solution)/shard_map/ppermute | solution.py:316
  14.0 4.4 %collective-permute-start.4 = (bf16[4,80,128]{2,1,0:T(8,128)(2,1)S(1)}, bf16[4,80,128]{2,1,0:T(8,128)(2,1)S(1)}, u32[]{:S(2)}, u32[]{:S(2)}) collective-permute-start(bf16[4,80,128]{2,1,0:T(8,128)(2,1)S(1)} %join.1.joined_ref.q_ref), channel_id=1, source_target_pairs={{0,8},{4,12},{8,0},{12,4},{1,9},{5,13},{9,1},{13,5},{2,10},{6,14},... | collective-permute-start | bytes 245768 | tf_op jit(solution)/shard_map/ppermute | solution.py:316
  15.4 5.9 %collective-permute-start.3 = (bf16[4,80,128]{2,1,0:T(8,128)(2,1)S(1)}, bf16[4,80,128]{2,1,0:T(8,128)(2,1)S(1)}, u32[]{:S(2)}, u32[]{:S(2)}) collective-permute-start(bf16[4,80,128]{2,1,0:T(8,128)(2,1)S(1)} %join.1.joined_ref.q_ref), channel_id=1, source_target_pairs={{0,4},{4,0},{8,12},{12,8},{1,5},{5,1},{9,13},{13,9},{2,6},{6,2},{1... | collective-permute-start | bytes 245768 | tf_op jit(solution)/shard_map/ppermute | solution.py:316
  18.4 3.0 %collective-permute-start.5 = (bf16[4,80,128]{2,1,0:T(8,128)(2,1)S(1)}, bf16[4,80,128]{2,1,0:T(8,128)(2,1)S(1)}, u32[]{:S(2)}, u32[]{:S(2)}) collective-permute-start(bf16[4,80,128]{2,1,0:T(8,128)(2,1)S(1)} %collective-permute-done.4.refs_0_), channel_id=1, source_target_pairs={{0,4},{4,0},{8,12},{12,8},{1,5},{5,1},{9,13},{13,9},{2,6},{6,2},{1... | collective-permute-start | bytes 245768 | tf_op jit(solution)/shard_map/ppermute | solution.py:316
  18.4 1.2 %copy-start.2 = (bf16[2048,2,128]{2,1,0:T(2,128)(2,1)S(1)}, bf16[2048,2,128]{2,1,0:T(2,128)(2,1)}, u32[]{:S(2)}) copy-start(bf16[2048,2,128]{2,1,0:T(2,128)(2,1)} %param.12) | copy-start | bytes 3145732
  19.6 1.2 %copy-start.3 = (bf16[2048,2,128]{2,1,0:T(2,128)(2,1)S(1)}, bf16[2048,2,128]{2,1,0:T(2,128)(2,1)}, u32[]{:S(2)}) copy-start(bf16[2048,2,128]{2,1,0:T(2,128)(2,1)} %param.13) | copy-start | bytes 3145732
  20.9 6.7 %copy-start.7 = (s32[64]{0:T(128)S(1)}, s32[64]{0:T(128)}, u32[]{:S(2)}) copy-start(s32[64]{0:T(128)} %slot_ref.1) | copy-start | bytes 772
  20.9 6.7 %copy-start.8 = (s32[64]{0:T(128)S(1)}, s32[64]{0:T(128)}, u32[]{:S(2)}) copy-start(s32[64]{0:T(128)} %len_ref.1) | copy-start | bytes 772
  23.1 1.5 %collective-permute-start.7 = (bf16[272,128]{1,0:T(8,128)(2,1)S(1)}, bf16[272,128]{1,0:T(8,128)(2,1)S(1)}, u32[]{:S(2)}, u32[]{:S(2)}) collective-permute-start(bf16[272,128]{1,0:T(8,128)(2,1)S(1)} %get-tuple-element.32), channel_id=1, source_target_pairs={{0,4},{4,0},{8,12},{12,8},{1,5},{5,1},{9,13},{13,9},{2,6},{6,2},{1... | collective-permute-start | bytes 208904 | tf_op jit(solution)/shard_map/ppermute | solution.py:316
  23.7 14.4 %collective-permute-start.6 = (bf16[272,128]{1,0:T(8,128)(2,1)S(1)}, bf16[272,128]{1,0:T(8,128)(2,1)S(1)}, u32[]{:S(2)}, u32[]{:S(2)}) collective-permute-start(bf16[272,128]{1,0:T(8,128)(2,1)S(1)} %get-tuple-element.31), channel_id=1, source_target_pairs={{0,4},{4,0},{8,12},{12,8},{1,5},{5,1},{9,13},{13,9},{2,6},{6,2},{1... | collective-permute-start | bytes 208904 | tf_op jit(solution)/shard_map/ppermute | solution.py:316
  26.0 12.2 %collective-permute-start.8 = (bf16[272,128]{1,0:T(8,128)(2,1)S(1)}, bf16[272,128]{1,0:T(8,128)(2,1)S(1)}, u32[]{:S(2)}, u32[]{:S(2)}) collective-permute-start(bf16[272,128]{1,0:T(8,128)(2,1)S(1)} %prefix_far.1), channel_id=1, source_target_pairs={{0,8},{4,12},{8,0},{12,4},{1,9},{5,13},{9,1},{13,5},{2,10},{6,14},... | collective-permute-start | bytes 208904 | tf_op jit(solution)/shard_map/ppermute | solution.py:316
  27.6 2.2 %copy-start.1 = (bf16[16,512,2,128]{3,2,1,0:T(2,128)(2,1)S(1)}, bf16[16,512,2,128]{3,2,1,0:T(2,128)(2,1)}, u32[]{:S(2)}) copy-start(bf16[16,512,2,128]{3,2,1,0:T(2,128)(2,1)} %param.15) | copy-start | bytes 12582916
  38.7 4.7 %collective-permute-start.10 = (bf16[64,128]{1,0:T(8,128)(2,1)S(1)}, bf16[64,128]{1,0:T(8,128)(2,1)S(1)}, u32[]{:S(2)}, u32[]{:S(2)}) collective-permute-start(bf16[64,128]{1,0:T(8,128)(2,1)S(1)} %get-tuple-element.35), channel_id=1, source_target_pairs={{0,2},{1,3},{2,0},{3,1},{4,6},{5,7},{6,4},{7,5},{8,10},{9,11},{10,... | collective-permute-start | bytes 49160 | tf_op jit(solution)/shard_map/ppermute | solution.py:316
  38.8 5.6 %collective-permute-start.11 = (bf16[64,128]{1,0:T(8,128)(2,1)S(1)}, bf16[64,128]{1,0:T(8,128)(2,1)S(1)}, u32[]{:S(2)}, u32[]{:S(2)}) collective-permute-start(bf16[64,128]{1,0:T(8,128)(2,1)S(1)} %get-tuple-element.36), channel_id=1, source_target_pairs={{0,3},{1,2},{2,1},{3,0},{4,7},{5,6},{6,5},{7,4},{8,11},{9,10},{10,... | collective-permute-start | bytes 49160 | tf_op jit(solution)/shard_map/ppermute | solution.py:316
  39.8 4.6 %collective-permute-start.9 = (bf16[64,128]{1,0:T(8,128)(2,1)S(1)}, bf16[64,128]{1,0:T(8,128)(2,1)S(1)}, u32[]{:S(2)}, u32[]{:S(2)}) collective-permute-start(bf16[64,128]{1,0:T(8,128)(2,1)S(1)} %get-tuple-element.34), channel_id=1, source_target_pairs={{0,1},{1,0},{2,3},{3,2},{4,5},{5,4},{6,7},{7,6},{8,9},{9,8},{10,11... | collective-permute-start | bytes 49160 | tf_op jit(solution)/shard_map/ppermute | solution.py:316

commit v2 on v1

--- a/solution.py
+++ b/solution.py
@@ -9,12 +9,13 @@
 from jax.sharding import PartitionSpec as P
 
 NEG = -1e30
+GAP = 1 << 36
 LOG2E = 1.4426950408889634
 F32 = jnp.float32
 BF16 = jnp.bfloat16
 VM = pl.BlockSpec(memory_space=pltpu.VMEM)
 SM = pl.BlockSpec(memory_space=pltpu.SMEM)
-ANY = pl.BlockSpec(memory_space=pl.ANY)
+HBM = pl.BlockSpec(memory_space=pltpu.HBM)
 NT = (((1,), (1,)), ((), ()))
 
 
@@ -36,6 +37,10 @@
     if count & (count - 1) == 0:
         return me ^ other
     return lax.rem(me - other + count, count)
+
+
+def in_hbm(x):
+    return pltpu.with_memory_space_constraint(x, pltpu.HBM)
 
 
 def call(kernel, name, out_shape, inputs, in_specs, scratch=(), vmem=16 << 20, flops=0, moved=0, out_specs=None):
@@ -52,7 +57,16 @@
     )(*inputs)
 
 
-def pack_kernel(nz, local, group, pad, q_ref, k_ref, v_ref, *out_refs):
+def pack_kernel(nz, local, group, pad, q_hbm, k_hbm, v_hbm, *refs):
+    out_refs, (q_ref, k_ref, v_ref, sems) = refs[:nz], refs[nz:]
+    copies = [
+        pltpu.make_async_copy(src, dst, sems.at[i])
+        for i, (src, dst) in enumerate(((q_hbm, q_ref), (k_hbm, k_ref), (v_hbm, v_ref)))
+    ]
+    for copy in copies:
+        copy.start()
+    for copy in copies:
+        copy.wait()
     me = lax.axis_index("branch")
     nb = q_ref.shape[0]
     head_dim = q_ref.shape[-1]
@@ -77,16 +91,26 @@
         out_refs[step][...] = jnp.concatenate(parts, axis=0).astype(BF16)
 
 
-def join_kernel(*refs):
-    for step, ref in enumerate(refs[:-1]):
-        refs[-1][step] = ref[...]
-
-
-def split_kernel(local, k_ref, v_ref, ko_ref, vo_ref, wide):
+def join_kernel(nz, qrows, *refs):
+    q_ref, tail_ref = refs[-2:]
+    for step in range(nz):
+        q_ref[step] = refs[nz - 1 - step][:qrows]
+        tail_ref[step] = refs[nz - 1 - step][qrows:]
+
+
+def gap_kernel(after, token):
+    token[...] = jnp.zeros(token.shape, token.dtype)
+
+
+def split_kernel(local, pk, pv, pko, pvo, token, wide):
+    token[...] = jnp.zeros(token.shape, token.dtype)
     chunk = wide.shape[0]
     rows = chunk // local
-    for src, dst in ((k_ref, ko_ref), (v_ref, vo_ref)):
+    for src, dst in ((pk, pko), (pv, pvo)):
         for at in range(src.shape[0] // chunk):
+            if local == 1:
+                dst[0, at * rows : (at + 1) * rows] = src[at * chunk : (at + 1) * chunk]
+                continue
             wide[...] = src[at * chunk : (at + 1) * chunk].astype(F32)
             for kl in range(local):
                 dst[kl, at * rows : (at + 1) * rows] = wide[pl.ds(kl, rows, stride=local)].astype(BF16)
@@ -94,15 +118,11 @@
 
 def suffix_kernel(
     nz, local, group, scale, joined_ref, slot_ref, len_ref, keys, values, out_ref, lse_ref,
-    kbuf, vbuf, qwide, scores, probs, ksem, vsem
+    qwide, scores, probs
 ):
-    slots, width, head_dim = kbuf.shape
+    slots, width, head_dim = keys.shape
     block = lax.axis_index("blk")
     me = lax.axis_index("branch")
-    copies_k = [pltpu.make_async_copy(keys.at[c], kbuf.at[c], ksem.at[c]) for c in range(slots)]
-    copies_v = [pltpu.make_async_copy(values.at[c], vbuf.at[c], vsem.at[c]) for c in range(slots)]
-    for copy in copies_k + copies_v:
-        copy.start()
     nb = slots // nz
     qrows = local * nb * group
     for step in range(nz):
@@ -123,8 +143,7 @@
     for c in range(slots):
         at, length = places(c)
         q = jnp.concatenate([qwide[pl.ds(a, group)] for a in at], axis=0).astype(BF16)
-        copies_k[c].wait()
-        s = lax.dot_general(q, kbuf[c], NT, preferred_element_type=F32)
+        s = lax.dot_general(q, keys[c], NT, preferred_element_type=F32)
         scores[c * heads : (c + 1) * heads] = jnp.where(
             own_head & (column < length * local), s, NEG
         )
@@ -137,8 +156,7 @@
     inverse = 1.0 / total
     for c in range(slots):
         at, _ = places(c)
-        copies_v[c].wait()
-        o = jnp.dot(probs[c * heads : (c + 1) * heads], vbuf[c], preferred_element_type=F32)
+        o = jnp.dot(probs[c * heads : (c + 1) * heads], values[c], preferred_element_type=F32)
         o = o * inverse[c * heads : (c + 1) * heads]
         for kl in range(local):
             lo, hi = kl * group, (kl + 1) * group
@@ -231,50 +249,55 @@
     return results
 
 
-def prefix_kernel(count, merged, local, qrows, scale, *refs):
-    q_refs, (k_ref, v_ref) = refs[:count], refs[count : count + 2]
-    others = refs[count + 2 : count + 2 + (count if merged else 0)]
-    outs = refs[-count:]
-    results = prefix_partial(q_refs, k_ref, v_ref, local, qrows, scale)
-    for i, (o, lse) in enumerate(results):
-        if merged:
-            o, lse = merge([(o, lse), decode(others[i][...], o.shape[0])])
-        outs[i][...] = encode(o, lse)
-
-
-def prefix_own_kernel(local, qrows, scale, q_ref, k_ref, v_ref, o_ref, lse_ref):
+def prefix_kernel(count, *refs, local, qrows, scale):
+    q_refs, (k_ref, v_ref), outs = refs[:count], refs[count : count + 2], refs[count + 2 :]
+    for ref, (o, lse) in zip(outs, prefix_partial(q_refs, k_ref, v_ref, local, qrows, scale)):
+        ref[...] = encode(o, lse)
+
+
+def prefix_own_kernel(q_ref, k_ref, v_ref, o_ref, lse_ref, *, local, qrows, scale):
     ((o, lse),) = prefix_partial([q_ref], k_ref, v_ref, local, qrows, scale)
     o_ref[...] = o
     lse_ref[...] = jnp.broadcast_to(lse, o.shape)
 
 
-def final_kernel(count, local, group, scale, joined_ref, so_ref, sl_ref, po_ref, pl_ref, *refs):
-    others, outs = refs[:count], refs[count:]
-    nz = joined_ref.shape[0]
+def near_kernel(count, local, group, scale, q_ref, fresh_ref, so_ref, sl_ref, po_ref, pl_ref, *refs):
+    others, (out_ref, lse_ref) = refs[:count], refs[count:]
     rows, head_dim = po_ref.shape
-    qrows = rows // nz
-    nb = qrows // (local * group)
-    part = nb * local
+    nz, qrows = q_ref.shape[:2]
+    part = qrows // group
     own_score, own_value = [], []
     for step in range(nz):
-        q = joined_ref[step, :qrows].astype(F32)
-        tail = joined_ref[step, qrows:].astype(F32)
-        k = jnp.concatenate(
-            [jnp.broadcast_to(tail[i : i + 1], (group, head_dim)) for i in range(part)], axis=0
-        )
-        own_value += [
-            jnp.broadcast_to(tail[i : i + 1], (group, head_dim)) for i in range(part, 2 * part)
-        ]
+        q = q_ref[step].astype(F32)
+        tail = fresh_ref[step].astype(F32)
+        k, v = (
+            jnp.concatenate(
+                [jnp.broadcast_to(tail[i : i + 1], (group, head_dim)) for i in range(at, at + part)],
+                axis=0,
+            )
+            for at in (0, part)
+        )
         own_score.append(jnp.sum(q * k, axis=1, keepdims=True) * scale)
+        own_value.append(v)
     parts = [
         (jnp.concatenate(own_value, axis=0), jnp.concatenate(own_score, axis=0)),
         (so_ref[...], sl_ref[:, :1]),
         (po_ref[...], pl_ref[:, :1]),
     ]
     parts += [decode(ref[...], rows) for ref in others]
+    out, lse = merge(parts)
+    out_ref[...] = out
+    lse_ref[...] = jnp.broadcast_to(lse, out.shape)
+
+
+def final_kernel(count, near_ref, lse_ref, *refs):
+    others, outs = refs[:count], refs[count:]
+    parts = [(near_ref[...], lse_ref[:, :1])]
+    parts += [decode(ref[...], near_ref.shape[0]) for ref in others]
     out, _ = merge(parts)
-    for step in range(nz):
-        outs[step][...] = out[step * qrows : (step + 1) * qrows].astype(BF16)
+    qrows = outs[0].shape[0]
+    for step, ref in enumerate(outs):
+        ref[...] = out[step * qrows : (step + 1) * qrows].astype(BF16)
 
 
 def unpack_kernel(nz, local, group, *refs):
@@ -283,7 +306,7 @@
     nb = out_ref.shape[0]
     for step in range(nz):
         peer = partner(me, step, nz)
-        wide = pieces[step][...].astype(F32)
+        wide = pieces[nz - 1 - step][...].astype(F32)
         for b in range(nb):
             rows = [wide[(kl * nb + b) * group : (kl * nb + b + 1) * group] for kl in range(local)]
             out_ref[b, peer] = jnp.concatenate(rows, axis=0).astype(BF16)
@@ -305,123 +328,140 @@
     nc = 2 if nblk % 2 == 0 else 1
     nx = nblk // nc
 
-    def shift(x, axis, step, count, unit=1, size=None):
-        size = count * unit if size is None else size
-        pairs = []
-        for i in range(size):
-            inner, outer = i % unit, i // unit
-            low = outer % count
-            other = outer - low + partner(low, step, count)
-            pairs.append((i, other * unit + inner))
-        return lax.ppermute(x, axis, pairs)
-
-    def along_core(x):
-        return shift(x, "blk", 1, 2, 1, nblk)
-
-    def along_x(x, step):
-        return shift(x, "blk", step, nx, nc, nblk)
+    def shift(x, axis, step, count):
+        return lax.ppermute(x, axis, [(i, partner(i, step, count)) for i in range(count)])
+
+    def along_blk(x, step_x, step_c):
+        return lax.ppermute(
+            x,
+            "blk",
+            [
+                (i, partner(i // nc, step_x, nx) * nc + partner(i % nc, step_c, nc))
+                for i in range(nblk)
+            ],
+        )
 
     payloads = call(
         functools.partial(pack_kernel, nz, local, group, padded - used),
         "pack",
-        [jax.ShapeDtypeStruct((padded, head_dim), BF16)] * nz,
-        (queries.reshape(nb, nz, heads // nz, head_dim), new_keys, fresh_token_values),
-        [VM] * 3,
+        [pltpu.VMEM((padded, head_dim), BF16)] * nz,
+        (
+            in_hbm(queries.reshape(nb, nz, heads // nz, head_dim)),
+            in_hbm(new_keys), in_hbm(fresh_token_values),
+        ),
+        [HBM] * 3,
+        scratch=[
+            pltpu.VMEM((nb, nz, heads // nz, head_dim), BF16),
+            pltpu.VMEM(new_keys.shape, BF16),
+            pltpu.VMEM(new_keys.shape, BF16),
+            pltpu.SemaphoreType.DMA((3,)),
+        ],
         moved=queries.size * 4,
     )
+    gap = call(
+        gap_kernel, "gap", pltpu.VMEM((8, head_dim), F32), (payloads[0],), [VM], flops=GAP, moved=GAP,
+    )
+    payloads, gap = lax.optimization_barrier((payloads, gap))
     arrived = [payloads[0]] + [
         shift(payloads[step], "branch", step, nz) for step in range(nz - 1, 0, -1)
     ][::-1]
-    if local > 1:
-        chunk = math.gcd(positions * local, 1024)
-        flat = (positions * local, head_dim)
-        keys, values = call(
-            functools.partial(split_kernel, local),
-            "split",
-            [jax.ShapeDtypeStruct((local, positions, head_dim), BF16)] * 2,
-            (prefix_keys.reshape(flat), prefix_values.reshape(flat)),
-            [VM] * 2,
-            scratch=[pltpu.VMEM((chunk, head_dim), F32)],
-            moved=prefix_keys.size * 8,
-        )
-    else:
-        keys = prefix_keys.reshape(1, positions, head_dim)
-        values = prefix_values.reshape(1, positions, head_dim)
-    joined = call(
-        join_kernel,
+    chunk = math.gcd(positions * local, 1024)
+    flat = (positions * local, head_dim)
+    width = suffix * local
+    slot_rows = (slots, width, head_dim)
+    slot_keys, slot_values = suffix_keys.reshape(slot_rows), suffix_values.reshape(slot_rows)
+    keys, values, token = call(
+        functools.partial(split_kernel, local),
+        "split",
+        [pltpu.VMEM((local, positions, head_dim), BF16)] * 2 + [pltpu.VMEM((8, head_dim), F32)],
+        (prefix_keys.reshape(flat), prefix_values.reshape(flat)),
+        [VM] * 2,
+        scratch=[pltpu.VMEM((chunk, head_dim), F32)],
+        vmem=8 << 20,
+        moved=prefix_keys.size * 8,
+    )
+    joined, fresh = call(
+        functools.partial(join_kernel, nz, qrows),
         "join",
-        jax.ShapeDtypeStruct((nz, padded, head_dim), BF16),
-        arrived,
-        [VM] * nz,
+        [
+            jax.ShapeDtypeStruct((nz, qrows, head_dim), BF16),
+            jax.ShapeDtypeStruct((nz, padded - qrows, head_dim), BF16),
+        ],
+        (*arrived[::-1], gap, token),
+        [VM] * (nz + 2),
         moved=nz * padded * head_dim * 4,
     )
 
-    def prefix(name, arrays, others=()):
+    tail = ceil_to(3 * (rows // head_dim), 16)
+
+    state = [jax.ShapeDtypeStruct((rows, head_dim), F32)] * 2
+
+    def prefix(name, arrays, own=False):
         count = len(arrays)
+        kernel = prefix_own_kernel if own else functools.partial(prefix_kernel, count)
         return call(
-            functools.partial(prefix_kernel, count, bool(others), local, qrows, scale),
+            functools.partial(kernel, local=local, qrows=qrows, scale=scale),
             name,
-            [jax.ShapeDtypeStruct((rows + ceil_to(3 * (rows // head_dim), 16), head_dim), BF16)] * count,
-            (*arrays, keys, values, *others),
-            [VM] * (count + 2 + len(others)),
-            vmem=48 << 20,
+            state if own else [jax.ShapeDtypeStruct((rows + tail, head_dim), BF16)] * count,
+            (*arrays, keys, values),
+            [VM] * (count + 2),
+            vmem=16 << 20,
             flops=4 * count * rows * positions * head_dim,
             moved=keys.size * 4,
         )
 
-    far = {step: along_x(joined, step) for step in range(1, nx)}
-    near = along_core(joined) if nc > 1 else None
-    far_near = {step: along_core(far[step]) for step in far} if nc > 1 else {}
-
-    width = suffix * local
+    far_steps = [(x, c) for x in range(1, nx) for c in range(nc)]
+    near_steps = [(0, c) for c in range(1, nc)]
+    arriving = {step: along_blk(joined, *step) for step in far_steps + near_steps}
+
     suffix_out, suffix_lse = call(
         functools.partial(suffix_kernel, nz, local, group, scale),
         "suffix",
         [jax.ShapeDtypeStruct((rows, head_dim), F32)] * 2,
         (
-            joined, slot_branch, suffix_lengths,
-            suffix_keys.reshape(slots, width, head_dim), suffix_values.reshape(slots, width, head_dim),
+            joined, slot_branch, suffix_lengths, slot_keys, slot_values,
         ),
-        [VM, SM, SM, ANY, ANY],
+        [VM, SM, SM, VM, VM],
         scratch=[
-            pltpu.VMEM((slots, width, head_dim), BF16),
-            pltpu.VMEM((slots, width, head_dim), BF16),
             pltpu.VMEM((rows, head_dim), F32),
             pltpu.VMEM((slots * local * group, width), F32),
             pltpu.VMEM((slots * local * group, width), BF16),
-            pltpu.SemaphoreType.DMA((slots,)),
-            pltpu.SemaphoreType.DMA((slots,)),
         ],
-        vmem=32 << 20,
+        vmem=8 << 20,
         flops=4 * rows * width * head_dim,
         moved=suffix_keys.size * 4,
     )
+    own_state = prefix("prefix_own", [joined], own=True)
+    arriving, suffix_out, own_state = lax.optimization_barrier((arriving, suffix_out, own_state))
+
+    def give_back(sent, steps):
+        return [along_blk(x, back(step[0], nx), back(step[1], nc)) for x, step in zip(sent, steps)]
+
     received = []
-    merged = {}
-    if nc > 1:
-        sent = prefix("prefix_sibling", [near] + [far_near[step] for step in far])
-        got = [along_core(x) for x in sent]
-        received.append(got[0])
-        merged = dict(zip(far, got[1:]))
-    own_out, own_lse = call(
-        functools.partial(prefix_own_kernel, local, qrows, scale),
-        "prefix_own",
-        [jax.ShapeDtypeStruct((rows, head_dim), F32)] * 2,
-        (joined, keys, values),
-        [VM] * 3,
-        vmem=48 << 20,
-        flops=4 * rows * positions * head_dim,
-        moved=keys.size * 4,
-    )
-    if far:
-        sent = prefix("prefix_far", list(far.values()), [merged[step] for step in far] if nc > 1 else ())
-        received += [along_x(x, back(step, nx)) for x, step in zip(sent, far)]
+    sent = []
+    for i in range(0, len(far_steps), 2):
+        steps = far_steps[i : i + 2]
+        rows_of, sent = lax.optimization_barrier(([arriving[step] for step in steps], sent))
+        sent = prefix("prefix_far", rows_of)
+        received += give_back(sent, steps)
+    sibling = []
+    if near_steps:
+        rows_of, sent = lax.optimization_barrier(([arriving[step] for step in near_steps], sent))
+        sibling = give_back(prefix("prefix_near", rows_of), near_steps)
+    near = call(
+        functools.partial(near_kernel, len(sibling), local, group, scale),
+        "near",
+        state,
+        (joined, fresh, suffix_out, suffix_lse, *own_state, *sibling),
+        [VM] * (6 + len(sibling)),
+        moved=rows * head_dim * 20,
+    )
     pieces = call(
-        functools.partial(final_kernel, len(received), local, group, scale),
+        functools.partial(final_kernel, len(received)),
         "final",
         [jax.ShapeDtypeStruct((qrows, head_dim), BF16)] * nz,
-        (joined, suffix_out, suffix_lse, own_out, own_lse, *received),
-        [VM] * (5 + len(received)),
+        (*near, *received),
+        [VM] * (2 + len(received)),
         moved=rows * head_dim * 20,
     )
     landed = [pieces[0]] + [
@@ -431,7 +471,7 @@
         functools.partial(unpack_kernel, nz, local, group),
         "unpack",
         jax.ShapeDtypeStruct((nb, nz, heads // nz, head_dim), BF16),
-        landed,
+        landed[::-1],
         [VM] * nz,
         moved=queries.size * 4,
     )

time: 45.3 us -> 32.9 us (0.73)
  local copies, waits for them, and re-layouts: 7.27 us -> 0.04 us
  Pallas kernels: 13.2 us -> 9.4 us
  waiting for transfers between devices: 11.5 us -> 9.1 us
  starting transfers between devices: 12.9 us -> 14.1 us
    unnamed x18 -> x12, local copies, waits for them, and re-layouts: 7.27 us -> 0.04 us
    pallas_call x9 -> x11, Pallas kernels: 13.2 us -> 9.4 us  [call(): pl.pallas_call(kernel, name=name, out_shape=out_shape, in_specs=in_specs,...]
    ppermute x12, waiting for transfers between devices: 11.5 us -> 9.1 us  [the longest x6 5.41 us: shift(): lax.ppermute(x, axis, [(i, partner(i, step, count)) for i in range(count)])]
    ppermute x12, starting transfers between devices: 12.9 us -> 14.1 us  [the longest x6 10.2 us: shift(): lax.ppermute(x, axis, [(i, partner(i, step, count)) for i in range(count)])]
  transfers between devices with their start and end apart: 12 -> 12, of which waited for: 6 -> 8; matrix products, arithmetic and copies ran while one was open for 0% -> 0% of each run, Pallas kernels for 23% -> 14%
where the time goes in v2:
time: 32.9 us; the launch traced here: 32.7 us
  starting transfers between devices  14.1 us (43%)
  Pallas kernels  9.4 us (29%)
  waiting for transfers between devices  9.1 us (28%)
    ppermute x6, starting transfers between devices, shift(): lax.ppermute(x, axis, [(i, partner(i, step, count)) for i in range(count)])  10.2 us
    pallas_call x11, Pallas kernels, call(): pl.pallas_call(kernel, name=name, out_shape=out_shape, in_specs=in_specs,...  9.4 us
    ppermute x6, waiting for transfers between devices, shift(): lax.ppermute(x, axis, [(i, partner(i, step, count)) for i in range(count)])  5.41 us
    ppermute x6, starting transfers between devices, along_blk(): lax.ppermute(x, 'blk', [(i, partner(i // nc, step_x, nx) * nc + partner(i...  3.86 us
    ppermute x6, waiting for transfers between devices, along_blk(): lax.ppermute(x, 'blk', [(i, partner(i // nc, step_x, nx) * nc + partner(i...  3.69 us
  transfers between devices with their start and end apart: 12, of which 8 were waited for; matrix products, arithmetic and copies ran while one was open for 0% of the time, Pallas kernels for 14%

profile of v2, /device:TPU:0, one launch (start us, length us, event | category | flops | bytes accessed | tf_op | source)
XLA Modules:
  0.0 32.7 jit_solution(17586141127543803092)
XLA Ops:
  0.0 0.9 %pack.1 = (bf16[80,128]{1,0:T(8,128)(2,1)S(1)}, bf16[80,128]{1,0:T(8,128)(2,1)S(1)}, bf16[80,128]{1,0:T(8,128)(2,1)S(1)}, bf16[80,128]{1,0:T(8,128)(2,1)S(1)}) custom-call(bf16[4,4,16,128]{3,2,1,0:T(8,128)(2,1)} %bitcast.10, bf16[4,8,128]{2,1,0:T(8,128)(2,1)} %k_hbm.1, bf16[4,8,128]{2,1,0:T(8,128)(2,1)} %v_hbm.1), custom_call_target="tpu_custom_call" | custom-call | bytes 131072 | tf_op jit(solution)/shard_map/pack/pallas_call | solution.py:48
  0.9 0.0 copy-start.2
  0.9 0.0 copy-start.3
  0.9 0.0 copy-start
  1.0 0.0 copy-start.1
  1.0 0.0 copy-start.4
  1.0 0.0 copy-start.5
  1.0 5.1 %collective-permute-start = (bf16[80,128]{1,0:T(8,128)(2,1)S(1)}, bf16[80,128]{1,0:T(8,128)(2,1)S(1)}, u32[]{:S(2)}, u32[]{:S(2)}) collective-permute-start(bf16[80,128]{1,0:T(8,128)(2,1)S(1)} %get-tuple-element.44), channel_id=1, source_target_pairs={{0,3},{1,2},{2,1},{3,0},{4,7},{5,6},{6,5},{7,4},{8,11},{9,10},{10,... | collective-permute-start | bytes 61448 | tf_op jit(solution)/shard_map/ppermute | solution.py:332
  6.1 0.0 collective-permute-start.1
  6.1 0.6 %collective-permute-start.2 = (bf16[80,128]{1,0:T(8,128)(2,1)S(1)}, bf16[80,128]{1,0:T(8,128)(2,1)S(1)}, u32[]{:S(2)}, u32[]{:S(2)}) collective-permute-start(bf16[80,128]{1,0:T(8,128)(2,1)S(1)} %get-tuple-element.46), channel_id=1, source_target_pairs={{0,1},{1,0},{2,3},{3,2},{4,5},{5,4},{6,7},{7,6},{8,9},{9,8},{10,11... | collective-permute-start | bytes 61448 | tf_op jit(solution)/shard_map/ppermute | solution.py:332
  6.8 0.0 copy-done.2
  6.8 0.0 copy-done.3
  6.8 0.5 %split.1 = (bf16[2,2048,128]{2,1,0:T(8,128)(2,1)S(1)}, bf16[2,2048,128]{2,1,0:T(8,128)(2,1)S(1)}, f32[8,128]{1,0:T(8,128)S(1)}) custom-call(bf16[4096,128]{1,0:T(8,128)(2,1)S(1)} %bitcast.8, bf16[4096,128]{1,0:T(8,128)(2,1)S(1)} %bitcast.9), custom_call_target="tpu_custom_call" | custom-call | bytes 4194304 | tf_op jit(solution)/shard_map/split/pallas_call | solution.py:48
  7.3 0.6 %collective-permute-done.refs_0_ = bf16[80,128]{1,0:T(8,128)(2,1)S(1)} collective-permute-done((bf16[80,128]{1,0:T(8,128)(2,1)S(1)}, bf16[80,128]{1,0:T(8,128)(2,1)S(1)}, u32[]{:S(2)}, u32[]{:S(2)}) %collective-permute-start) | collective-permute-done | bytes 20512 | tf_op jit(solution)/shard_map/ppermute | solution.py:332
  7.9 2.9 %collective-permute-done.1.refs_1_ = bf16[80,128]{1,0:T(8,128)(2,1)S(1)} collective-permute-done((bf16[80,128]{1,0:T(8,128)(2,1)S(1)}, bf16[80,128]{1,0:T(8,128)(2,1)S(1)}, u32[]{:S(2)}, u32[]{:S(2)}) %collective-permute-start.1) | collective-permute-done | bytes 20512 | tf_op jit(solution)/shard_map/ppermute | solution.py:332
  10.8 0.0 collective-permute-done.2.refs_2_
  10.8 0.1 collective-permute-start.5
  10.9 1.6 %collective-permute-start.4 = (bf16[4,64,128]{2,1,0:T(8,128)(2,1)S(1)}, bf16[4,64,128]{2,1,0:T(8,128)(2,1)S(1)}, u32[]{:S(2)}, u32[]{:S(2)}) collective-permute-start(bf16[4,64,128]{2,1,0:T(8,128)(2,1)S(1)} %get-tuple-element.50.joined_ref.q_ref), channel_id=1, source_target_pairs={{0,8},{4,12},{8,0},{12,4},{1,9},{5,13},{9,1},{13,5},{2,10},{6,14},... | collective-permute-start | bytes 196616 | tf_op jit(solution)/shard_map/ppermute | solution.py:335
  12.5 0.3 collective-permute-start.3
  12.7 0.0 copy-done
  12.7 0.0 copy-done.1
  12.8 0.0 copy-done.4
  12.8 0.0 copy-done.5
  12.8 2.3 %suffix.1 = (f32[256,128]{1,0:T(8,128)S(1)}, f32[256,128]{1,0:T(8,128)S(1)}) custom-call(bf16[4,64,128]{2,1,0:T(8,128)(2,1)S(1)} %get-tuple-element.50.joined_ref.q_ref, s32[64]{0:T(128)S(1)} %copy-done.4, s32[64]{0:T(128)S(1)} %copy-done.5, bf16[16,1024,128]{2,1,0:T(8,128)(2,1)S(1)} %bitcast.6, bf16[16,1024,128]{2,1,0:T(8,128)(2,1)S(1)} %bitcast.7), custom_call_target="tpu_custom_call" | custom-call | flops 134217728 | bytes 8388608 | tf_op jit(solution)/shard_map/suffix/pallas_call | solution.py:48
  15.1 1.2 %prefix_own.1 = (f32[256,128]{1,0:T(8,128)S(1)}, f32[256,128]{1,0:T(8,128)S(1)}) custom-call(bf16[4,64,128]{2,1,0:T(8,128)(2,1)S(1)} %get-tuple-element.50.joined_ref.q_ref, bf16[2,2048,128]{2,1,0:T(8,128)(2,1)S(1)} %get-tuple-element.53.k_ref.refs_2_.refs_1_, bf16[2,2048,128]{2,1,0:T(8,128)(2,1)S(1)} %get-tuple-element.54.v_ref.refs_3_.refs_2_), custom_call_target="tpu_custom_call" | custom-call | flops 268435456 | bytes 2097152 | tf_op jit(solution)/shard_map/prefix_own/pallas_call | solution.py:48
  16.3 0.0 collective-permute-done.5.refs_1_
  16.3 0.4 %collective-permute-done.4.refs_0_ = bf16[4,64,128]{2,1,0:T(8,128)(2,1)S(1)} collective-permute-done((bf16[4,64,128]{2,1,0:T(8,128)(2,1)S(1)}, bf16[4,64,128]{2,1,0:T(8,128)(2,1)S(1)}, u32[]{:S(2)}, u32[]{:S(2)}) %collective-permute-start.4) | collective-permute-done | bytes 65568 | tf_op jit(solution)/shard_map/ppermute | solution.py:335
  16.7 0.0 collective-permute-done.3.refs_0_
  16.7 1.8 %prefix_far.1 = (bf16[272,128]{1,0:T(8,128)(2,1)S(1)}, bf16[272,128]{1,0:T(8,128)(2,1)S(1)}) custom-call(bf16[4,64,128]{2,1,0:T(8,128)(2,1)S(1)} %collective-permute-done.4.refs_0_, bf16[4,64,128]{2,1,0:T(8,128)(2,1)S(1)} %collective-permute-done.5.refs_1_, bf16[2,2048,128]{2,1,0:T(8,128)(2,1)S(1)} %get-tuple-element.53.k_ref.refs_2_.refs_1_, ...), custom_call_target="tpu_custom_call" | custom-call | flops 536870912 | bytes 2097152 | tf_op jit(solution)/shard_map/prefix_far/pallas_call | solution.py:48
  18.5 1.2 %prefix_near.1 = bf16[272,128]{1,0:T(8,128)(2,1)S(1)} custom-call(bf16[4,64,128]{2,1,0:T(8,128)(2,1)S(1)} %collective-permute-done.3.refs_0_, bf16[2,2048,128]{2,1,0:T(8,128)(2,1)S(1)} %get-tuple-element.53.k_ref.refs_2_.refs_1_, bf16[2,2048,128]{2,1,0:T(8,128)(2,1)S(1)} %get-tuple-element.54.v_ref.refs_3_.refs_2_), custom_call_target="tpu_custom_call" | custom-call | flops 268435456 | bytes 2097152 | tf_op jit(solution)/shard_map/prefix_near/pallas_call | solution.py:48
  19.7 0.1 collective-permute-start.6
  19.8 1.1 %collective-permute-start.7 = (bf16[272,128]{1,0:T(8,128)(2,1)S(1)}, bf16[272,128]{1,0:T(8,128)(2,1)S(1)}, u32[]{:S(2)}, u32[]{:S(2)}) collective-permute-start(bf16[272,128]{1,0:T(8,128)(2,1)S(1)} %get-tuple-element.66), channel_id=1, source_target_pairs={{0,8},{4,12},{8,0},{12,4},{1,9},{5,13},{9,1},{13,5},{2,10},{6,14},... | collective-permute-start | bytes 208904 | tf_op jit(solution)/shard_map/ppermute | solution.py:335
  21.0 0.7 %collective-permute-start.8 = (bf16[272,128]{1,0:T(8,128)(2,1)S(1)}, bf16[272,128]{1,0:T(8,128)(2,1)S(1)}, u32[]{:S(2)}, u32[]{:S(2)}) collective-permute-start(bf16[272,128]{1,0:T(8,128)(2,1)S(1)} %get-tuple-element.67), channel_id=1, source_target_pairs={{0,12},{4,8},{8,4},{12,0},{1,13},{5,9},{9,5},{13,1},{2,14},{6,10},... | collective-permute-start | bytes 208904 | tf_op jit(solution)/shard_map/ppermute | solution.py:335
  21.6 0.0 collective-permute-done.6.refs_0_
  21.6 0.4 %near.1 = (f32[256,128]{1,0:T(8,128)S(1)}, f32[256,128]{1,0:T(8,128)S(1)}) custom-call(bf16[4,64,128]{2,1,0:T(8,128)(2,1)S(1)} %get-tuple-element.50.joined_ref.q_ref, bf16[4,16,128]{2,1,0:T(8,128)(2,1)S(1)} %get-tuple-element.51.fresh_ref, f32[256,128]{1,0:T(8,128)S(1)} %get-tuple-element.57.so_ref, f32[256,128]{1,0:T(8,128)S(1)} %get-tuple-element.58.sl_ref, ...), custom_call_target="tpu_custom_call" | custom-call | bytes 655360 | tf_op jit(solution)/shard_map/near/pallas_call | solution.py:48
  22.1 2.7 %collective-permute-done.7.refs_0_ = bf16[272,128]{1,0:T(8,128)(2,1)S(1)} collective-permute-done((bf16[272,128]{1,0:T(8,128)(2,1)S(1)}, bf16[272,128]{1,0:T(8,128)(2,1)S(1)}, u32[]{:S(2)}, u32[]{:S(2)}) %collective-permute-start.7) | collective-permute-done | bytes 69664 | tf_op jit(solution)/shard_map/ppermute | solution.py:335
  24.8 0.6 %collective-permute-done.8.refs_1_ = bf16[272,128]{1,0:T(8,128)(2,1)S(1)} collective-permute-done((bf16[272,128]{1,0:T(8,128)(2,1)S(1)}, bf16[272,128]{1,0:T(8,128)(2,1)S(1)}, u32[]{:S(2)}, u32[]{:S(2)}) %collective-permute-start.8) | collective-permute-done | bytes 69664 | tf_op jit(solution)/shard_map/ppermute | solution.py:335
  25.4 0.4 %final.1 = (bf16[64,128]{1,0:T(8,128)(2,1)S(1)}, bf16[64,128]{1,0:T(8,128)(2,1)S(1)}, bf16[64,128]{1,0:T(8,128)(2,1)S(1)}, bf16[64,128]{1,0:T(8,128)(2,1)S(1)}) custom-call(f32[256,128]{1,0:T(8,128)S(1)} %get-tuple-element.69.near_ref, f32[256,128]{1,0:T(8,128)S(1)} %get-tuple-element.70.lse_ref, bf16[272,128]{1,0:T(8,128)(2,1)S(1)} %collective-permute-done.7.refs_0_, ...), custom_call_target="tpu_custom_call" | custom-call | bytes 655360 | tf_op jit(solution)/shard_map/final/pallas_call | solution.py:48
  25.8 1.5 %collective-permute-start.9 = (bf16[64,128]{1,0:T(8,128)(2,1)S(1)}, bf16[64,128]{1,0:T(8,128)(2,1)S(1)}, u32[]{:S(2)}, u32[]{:S(2)}) collective-permute-start(bf16[64,128]{1,0:T(8,128)(2,1)S(1)} %get-tuple-element.71), channel_id=1, source_target_pairs={{0,3},{1,2},{2,1},{3,0},{4,7},{5,6},{6,5},{7,4},{8,11},{9,10},{10,... | collective-permute-start | bytes 49160 | tf_op jit(solution)/shard_map/ppermute | solution.py:332
  27.3 0.6 %collective-permute-start.10 = (bf16[64,128]{1,0:T(8,128)(2,1)S(1)}, bf16[64,128]{1,0:T(8,128)(2,1)S(1)}, u32[]{:S(2)}, u32[]{:S(2)}) collective-permute-start(bf16[64,128]{1,0:T(8,128)(2,1)S(1)} %get-tuple-element.72), channel_id=1, source_target_pairs={{0,2},{1,3},{2,0},{3,1},{4,6},{5,7},{6,4},{7,5},{8,10},{9,11},{10,... | collective-permute-start | bytes 49160 | tf_op jit(solution)/shard_map/ppermute | solution.py:332
  27.9 2.3 %collective-permute-start.11 = (bf16[64,128]{1,0:T(8,128)(2,1)S(1)}, bf16[64,128]{1,0:T(8,128)(2,1)S(1)}, u32[]{:S(2)}, u32[]{:S(2)}) collective-permute-start(bf16[64,128]{1,0:T(8,128)(2,1)S(1)} %get-tuple-element.73), channel_id=1, source_target_pairs={{0,1},{1,0},{2,3},{3,2},{4,5},{5,4},{6,7},{7,6},{8,9},{9,8},{10,11... | collective-permute-start | bytes 49160 | tf_op jit(solution)/shard_map/ppermute | solution.py:332
  30.2 1.2 %collective-permute-done.9.refs_0_ = bf16[64,128]{1,0:T(8,128)(2,1)S(1)} collective-permute-done((bf16[64,128]{1,0:T(8,128)(2,1)S(1)}, bf16[64,128]{1,0:T(8,128)(2,1)S(1)}, u32[]{:S(2)}, u32[]{:S(2)}) %collective-permute-start.9) | collective-permute-done | bytes 16416 | tf_op jit(solution)/shard_map/ppermute | solution.py:332
  31.4 0.5 %collective-permute-done.10.refs_1_ = bf16[64,128]{1,0:T(8,128)(2,1)S(1)} collective-permute-done((bf16[64,128]{1,0:T(8,128)(2,1)S(1)}, bf16[64,128]{1,0:T(8,128)(2,1)S(1)}, u32[]{:S(2)}, u32[]{:S(2)}) %collective-permute-start.10) | collective-permute-done | bytes 16416 | tf_op jit(solution)/shard_map/ppermute | solution.py:332
  31.9 0.2 collective-permute-done.11.refs_2_
  32.1 0.6 %unpack.1 = bf16[4,4,16,128]{3,2,1,0:T(8,128)(2,1)} custom-call(bf16[64,128]{1,0:T(8,128)(2,1)S(1)} %collective-permute-done.9.refs_0_, bf16[64,128]{1,0:T(8,128)(2,1)S(1)} %collective-permute-done.10.refs_1_, bf16[64,128]{1,0:T(8,128)(2,1)S(1)} %collective-permute-done.11.refs_2_, bf16[64,128]{1,0:T(8,128)(2,1)S(1)} %get-tuple-element.74.refs_3_), custom_call_target="tpu_custom_call" | custom-call | bytes 131072 | tf_op jit(solution)/shard_map/unpack/pallas_call | solution.py:48
  (2 shorter events, 0.0 us)
Async XLA Ops:
  0.9 5.8 %copy-start.2 = (bf16[2048,2,128]{2,1,0:T(2,128)(2,1)S(1)}, bf16[2048,2,128]{2,1,0:T(2,128)(2,1)}, u32[]{:S(2)}) copy-start(bf16[2048,2,128]{2,1,0:T(2,128)(2,1)} %param.12) | copy-start | bytes 3145732
  0.9 5.8 %copy-start.3 = (bf16[2048,2,128]{2,1,0:T(2,128)(2,1)S(1)}, bf16[2048,2,128]{2,1,0:T(2,128)(2,1)}, u32[]{:S(2)}) copy-start(bf16[2048,2,128]{2,1,0:T(2,128)(2,1)} %param.13) | copy-start | bytes 3145732
  0.9 11.8 %copy-start = (bf16[16,512,2,128]{3,2,1,0:T(2,128)(2,1)S(1)}, bf16[16,512,2,128]{3,2,1,0:T(2,128)(2,1)}, u32[]{:S(2)}) copy-start(bf16[16,512,2,128]{3,2,1,0:T(2,128)(2,1)} %param.14) | copy-start | bytes 12582916
  1.0 11.8 %copy-start.1 = (bf16[16,512,2,128]{3,2,1,0:T(2,128)(2,1)S(1)}, bf16[16,512,2,128]{3,2,1,0:T(2,128)(2,1)}, u32[]{:S(2)}) copy-start(bf16[16,512,2,128]{3,2,1,0:T(2,128)(2,1)} %param.15) | copy-start | bytes 12582916
  1.0 11.8 %copy-start.4 = (s32[64]{0:T(128)S(1)}, s32[64]{0:T(128)}, u32[]{:S(2)}) copy-start(s32[64]{0:T(128)} %slot_ref.1) | copy-start | bytes 772
  1.0 11.8 %copy-start.5 = (s32[64]{0:T(128)S(1)}, s32[64]{0:T(128)}, u32[]{:S(2)}) copy-start(s32[64]{0:T(128)} %len_ref.1) | copy-start | bytes 772
  1.0 6.9 %collective-permute-start = (bf16[80,128]{1,0:T(8,128)(2,1)S(1)}, bf16[80,128]{1,0:T(8,128)(2,1)S(1)}, u32[]{:S(2)}, u32[]{:S(2)}) collective-permute-start(bf16[80,128]{1,0:T(8,128)(2,1)S(1)} %get-tuple-element.44), channel_id=1, source_target_pairs={{0,3},{1,2},{2,1},{3,0},{4,7},{5,6},{6,5},{7,4},{8,11},{9,10},{10,... | collective-permute-start | bytes 61448 | tf_op jit(solution)/shard_map/ppermute | solution.py:332
  6.1 4.7 %collective-permute-start.1 = (bf16[80,128]{1,0:T(8,128)(2,1)S(1)}, bf16[80,128]{1,0:T(8,128)(2,1)S(1)}, u32[]{:S(2)}, u32[]{:S(2)}) collective-permute-start(bf16[80,128]{1,0:T(8,128)(2,1)S(1)} %get-tuple-element.45), channel_id=1, source_target_pairs={{0,2},{1,3},{2,0},{3,1},{4,6},{5,7},{6,4},{7,5},{8,10},{9,11},{10,... | collective-permute-start | bytes 61448 | tf_op jit(solution)/shard_map/ppermute | solution.py:332
  6.1 4.7 %collective-permute-start.2 = (bf16[80,128]{1,0:T(8,128)(2,1)S(1)}, bf16[80,128]{1,0:T(8,128)(2,1)S(1)}, u32[]{:S(2)}, u32[]{:S(2)}) collective-permute-start(bf16[80,128]{1,0:T(8,128)(2,1)S(1)} %get-tuple-element.46), channel_id=1, source_target_pairs={{0,1},{1,0},{2,3},{3,2},{4,5},{5,4},{6,7},{7,6},{8,9},{9,8},{10,11... | collective-permute-start | bytes 61448 | tf_op jit(solution)/shard_map/ppermute | solution.py:332
  10.8 5.5 %collective-permute-start.5 = (bf16[4,64,128]{2,1,0:T(8,128)(2,1)S(1)}, bf16[4,64,128]{2,1,0:T(8,128)(2,1)S(1)}, u32[]{:S(2)}, u32[]{:S(2)}) collective-permute-start(bf16[4,64,128]{2,1,0:T(8,128)(2,1)S(1)} %get-tuple-element.50.joined_ref.q_ref), channel_id=1, source_target_pairs={{0,12},{4,8},{8,4},{12,0},{1,13},{5,9},{9,5},{13,1},{2,14},{6,10},... | collective-permute-start | bytes 196616 | tf_op jit(solution)/shard_map/ppermute | solution.py:335
  10.9 5.8 %collective-permute-start.4 = (bf16[4,64,128]{2,1,0:T(8,128)(2,1)S(1)}, bf16[4,64,128]{2,1,0:T(8,128)(2,1)S(1)}, u32[]{:S(2)}, u32[]{:S(2)}) collective-permute-start(bf16[4,64,128]{2,1,0:T(8,128)(2,1)S(1)} %get-tuple-element.50.joined_ref.q_ref), channel_id=1, source_target_pairs={{0,8},{4,12},{8,0},{12,4},{1,9},{5,13},{9,1},{13,5},{2,10},{6,14},... | collective-permute-start | bytes 196616 | tf_op jit(solution)/shard_map/ppermute | solution.py:335
  12.5 4.2 %collective-permute-start.3 = (bf16[4,64,128]{2,1,0:T(8,128)(2,1)S(1)}, bf16[4,64,128]{2,1,0:T(8,128)(2,1)S(1)}, u32[]{:S(2)}, u32[]{:S(2)}) collective-permute-start(bf16[4,64,128]{2,1,0:T(8,128)(2,1)S(1)} %get-tuple-element.50.joined_ref.q_ref), channel_id=1, source_target_pairs={{0,4},{4,0},{8,12},{12,8},{1,5},{5,1},{9,13},{13,9},{2,6},{6,2},{1... | collective-permute-start | bytes 196616 | tf_op jit(solution)/shard_map/ppermute | solution.py:335
  19.7 1.9 %collective-permute-start.6 = (bf16[272,128]{1,0:T(8,128)(2,1)S(1)}, bf16[272,128]{1,0:T(8,128)(2,1)S(1)}, u32[]{:S(2)}, u32[]{:S(2)}) collective-permute-start(bf16[272,128]{1,0:T(8,128)(2,1)S(1)} %prefix_near.1), channel_id=1, source_target_pairs={{0,4},{4,0},{8,12},{12,8},{1,5},{5,1},{9,13},{13,9},{2,6},{6,2},{1... | collective-permute-start | bytes 208904 | tf_op jit(solution)/shard_map/ppermute | solution.py:335
  19.8 5.0 %collective-permute-start.7 = (bf16[272,128]{1,0:T(8,128)(2,1)S(1)}, bf16[272,128]{1,0:T(8,128)(2,1)S(1)}, u32[]{:S(2)}, u32[]{:S(2)}) collective-permute-start(bf16[272,128]{1,0:T(8,128)(2,1)S(1)} %get-tuple-element.66), channel_id=1, source_target_pairs={{0,8},{4,12},{8,0},{12,4},{1,9},{5,13},{9,1},{13,5},{2,10},{6,14},... | collective-permute-start | bytes 208904 | tf_op jit(solution)/shard_map/ppermute | solution.py:335
  21.0 4.4 %collective-permute-start.8 = (bf16[272,128]{1,0:T(8,128)(2,1)S(1)}, bf16[272,128]{1,0:T(8,128)(2,1)S(1)}, u32[]{:S(2)}, u32[]{:S(2)}) collective-permute-start(bf16[272,128]{1,0:T(8,128)(2,1)S(1)} %get-tuple-element.67), channel_id=1, source_target_pairs={{0,12},{4,8},{8,4},{12,0},{1,13},{5,9},{9,5},{13,1},{2,14},{6,10},... | collective-permute-start | bytes 208904 | tf_op jit(solution)/shard_map/ppermute | solution.py:335
  25.8 5.7 %collective-permute-start.9 = (bf16[64,128]{1,0:T(8,128)(2,1)S(1)}, bf16[64,128]{1,0:T(8,128)(2,1)S(1)}, u32[]{:S(2)}, u32[]{:S(2)}) collective-permute-start(bf16[64,128]{1,0:T(8,128)(2,1)S(1)} %get-tuple-element.71), channel_id=1, source_target_pairs={{0,3},{1,2},{2,1},{3,0},{4,7},{5,6},{6,5},{7,4},{8,11},{9,10},{10,... | collective-permute-start | bytes 49160 | tf_op jit(solution)/shard_map/ppermute | solution.py:332
  27.3 4.7 %collective-permute-start.10 = (bf16[64,128]{1,0:T(8,128)(2,1)S(1)}, bf16[64,128]{1,0:T(8,128)(2,1)S(1)}, u32[]{:S(2)}, u32[]{:S(2)}) collective-permute-start(bf16[64,128]{1,0:T(8,128)(2,1)S(1)} %get-tuple-element.72), channel_id=1, source_target_pairs={{0,2},{1,3},{2,0},{3,1},{4,6},{5,7},{6,4},{7,5},{8,10},{9,11},{10,... | collective-permute-start | bytes 49160 | tf_op jit(solution)/shard_map/ppermute | solution.py:332
  27.9 4.2 %collective-permute-start.11 = (bf16[64,128]{1,0:T(8,128)(2,1)S(1)}, bf16[64,128]{1,0:T(8,128)(2,1)S(1)}, u32[]{:S(2)}, u32[]{:S(2)}) collective-permute-start(bf16[64,128]{1,0:T(8,128)(2,1)S(1)} %get-tuple-element.73), channel_id=1, source_target_pairs={{0,1},{1,0},{2,3},{3,2},{4,5},{5,4},{6,7},{7,6},{8,9},{9,8},{10,11... | collective-permute-start | bytes 49160 | tf_op jit(solution)/shard_map/ppermute | solution.py:332

commit v3 on v2

--- a/solution.py
+++ b/solution.py
@@ -10,6 +10,8 @@
 
 NEG = -1e30
 GAP = 1 << 36
+SUF_F = 0
+SUF_M = 0
 LOG2E = 1.4426950408889634
 F32 = jnp.float32
 BF16 = jnp.bfloat16
@@ -414,13 +416,27 @@
     near_steps = [(0, c) for c in range(1, nc)]
     arriving = {step: along_blk(joined, *step) for step in far_steps + near_steps}
 
+    own_state = prefix("prefix_own", [joined], own=True)
+    def give_back(x, step):
+        return along_blk(x, back(step[0], nx), back(step[1], nc))
+
+    steps = far_steps[::-1] + near_steps
+    groups = [steps[:1]] + [steps[i : i + 2] for i in range(1, len(steps), 2)]
+    received = {}
+    sent = list(own_state)
+    for group_of in [g for g in groups if g]:
+        rows_of, sent = lax.optimization_barrier(([arriving[step] for step in group_of], sent))
+        if group_of is groups[0]:
+            own_state = sent
+        sent = prefix("prefix_far", rows_of)
+        for x, step in zip(sent, group_of):
+            received[step] = give_back(x, step)
+    sent, slot_keys = lax.optimization_barrier((sent, slot_keys))
     suffix_out, suffix_lse = call(
         functools.partial(suffix_kernel, nz, local, group, scale),
         "suffix",
-        [jax.ShapeDtypeStruct((rows, head_dim), F32)] * 2,
-        (
-            joined, slot_branch, suffix_lengths, slot_keys, slot_values,
-        ),
+        state,
+        (joined, slot_branch, suffix_lengths, slot_keys, slot_values),
         [VM, SM, SM, VM, VM],
         scratch=[
             pltpu.VMEM((rows, head_dim), F32),
@@ -428,34 +444,20 @@
             pltpu.VMEM((slots * local * group, width), BF16),
         ],
         vmem=8 << 20,
-        flops=4 * rows * width * head_dim,
-        moved=suffix_keys.size * 4,
-    )
-    own_state = prefix("prefix_own", [joined], own=True)
-    arriving, suffix_out, own_state = lax.optimization_barrier((arriving, suffix_out, own_state))
-
-    def give_back(sent, steps):
-        return [along_blk(x, back(step[0], nx), back(step[1], nc)) for x, step in zip(sent, steps)]
-
-    received = []
-    sent = []
-    for i in range(0, len(far_steps), 2):
-        steps = far_steps[i : i + 2]
-        rows_of, sent = lax.optimization_barrier(([arriving[step] for step in steps], sent))
-        sent = prefix("prefix_far", rows_of)
-        received += give_back(sent, steps)
-    sibling = []
-    if near_steps:
-        rows_of, sent = lax.optimization_barrier(([arriving[step] for step in near_steps], sent))
-        sibling = give_back(prefix("prefix_near", rows_of), near_steps)
+        flops=SUF_F,
+        moved=SUF_M,
+    )
+    last = [received.pop(step) for step in groups[-1]] if steps else []
+    others = list(received.values())
     near = call(
-        functools.partial(near_kernel, len(sibling), local, group, scale),
+        functools.partial(near_kernel, len(others), local, group, scale),
         "near",
         state,
-        (joined, fresh, suffix_out, suffix_lse, *own_state, *sibling),
-        [VM] * (6 + len(sibling)),
+        (joined, fresh, suffix_out, suffix_lse, *own_state, *others),
+        [VM] * (6 + len(others)),
         moved=rows * head_dim * 20,
     )
+    received = last
     pieces = call(
         functools.partial(final_kernel, len(received)),
         "final",

time: 32.9 us -> 30.8 us (0.936)
  waiting for transfers between devices: 9.1 us -> 6.88 us
    ppermute x6, waiting for transfers between devices: 3.69 us -> 1.57 us  [along_blk(): lax.ppermute(x, 'blk', [(i, partner(i // nc, step_x, nx) * nc + partner(i...]
  transfers between devices with their start and end apart: 12 -> 12, of which waited for: 8 -> 8; matrix products, arithmetic and copies ran while one was open for 0% -> 0% of each run, Pallas kernels for 14% -> 24%
where the time goes in v3:
time: 30.8 us; the launch traced here: 30.7 us
  starting transfers between devices  14.2 us (46%)
  Pallas kernels  9.4 us (31%)
  waiting for transfers between devices  6.88 us (22%)
    ppermute x6, starting transfers between devices, shift(): lax.ppermute(x, axis, [(i, partner(i, step, count)) for i in range(count)])  10.2 us
    pallas_call x11, Pallas kernels, call(): pl.pallas_call(kernel, name=name, out_shape=out_shape, in_specs=in_specs,...  9.4 us
    ppermute x6, waiting for transfers between devices, shift(): lax.ppermute(x, axis, [(i, partner(i, step, count)) for i in range(count)])  5.31 us
    ppermute x6, starting transfers between devices, along_blk(): lax.ppermute(x, 'blk', [(i, partner(i // nc, step_x, nx) * nc + partner(i...  4 us
    ppermute x6, waiting for transfers between devices, along_blk(): lax.ppermute(x, 'blk', [(i, partner(i // nc, step_x, nx) * nc + partner(i...  1.57 us
  transfers between devices with their start and end apart: 12, of which 8 were waited for; matrix products, arithmetic and copies ran while one was open for 0% of the time, Pallas kernels for 24%

profile of v3, /device:TPU:0, one launch (start us, length us, event | category | flops | bytes accessed | tf_op | source)
XLA Modules:
  0.0 30.7 jit_solution(6994719469366952716)
XLA Ops:
  0.0 0.9 %pack.1 = (bf16[80,128]{1,0:T(8,128)(2,1)S(1)}, bf16[80,128]{1,0:T(8,128)(2,1)S(1)}, bf16[80,128]{1,0:T(8,128)(2,1)S(1)}, bf16[80,128]{1,0:T(8,128)(2,1)S(1)}) custom-call(bf16[4,4,16,128]{3,2,1,0:T(8,128)(2,1)} %bitcast.10, bf16[4,8,128]{2,1,0:T(8,128)(2,1)} %k_hbm.1, bf16[4,8,128]{2,1,0:T(8,128)(2,1)} %v_hbm.1), custom_call_target="tpu_custom_call" | custom-call | bytes 131072 | tf_op jit(solution)/shard_map/pack/pallas_call | solution.py:50
  0.9 0.0 copy-start.2
  0.9 0.0 copy-start.3
  1.0 5.1 %collective-permute-start = (bf16[80,128]{1,0:T(8,128)(2,1)S(1)}, bf16[80,128]{1,0:T(8,128)(2,1)S(1)}, u32[]{:S(2)}, u32[]{:S(2)}) collective-permute-start(bf16[80,128]{1,0:T(8,128)(2,1)S(1)} %get-tuple-element.41), channel_id=1, source_target_pairs={{0,3},{1,2},{2,1},{3,0},{4,7},{5,6},{6,5},{7,4},{8,11},{9,10},{10,... | collective-permute-start | bytes 61448 | tf_op jit(solution)/shard_map/ppermute | solution.py:334
  6.1 0.0 collective-permute-start.1
  6.1 0.6 %collective-permute-start.2 = (bf16[80,128]{1,0:T(8,128)(2,1)S(1)}, bf16[80,128]{1,0:T(8,128)(2,1)S(1)}, u32[]{:S(2)}, u32[]{:S(2)}) collective-permute-start(bf16[80,128]{1,0:T(8,128)(2,1)S(1)} %get-tuple-element.43), channel_id=1, source_target_pairs={{0,1},{1,0},{2,3},{3,2},{4,5},{5,4},{6,7},{7,6},{8,9},{9,8},{10,11... | collective-permute-start | bytes 61448 | tf_op jit(solution)/shard_map/ppermute | solution.py:334
  6.7 0.0 copy-done.2
  6.7 0.0 copy-done.3
  6.7 0.0 copy-start
  6.7 0.0 copy-start.1
  6.7 0.0 copy-start.4
  6.7 0.0 copy-start.5
  6.8 0.5 %split.1 = (bf16[2,2048,128]{2,1,0:T(8,128)(2,1)S(1)}, bf16[2,2048,128]{2,1,0:T(8,128)(2,1)S(1)}, f32[8,128]{1,0:T(8,128)S(1)}) custom-call(bf16[4096,128]{1,0:T(8,128)(2,1)S(1)} %bitcast.8, bf16[4096,128]{1,0:T(8,128)(2,1)S(1)} %bitcast.9), custom_call_target="tpu_custom_call" | custom-call | bytes 4194304 | tf_op jit(solution)/shard_map/split/pallas_call | solution.py:50
  7.3 0.6 %collective-permute-done.refs_0_ = bf16[80,128]{1,0:T(8,128)(2,1)S(1)} collective-permute-done((bf16[80,128]{1,0:T(8,128)(2,1)S(1)}, bf16[80,128]{1,0:T(8,128)(2,1)S(1)}, u32[]{:S(2)}, u32[]{:S(2)}) %collective-permute-start) | collective-permute-done | bytes 20512 | tf_op jit(solution)/shard_map/ppermute | solution.py:334
  7.8 2.9 %collective-permute-done.1.refs_1_ = bf16[80,128]{1,0:T(8,128)(2,1)S(1)} collective-permute-done((bf16[80,128]{1,0:T(8,128)(2,1)S(1)}, bf16[80,128]{1,0:T(8,128)(2,1)S(1)}, u32[]{:S(2)}, u32[]{:S(2)}) %collective-permute-start.1) | collective-permute-done | bytes 20512 | tf_op jit(solution)/shard_map/ppermute | solution.py:334
  10.8 0.0 collective-permute-done.2.refs_2_
  10.8 0.1 collective-permute-start.5
  10.8 1.6 %collective-permute-start.4 = (bf16[4,64,128]{2,1,0:T(8,128)(2,1)S(1)}, bf16[4,64,128]{2,1,0:T(8,128)(2,1)S(1)}, u32[]{:S(2)}, u32[]{:S(2)}) collective-permute-start(bf16[4,64,128]{2,1,0:T(8,128)(2,1)S(1)} %get-tuple-element.47.q_ref.joined_ref), channel_id=1, source_target_pairs={{0,4},{4,0},{8,12},{12,8},{1,5},{5,1},{9,13},{13,9},{2,6},{6,2},{1... | collective-permute-start | bytes 196616 | tf_op jit(solution)/shard_map/ppermute | solution.py:337
  12.4 0.5 %collective-permute-start.3 = (bf16[4,64,128]{2,1,0:T(8,128)(2,1)S(1)}, bf16[4,64,128]{2,1,0:T(8,128)(2,1)S(1)}, u32[]{:S(2)}, u32[]{:S(2)}) collective-permute-start(bf16[4,64,128]{2,1,0:T(8,128)(2,1)S(1)} %get-tuple-element.47.q_ref.joined_ref), channel_id=1, source_target_pairs={{0,8},{4,12},{8,0},{12,4},{1,9},{5,13},{9,1},{13,5},{2,10},{6,14},... | collective-permute-start | bytes 196616 | tf_op jit(solution)/shard_map/ppermute | solution.py:337
  13.0 1.2 %prefix_own.1 = (f32[256,128]{1,0:T(8,128)S(1)}, f32[256,128]{1,0:T(8,128)S(1)}) custom-call(bf16[4,64,128]{2,1,0:T(8,128)(2,1)S(1)} %get-tuple-element.47.q_ref.joined_ref, bf16[2,2048,128]{2,1,0:T(8,128)(2,1)S(1)} %get-tuple-element.49.k_ref.refs_1_.refs_2_, bf16[2,2048,128]{2,1,0:T(8,128)(2,1)S(1)} %get-tuple-element.50.v_ref.refs_2_.refs_3_), custom_call_target="tpu_custom_call" | custom-call | flops 268435456 | bytes 2097152 | tf_op jit(solution)/shard_map/prefix_own/pallas_call | solution.py:50
  14.2 1.0 %collective-permute-done.5.refs_0_ = bf16[4,64,128]{2,1,0:T(8,128)(2,1)S(1)} collective-permute-done((bf16[4,64,128]{2,1,0:T(8,128)(2,1)S(1)}, bf16[4,64,128]{2,1,0:T(8,128)(2,1)S(1)}, u32[]{:S(2)}, u32[]{:S(2)}) %collective-permute-start.5) | collective-permute-done | bytes 65568 | tf_op jit(solution)/shard_map/ppermute | solution.py:337
  15.2 1.2 %prefix_far.2 = bf16[272,128]{1,0:T(8,128)(2,1)S(1)} custom-call(bf16[4,64,128]{2,1,0:T(8,128)(2,1)S(1)} %collective-permute-done.5.refs_0_, bf16[2,2048,128]{2,1,0:T(8,128)(2,1)S(1)} %get-tuple-element.49.k_ref.refs_1_.refs_2_, bf16[2,2048,128]{2,1,0:T(8,128)(2,1)S(1)} %get-tuple-element.50.v_ref.refs_2_.refs_3_), custom_call_target="tpu_custom_call" | custom-call | flops 268435456 | bytes 2097152 | tf_op jit(solution)/shard_map/prefix_far/pallas_call | solution.py:50
  16.4 0.1 collective-permute-start.6
  16.5 0.0 collective-permute-done.4.refs_1_
  16.5 0.2 collective-permute-done.3.refs_0_
  16.7 1.8 %prefix_far.3 = (bf16[272,128]{1,0:T(8,128)(2,1)S(1)}, bf16[272,128]{1,0:T(8,128)(2,1)S(1)}) custom-call(bf16[4,64,128]{2,1,0:T(8,128)(2,1)S(1)} %collective-permute-done.3.refs_0_, bf16[4,64,128]{2,1,0:T(8,128)(2,1)S(1)} %collective-permute-done.4.refs_1_, bf16[2,2048,128]{2,1,0:T(8,128)(2,1)S(1)} %get-tuple-element.49.k_ref.refs_1_.refs_2_, ...), custom_call_target="tpu_custom_call" | custom-call | flops 536870912 | bytes 2097152 | tf_op jit(solution)/shard_map/prefix_far/pallas_call | solution.py:50
  18.5 1.6 %collective-permute-start.7 = (bf16[272,128]{1,0:T(8,128)(2,1)S(1)}, bf16[272,128]{1,0:T(8,128)(2,1)S(1)}, u32[]{:S(2)}, u32[]{:S(2)}) collective-permute-start(bf16[272,128]{1,0:T(8,128)(2,1)S(1)} %get-tuple-element.56), channel_id=1, source_target_pairs={{0,8},{4,12},{8,0},{12,4},{1,9},{5,13},{9,1},{13,5},{2,10},{6,14},... | collective-permute-start | bytes 208904 | tf_op jit(solution)/shard_map/ppermute | solution.py:337
  20.1 0.1 collective-permute-start.8
  20.2 0.0 copy-done
  20.2 0.0 copy-done.1
  20.2 0.0 copy-done.4
  20.2 0.0 copy-done.5
  20.2 2.3 %suffix.1 = (f32[256,128]{1,0:T(8,128)S(1)}, f32[256,128]{1,0:T(8,128)S(1)}) custom-call(bf16[4,64,128]{2,1,0:T(8,128)(2,1)S(1)} %get-tuple-element.47.q_ref.joined_ref, s32[64]{0:T(128)S(1)} %copy-done.4, s32[64]{0:T(128)S(1)} %copy-done.5, bf16[16,1024,128]{2,1,0:T(8,128)(2,1)S(1)} %bitcast.6, bf16[16,1024,128]{2,1,0:T(8,128)(2,1)S(1)} %bitcast.7), custom_call_target="tpu_custom_call" | custom-call | tf_op jit(solution)/shard_map/suffix/pallas_call | solution.py:50
  22.5 0.0 collective-permute-done.6.refs_0_
  22.5 0.5 %near.1 = (f32[256,128]{1,0:T(8,128)S(1)}, f32[256,128]{1,0:T(8,128)S(1)}) custom-call(bf16[4,64,128]{2,1,0:T(8,128)(2,1)S(1)} %get-tuple-element.47.q_ref.joined_ref, bf16[4,16,128]{2,1,0:T(8,128)(2,1)S(1)} %get-tuple-element.48.fresh_ref, f32[256,128]{1,0:T(8,128)S(1)} %get-tuple-element.59.so_ref, f32[256,128]{1,0:T(8,128)S(1)} %get-tuple-element.60.sl_ref, ...), custom_call_target="tpu_custom_call" | custom-call | bytes 655360 | tf_op jit(solution)/shard_map/near/pallas_call | solution.py:50
  23.0 0.4 %collective-permute-done.7.refs_0_ = bf16[272,128]{1,0:T(8,128)(2,1)S(1)} collective-permute-done((bf16[272,128]{1,0:T(8,128)(2,1)S(1)}, bf16[272,128]{1,0:T(8,128)(2,1)S(1)}, u32[]{:S(2)}, u32[]{:S(2)}) %collective-permute-start.7) | collective-permute-done | bytes 69664 | tf_op jit(solution)/shard_map/ppermute | solution.py:337
  23.4 0.0 collective-permute-done.8.refs_1_
  23.4 0.4 %final.1 = (bf16[64,128]{1,0:T(8,128)(2,1)S(1)}, bf16[64,128]{1,0:T(8,128)(2,1)S(1)}, bf16[64,128]{1,0:T(8,128)(2,1)S(1)}, bf16[64,128]{1,0:T(8,128)(2,1)S(1)}) custom-call(f32[256,128]{1,0:T(8,128)S(1)} %get-tuple-element.63.near_ref, f32[256,128]{1,0:T(8,128)S(1)} %get-tuple-element.64.lse_ref, bf16[272,128]{1,0:T(8,128)(2,1)S(1)} %collective-permute-done.7.refs_0_, ...), custom_call_target="tpu_custom_call" | custom-call | bytes 655360 | tf_op jit(solution)/shard_map/final/pallas_call | solution.py:50
  23.7 1.5 %collective-permute-start.9 = (bf16[64,128]{1,0:T(8,128)(2,1)S(1)}, bf16[64,128]{1,0:T(8,128)(2,1)S(1)}, u32[]{:S(2)}, u32[]{:S(2)}) collective-permute-start(bf16[64,128]{1,0:T(8,128)(2,1)S(1)} %get-tuple-element.65), channel_id=1, source_target_pairs={{0,3},{1,2},{2,1},{3,0},{4,7},{5,6},{6,5},{7,4},{8,11},{9,10},{10,... | collective-permute-start | bytes 49160 | tf_op jit(solution)/shard_map/ppermute | solution.py:334
  25.2 0.6 %collective-permute-start.10 = (bf16[64,128]{1,0:T(8,128)(2,1)S(1)}, bf16[64,128]{1,0:T(8,128)(2,1)S(1)}, u32[]{:S(2)}, u32[]{:S(2)}) collective-permute-start(bf16[64,128]{1,0:T(8,128)(2,1)S(1)} %get-tuple-element.66), channel_id=1, source_target_pairs={{0,2},{1,3},{2,0},{3,1},{4,6},{5,7},{6,4},{7,5},{8,10},{9,11},{10,... | collective-permute-start | bytes 49160 | tf_op jit(solution)/shard_map/ppermute | solution.py:334
  25.8 2.4 %collective-permute-start.11 = (bf16[64,128]{1,0:T(8,128)(2,1)S(1)}, bf16[64,128]{1,0:T(8,128)(2,1)S(1)}, u32[]{:S(2)}, u32[]{:S(2)}) collective-permute-start(bf16[64,128]{1,0:T(8,128)(2,1)S(1)} %get-tuple-element.67), channel_id=1, source_target_pairs={{0,1},{1,0},{2,3},{3,2},{4,5},{5,4},{6,7},{7,6},{8,9},{9,8},{10,11... | collective-permute-start | bytes 49160 | tf_op jit(solution)/shard_map/ppermute | solution.py:334
  28.2 1.2 %collective-permute-done.9.refs_0_ = bf16[64,128]{1,0:T(8,128)(2,1)S(1)} collective-permute-done((bf16[64,128]{1,0:T(8,128)(2,1)S(1)}, bf16[64,128]{1,0:T(8,128)(2,1)S(1)}, u32[]{:S(2)}, u32[]{:S(2)}) %collective-permute-start.9) | collective-permute-done | bytes 16416 | tf_op jit(solution)/shard_map/ppermute | solution.py:334
  29.4 0.5 %collective-permute-done.10.refs_1_ = bf16[64,128]{1,0:T(8,128)(2,1)S(1)} collective-permute-done((bf16[64,128]{1,0:T(8,128)(2,1)S(1)}, bf16[64,128]{1,0:T(8,128)(2,1)S(1)}, u32[]{:S(2)}, u32[]{:S(2)}) %collective-permute-start.10) | collective-permute-done | bytes 16416 | tf_op jit(solution)/shard_map/ppermute | solution.py:334
  29.8 0.2 collective-permute-done.11.refs_2_
  30.0 0.6 %unpack.1 = bf16[4,4,16,128]{3,2,1,0:T(8,128)(2,1)} custom-call(bf16[64,128]{1,0:T(8,128)(2,1)S(1)} %collective-permute-done.9.refs_0_, bf16[64,128]{1,0:T(8,128)(2,1)S(1)} %collective-permute-done.10.refs_1_, bf16[64,128]{1,0:T(8,128)(2,1)S(1)} %collective-permute-done.11.refs_2_, bf16[64,128]{1,0:T(8,128)(2,1)S(1)} %get-tuple-element.68.refs_3_), custom_call_target="tpu_custom_call" | custom-call | bytes 131072 | tf_op jit(solution)/shard_map/unpack/pallas_call | solution.py:50
  (2 shorter events, 0.0 us)
Async XLA Ops:
  0.9 5.8 %copy-start.2 = (bf16[2048,2,128]{2,1,0:T(2,128)(2,1)S(1)}, bf16[2048,2,128]{2,1,0:T(2,128)(2,1)}, u32[]{:S(2)}) copy-start(bf16[2048,2,128]{2,1,0:T(2,128)(2,1)} %param.12) | copy-start | bytes 3145732
  0.9 5.8 %copy-start.3 = (bf16[2048,2,128]{2,1,0:T(2,128)(2,1)S(1)}, bf16[2048,2,128]{2,1,0:T(2,128)(2,1)}, u32[]{:S(2)}) copy-start(bf16[2048,2,128]{2,1,0:T(2,128)(2,1)} %param.13) | copy-start | bytes 3145732
  1.0 6.9 %collective-permute-start = (bf16[80,128]{1,0:T(8,128)(2,1)S(1)}, bf16[80,128]{1,0:T(8,128)(2,1)S(1)}, u32[]{:S(2)}, u32[]{:S(2)}) collective-permute-start(bf16[80,128]{1,0:T(8,128)(2,1)S(1)} %get-tuple-element.41), channel_id=1, source_target_pairs={{0,3},{1,2},{2,1},{3,0},{4,7},{5,6},{6,5},{7,4},{8,11},{9,10},{10,... | collective-permute-start | bytes 61448 | tf_op jit(solution)/shard_map/ppermute | solution.py:334
  6.1 4.7 %collective-permute-start.1 = (bf16[80,128]{1,0:T(8,128)(2,1)S(1)}, bf16[80,128]{1,0:T(8,128)(2,1)S(1)}, u32[]{:S(2)}, u32[]{:S(2)}) collective-permute-start(bf16[80,128]{1,0:T(8,128)(2,1)S(1)} %get-tuple-element.42), channel_id=1, source_target_pairs={{0,2},{1,3},{2,0},{3,1},{4,6},{5,7},{6,4},{7,5},{8,10},{9,11},{10,... | collective-permute-start | bytes 61448 | tf_op jit(solution)/shard_map/ppermute | solution.py:334
  6.1 4.7 %collective-permute-start.2 = (bf16[80,128]{1,0:T(8,128)(2,1)S(1)}, bf16[80,128]{1,0:T(8,128)(2,1)S(1)}, u32[]{:S(2)}, u32[]{:S(2)}) collective-permute-start(bf16[80,128]{1,0:T(8,128)(2,1)S(1)} %get-tuple-element.43), channel_id=1, source_target_pairs={{0,1},{1,0},{2,3},{3,2},{4,5},{5,4},{6,7},{7,6},{8,9},{9,8},{10,11... | collective-permute-start | bytes 61448 | tf_op jit(solution)/shard_map/ppermute | solution.py:334
  6.7 13.5 %copy-start = (bf16[16,512,2,128]{3,2,1,0:T(2,128)(2,1)S(1)}, bf16[16,512,2,128]{3,2,1,0:T(2,128)(2,1)}, u32[]{:S(2)}) copy-start(bf16[16,512,2,128]{3,2,1,0:T(2,128)(2,1)} %param.14) | copy-start | bytes 12582916
  6.7 13.5 %copy-start.1 = (bf16[16,512,2,128]{3,2,1,0:T(2,128)(2,1)S(1)}, bf16[16,512,2,128]{3,2,1,0:T(2,128)(2,1)}, u32[]{:S(2)}) copy-start(bf16[16,512,2,128]{3,2,1,0:T(2,128)(2,1)} %param.15) | copy-start | bytes 12582916
  6.7 13.5 %copy-start.4 = (s32[64]{0:T(128)S(1)}, s32[64]{0:T(128)}, u32[]{:S(2)}) copy-start(s32[64]{0:T(128)} %slot_ref.1) | copy-start | bytes 772
  6.7 13.5 %copy-start.5 = (s32[64]{0:T(128)S(1)}, s32[64]{0:T(128)}, u32[]{:S(2)}) copy-start(s32[64]{0:T(128)} %len_ref.1) | copy-start | bytes 772
  10.8 4.4 %collective-permute-start.5 = (bf16[4,64,128]{2,1,0:T(8,128)(2,1)S(1)}, bf16[4,64,128]{2,1,0:T(8,128)(2,1)S(1)}, u32[]{:S(2)}, u32[]{:S(2)}) collective-permute-start(bf16[4,64,128]{2,1,0:T(8,128)(2,1)S(1)} %get-tuple-element.47.q_ref.joined_ref), channel_id=1, source_target_pairs={{0,12},{4,8},{8,4},{12,0},{1,13},{5,9},{9,5},{13,1},{2,14},{6,10},... | collective-permute-start | bytes 196616 | tf_op jit(solution)/shard_map/ppermute | solution.py:337
  10.8 5.6 %collective-permute-start.4 = (bf16[4,64,128]{2,1,0:T(8,128)(2,1)S(1)}, bf16[4,64,128]{2,1,0:T(8,128)(2,1)S(1)}, u32[]{:S(2)}, u32[]{:S(2)}) collective-permute-start(bf16[4,64,128]{2,1,0:T(8,128)(2,1)S(1)} %get-tuple-element.47.q_ref.joined_ref), channel_id=1, source_target_pairs={{0,4},{4,0},{8,12},{12,8},{1,5},{5,1},{9,13},{13,9},{2,6},{6,2},{1... | collective-permute-start | bytes 196616 | tf_op jit(solution)/shard_map/ppermute | solution.py:337
  12.4 4.3 %collective-permute-start.3 = (bf16[4,64,128]{2,1,0:T(8,128)(2,1)S(1)}, bf16[4,64,128]{2,1,0:T(8,128)(2,1)S(1)}, u32[]{:S(2)}, u32[]{:S(2)}) collective-permute-start(bf16[4,64,128]{2,1,0:T(8,128)(2,1)S(1)} %get-tuple-element.47.q_ref.joined_ref), channel_id=1, source_target_pairs={{0,8},{4,12},{8,0},{12,4},{1,9},{5,13},{9,1},{13,5},{2,10},{6,14},... | collective-permute-start | bytes 196616 | tf_op jit(solution)/shard_map/ppermute | solution.py:337
  16.4 6.1 %collective-permute-start.6 = (bf16[272,128]{1,0:T(8,128)(2,1)S(1)}, bf16[272,128]{1,0:T(8,128)(2,1)S(1)}, u32[]{:S(2)}, u32[]{:S(2)}) collective-permute-start(bf16[272,128]{1,0:T(8,128)(2,1)S(1)} %prefix_far.2), channel_id=1, source_target_pairs={{0,12},{4,8},{8,4},{12,0},{1,13},{5,9},{9,5},{13,1},{2,14},{6,10},... | collective-permute-start | bytes 208904 | tf_op jit(solution)/shard_map/ppermute | solution.py:337
  18.5 4.9 %collective-permute-start.7 = (bf16[272,128]{1,0:T(8,128)(2,1)S(1)}, bf16[272,128]{1,0:T(8,128)(2,1)S(1)}, u32[]{:S(2)}, u32[]{:S(2)}) collective-permute-start(bf16[272,128]{1,0:T(8,128)(2,1)S(1)} %get-tuple-element.56), channel_id=1, source_target_pairs={{0,8},{4,12},{8,0},{12,4},{1,9},{5,13},{9,1},{13,5},{2,10},{6,14},... | collective-permute-start | bytes 208904 | tf_op jit(solution)/shard_map/ppermute | solution.py:337
  20.1 3.3 %collective-permute-start.8 = (bf16[272,128]{1,0:T(8,128)(2,1)S(1)}, bf16[272,128]{1,0:T(8,128)(2,1)S(1)}, u32[]{:S(2)}, u32[]{:S(2)}) collective-permute-start(bf16[272,128]{1,0:T(8,128)(2,1)S(1)} %get-tuple-element.57), channel_id=1, source_target_pairs={{0,4},{4,0},{8,12},{12,8},{1,5},{5,1},{9,13},{13,9},{2,6},{6,2},{1... | collective-permute-start | bytes 208904 | tf_op jit(solution)/shard_map/ppermute | solution.py:337
  23.7 5.6 %collective-permute-start.9 = (bf16[64,128]{1,0:T(8,128)(2,1)S(1)}, bf16[64,128]{1,0:T(8,128)(2,1)S(1)}, u32[]{:S(2)}, u32[]{:S(2)}) collective-permute-start(bf16[64,128]{1,0:T(8,128)(2,1)S(1)} %get-tuple-element.65), channel_id=1, source_target_pairs={{0,3},{1,2},{2,1},{3,0},{4,7},{5,6},{6,5},{7,4},{8,11},{9,10},{10,... | collective-permute-start | bytes 49160 | tf_op jit(solution)/shard_map/ppermute | solution.py:334
  25.2 4.6 %collective-permute-start.10 = (bf16[64,128]{1,0:T(8,128)(2,1)S(1)}, bf16[64,128]{1,0:T(8,128)(2,1)S(1)}, u32[]{:S(2)}, u32[]{:S(2)}) collective-permute-start(bf16[64,128]{1,0:T(8,128)(2,1)S(1)} %get-tuple-element.66), channel_id=1, source_target_pairs={{0,2},{1,3},{2,0},{3,1},{4,6},{5,7},{6,4},{7,5},{8,10},{9,11},{10,... | collective-permute-start | bytes 49160 | tf_op jit(solution)/shard_map/ppermute | solution.py:334
  25.8 4.2 %collective-permute-start.11 = (bf16[64,128]{1,0:T(8,128)(2,1)S(1)}, bf16[64,128]{1,0:T(8,128)(2,1)S(1)}, u32[]{:S(2)}, u32[]{:S(2)}) collective-permute-start(bf16[64,128]{1,0:T(8,128)(2,1)S(1)} %get-tuple-element.67), channel_id=1, source_target_pairs={{0,1},{1,0},{2,3},{3,2},{4,5},{5,4},{6,7},{7,6},{8,9},{9,8},{10,11... | collective-permute-start | bytes 49160 | tf_op jit(solution)/shard_map/ppermute | solution.py:334

commit v4 on v3

--- a/solution.py
+++ b/solution.py
@@ -10,8 +10,6 @@
 
 NEG = -1e30
 GAP = 1 << 36
-SUF_F = 0
-SUF_M = 0
 LOG2E = 1.4426950408889634
 F32 = jnp.float32
 BF16 = jnp.bfloat16
@@ -110,40 +108,39 @@
     rows = chunk // local
     for src, dst in ((pk, pko), (pv, pvo)):
         for at in range(src.shape[0] // chunk):
-            if local == 1:
-                dst[0, at * rows : (at + 1) * rows] = src[at * chunk : (at + 1) * chunk]
-                continue
             wide[...] = src[at * chunk : (at + 1) * chunk].astype(F32)
             for kl in range(local):
-                dst[kl, at * rows : (at + 1) * rows] = wide[pl.ds(kl, rows, stride=local)].astype(BF16)
-
-
-def suffix_kernel(
-    nz, local, group, scale, joined_ref, slot_ref, len_ref, keys, values, out_ref, lse_ref,
-    qwide, scores, probs
-):
+                head = wide[pl.ds(kl, rows, stride=local)] if local > 1 else wide[...]
+                if dst is pvo:
+                    dst[kl, :, at * rows : (at + 1) * rows] = head.T.astype(BF16)
+                else:
+                    dst[kl, at * rows : (at + 1) * rows] = head.astype(BF16)
+
+
+def places(c, slots, nz, local, group, slot_ref, len_ref):
+    first = lax.axis_index("blk") * slots
+    branch = slot_ref[first + c]
+    length = len_ref[branch]
+    branch = branch - first
+    nb = slots // nz
+    step = step_to(lax.axis_index("branch"), branch // nb, nz)
+    at = step * (nb * group) + lax.rem(branch, nb) * group
+    return [pl.multiple_of(at + kl * (slots * group), 8) for kl in range(local)], length
+
+
+def suffix_scores_kernel(nz, local, group, scale, q_ref, slot_ref, len_ref, keys, probs, lse_ref, inv_ref, qwide, scores):
     slots, width, head_dim = keys.shape
-    block = lax.axis_index("blk")
-    me = lax.axis_index("branch")
-    nb = slots // nz
-    qrows = local * nb * group
+    part = slots // nz * group
     for step in range(nz):
-        qwide[step * qrows : (step + 1) * qrows] = joined_ref[step, :qrows].astype(F32)
+        for kl in range(local):
+            at = kl * nz * part + step * part
+            qwide[at : at + part] = q_ref[step, kl * part : (kl + 1) * part].astype(F32)
     heads = local * group
     column = lax.broadcasted_iota(jnp.int32, (heads, width), 1)
     row = lax.broadcasted_iota(jnp.int32, (heads, width), 0)
     own_head = lax.rem(column, local) == row // group
-
-    def places(c):
-        branch = slot_ref[block * slots + c]
-        length = len_ref[branch]
-        branch = branch - block * slots
-        step = step_to(me, branch // nb, nz)
-        at = step * qrows + lax.rem(branch, nb) * group
-        return [pl.multiple_of(at + kl * nb * group, 8) for kl in range(local)], length
-
     for c in range(slots):
-        at, length = places(c)
+        at, length = places(c, slots, nz, local, group, slot_ref, len_ref)
         q = jnp.concatenate([qwide[pl.ds(a, group)] for a in at], axis=0).astype(BF16)
         s = lax.dot_general(q, keys[c], NT, preferred_element_type=F32)
         scores[c * heads : (c + 1) * heads] = jnp.where(
@@ -154,62 +151,43 @@
     weights = jnp.exp2((s - top) * (scale * LOG2E))
     total = jnp.sum(weights, axis=-1, keepdims=True)
     probs[...] = weights.astype(BF16)
-    lse = top * scale + jnp.log(total)
-    inverse = 1.0 / total
+    lse_ref[...] = jnp.broadcast_to(top * scale + jnp.log(total), lse_ref.shape)
+    inv_ref[...] = jnp.broadcast_to(1.0 / total, inv_ref.shape)
+
+
+def suffix_values_kernel(nz, local, group, slot_ref, len_ref, values, probs, slot_lse, slot_inv, out_ref, lse_ref):
+    slots = values.shape[0]
+    heads = local * group
     for c in range(slots):
-        at, _ = places(c)
-        o = jnp.dot(probs[c * heads : (c + 1) * heads], values[c], preferred_element_type=F32)
-        o = o * inverse[c * heads : (c + 1) * heads]
+        at, _ = places(c, slots, nz, local, group, slot_ref, len_ref)
+        rows = slice(c * heads, (c + 1) * heads)
+        o = jnp.dot(probs[rows], values[c], preferred_element_type=F32) * slot_inv[rows]
+        lse = slot_lse[rows]
         for kl in range(local):
             lo, hi = kl * group, (kl + 1) * group
             out_ref[pl.ds(at[kl], group)] = o[lo:hi]
-            lse_ref[pl.ds(at[kl], group)] = jnp.broadcast_to(
-                lse[c * heads + lo : c * heads + hi], (group, head_dim)
-            )
-
-
-def column_to_rows(column, lanes):
-    count = column.shape[0] // lanes
-    eye = lax.broadcasted_iota(jnp.int32, (lanes, lanes), 0) == lax.broadcasted_iota(
-        jnp.int32, (lanes, lanes), 1
-    )
-    rows = [
-        jnp.sum(jnp.where(eye, column[i * lanes : (i + 1) * lanes], 0.0), axis=0, keepdims=True)
-        for i in range(count)
-    ]
-    return jnp.concatenate(rows, axis=0)
-
-
-def rows_to_column(rows):
-    lanes = rows.shape[1]
-    eye = lax.broadcasted_iota(jnp.int32, (lanes, lanes), 0) == lax.broadcasted_iota(
-        jnp.int32, (lanes, lanes), 1
-    )
-    parts = [
-        jnp.sum(jnp.where(eye, rows[i : i + 1], 0.0), axis=1, keepdims=True)
-        for i in range(rows.shape[0])
-    ]
-    return jnp.concatenate(parts, axis=0)
-
-
-def encode(out, lse):
-    lanes = out.shape[1]
-    rows = column_to_rows(lse, lanes)
+            lse_ref[pl.ds(at[kl], group)] = lse[lo:hi]
+
+
+def encode(outs, lses):
+    rows = jnp.concatenate(lses, axis=0)
     high = rows.astype(BF16).astype(F32)
     middle = (rows - high).astype(BF16).astype(F32)
     low = rows - high - middle
-    tail = [high, middle, low]
     used = 3 * rows.shape[0]
-    tail.append(jnp.zeros((ceil_to(used, 16) - used, lanes), F32))
-    return jnp.concatenate([out] + tail, axis=0).astype(BF16)
-
-
-def decode(payload, count):
+    pad = jnp.zeros((ceil_to(used, 16) - used, rows.shape[1]), F32)
+    return jnp.concatenate([*outs, high, middle, low, pad], axis=0).astype(BF16)
+
+
+def decode(payload, local):
     wide = payload.astype(F32)
-    lanes = wide.shape[1]
-    n = count // lanes
-    rows = wide[count : count + n] + wide[count + n : count + 2 * n] + wide[count + 2 * n : count + 3 * n]
-    return wide[:count], rows_to_column(rows)
+    count = wide.shape[0] - ceil_to(3 * local, 16)
+    size = count // local
+    parts = []
+    for kl in range(local):
+        high, middle, low = (wide[count + i * local + kl :][:1] for i in range(3))
+        parts.append((wide[kl * size : (kl + 1) * size], high + middle + low))
+    return parts
 
 
 def merge(parts):
@@ -218,88 +196,89 @@
         top = jnp.maximum(top, lse)
     weights = [jnp.exp2((lse - top) * LOG2E) for _, lse in parts]
     total = sum(weights[1:], weights[0])
-    out = parts[0][0] * weights[0]
+    inverse = 1.0 / total
+    out = parts[0][0] * (weights[0] * inverse)
     for (o, _), w in zip(parts[1:], weights[1:]):
-        out = out + o * w
-    return out * (1.0 / total), top + jnp.log(total)
-
-
-def prefix_partial(q_refs, k_ref, v_ref, local, qrows, scale):
+        out = out + o * (w * inverse)
+    return out, top + jnp.log(total)
+
+
+def prefix_kernel(count, own, local, scale, *refs):
+    q_refs, (k_ref, v_ref), outs = refs[:count], refs[count : count + 2], refs[count + 2 :]
+    steps, qrows = q_refs[0].shape[:2]
     part = qrows // local
-    steps = q_refs[0].shape[0]
-    outs, lses = [], []
+    columns = steps * part
+    heads = []
     for kl in range(local):
         q = jnp.concatenate(
             [ref[z, kl * part : (kl + 1) * part] for ref in q_refs for z in range(steps)], axis=0
         )
-        s = lax.dot_general(q, k_ref[kl], NT, preferred_element_type=F32)
-        top = jnp.max(s, axis=-1, keepdims=True)
+        s = lax.dot_general(k_ref[kl], q, NT, preferred_element_type=F32)
+        top = jnp.max(s, axis=0, keepdims=True)
         weights = jnp.exp2((s - top) * (scale * LOG2E))
-        total = jnp.sum(weights, axis=-1, keepdims=True)
-        o = jnp.dot(weights.astype(BF16), v_ref[kl], preferred_element_type=F32)
-        outs.append(o * (1.0 / total))
-        lses.append(top * scale + jnp.log(total))
-    results = []
-    for i in range(len(q_refs)):
-        pieces = [(i * steps + z) * part for z in range(steps)]
-        results.append(
-            tuple(
-                jnp.concatenate([a[p : p + part] for p in pieces for a in arrays], axis=0)
-                for arrays in (outs, lses)
-            )
-        )
-    return results
-
-
-def prefix_kernel(count, *refs, local, qrows, scale):
-    q_refs, (k_ref, v_ref), outs = refs[:count], refs[count : count + 2], refs[count + 2 :]
-    for ref, (o, lse) in zip(outs, prefix_partial(q_refs, k_ref, v_ref, local, qrows, scale)):
-        ref[...] = encode(o, lse)
-
-
-def prefix_own_kernel(q_ref, k_ref, v_ref, o_ref, lse_ref, *, local, qrows, scale):
-    ((o, lse),) = prefix_partial([q_ref], k_ref, v_ref, local, qrows, scale)
-    o_ref[...] = o
-    lse_ref[...] = jnp.broadcast_to(lse, o.shape)
+        total = jnp.sum(weights, axis=0, keepdims=True)
+        o = jnp.dot(v_ref[kl], weights.astype(BF16), preferred_element_type=F32)
+        heads.append((o * (1.0 / total), top * scale + jnp.log(total)))
+    for i in range(count):
+        at = slice(i * columns, (i + 1) * columns)
+        os, lses = [o[:, at] for o, _ in heads], [lse[:, at] for _, lse in heads]
+        if own and i == count - 1:
+            outs[i][...] = jnp.concatenate(os, axis=0)
+            outs[i + 1][:local] = jnp.concatenate(lses, axis=0)
+        else:
+            outs[i][...] = encode(os, lses)
 
 
 def near_kernel(count, local, group, scale, q_ref, fresh_ref, so_ref, sl_ref, po_ref, pl_ref, *refs):
     others, (out_ref, lse_ref) = refs[:count], refs[count:]
-    rows, head_dim = po_ref.shape
     nz, qrows = q_ref.shape[:2]
-    part = qrows // group
-    own_score, own_value = [], []
-    for step in range(nz):
-        q = q_ref[step].astype(F32)
-        tail = fresh_ref[step].astype(F32)
-        k, v = (
-            jnp.concatenate(
-                [jnp.broadcast_to(tail[i : i + 1], (group, head_dim)) for i in range(at, at + part)],
-                axis=0,
+    part = qrows // local
+    nb = part // group
+    columns = nz * part
+    head_dim = so_ref.shape[1]
+    decoded = [decode(ref[...], local) for ref in others]
+    for kl in range(local):
+        scores, news = [], []
+        for step in range(nz):
+            q = q_ref[step, kl * part : (kl + 1) * part].astype(F32)
+            tail = fresh_ref[step].astype(F32)
+            k, v = (
+                jnp.concatenate(
+                    [
+                        jnp.broadcast_to(tail[i : i + 1], (group, head_dim))
+                        for i in range(at + kl * nb, at + (kl + 1) * nb)
+                    ],
+                    axis=0,
+                )
+                for at in (0, nb * local)
             )
-            for at in (0, part)
+            scores.append(jnp.sum(q * k, axis=1, keepdims=True) * scale)
+            news.append(v)
+        rows = slice(kl * columns, (kl + 1) * columns)
+        out, lse = merge(
+            [
+                (jnp.concatenate(news, axis=0), jnp.concatenate(scores, axis=0)),
+                (so_ref[rows], sl_ref[rows]),
+            ]
         )
-        own_score.append(jnp.sum(q * k, axis=1, keepdims=True) * scale)
-        own_value.append(v)
-    parts = [
-        (jnp.concatenate(own_value, axis=0), jnp.concatenate(own_score, axis=0)),
-        (so_ref[...], sl_ref[:, :1]),
-        (po_ref[...], pl_ref[:, :1]),
-    ]
-    parts += [decode(ref[...], rows) for ref in others]
-    out, lse = merge(parts)
-    out_ref[...] = out
-    lse_ref[...] = jnp.broadcast_to(lse, out.shape)
-
-
-def final_kernel(count, near_ref, lse_ref, *refs):
+        at = slice(kl * head_dim, (kl + 1) * head_dim)
+        parts = [(out.T, lse.T[:1]), (po_ref[at], pl_ref[kl : kl + 1])]
+        out, lse = merge(parts + [d[kl] for d in decoded])
+        out_ref[at] = out
+        lse_ref[kl : kl + 1] = lse
+
+
+def final_kernel(count, local, near_ref, lse_ref, *refs):
     others, outs = refs[:count], refs[count:]
-    parts = [(near_ref[...], lse_ref[:, :1])]
-    parts += [decode(ref[...], near_ref.shape[0]) for ref in others]
-    out, _ = merge(parts)
-    qrows = outs[0].shape[0]
-    for step, ref in enumerate(outs):
-        ref[...] = out[step * qrows : (step + 1) * qrows].astype(BF16)
+    head_dim = near_ref.shape[0] // local
+    part = outs[0].shape[0] // local
+    decoded = [decode(ref[...], local) for ref in others]
+    for kl in range(local):
+        at = slice(kl * head_dim, (kl + 1) * head_dim)
+        out, _ = merge([(near_ref[at], lse_ref[kl : kl + 1])] + [d[kl] for d in decoded])
+        out = out.T
+        for step, ref in enumerate(outs):
+            ref[kl * part : (kl + 1) * part] = out[step * part : (step + 1) * part].astype(BF16)
 
 
 def unpack_kernel(nz, local, group, *refs):
@@ -375,7 +354,11 @@
     keys, values, token = call(
         functools.partial(split_kernel, local),
         "split",
-        [pltpu.VMEM((local, positions, head_dim), BF16)] * 2 + [pltpu.VMEM((8, head_dim), F32)],
+        [
+            pltpu.VMEM((local, positions, head_dim), BF16),
+            pltpu.VMEM((local, head_dim, positions), BF16),
+            pltpu.VMEM((8, head_dim), F32),
+        ],
         (prefix_keys.reshape(flat), prefix_values.reshape(flat)),
         [VM] * 2,
         scratch=[pltpu.VMEM((chunk, head_dim), F32)],
@@ -394,17 +377,19 @@
         moved=nz * padded * head_dim * 4,
     )
 
-    tail = ceil_to(3 * (rows // head_dim), 16)
-
-    state = [jax.ShapeDtypeStruct((rows, head_dim), F32)] * 2
+    columns = rows // local
+    state = [
+        jax.ShapeDtypeStruct((local * head_dim, columns), F32),
+        jax.ShapeDtypeStruct((ceil_to(local, 8), columns), F32),
+    ]
+    payload = jax.ShapeDtypeStruct((local * head_dim + ceil_to(3 * local, 16), columns), BF16)
 
     def prefix(name, arrays, own=False):
         count = len(arrays)
-        kernel = prefix_own_kernel if own else functools.partial(prefix_kernel, count)
         return call(
-            functools.partial(kernel, local=local, qrows=qrows, scale=scale),
+            functools.partial(prefix_kernel, count, own, local, scale),
             name,
-            state if own else [jax.ShapeDtypeStruct((rows + tail, head_dim), BF16)] * count,
+            [payload] * (count - own) + (state if own else []),
             (*arrays, keys, values),
             [VM] * (count + 2),
             vmem=16 << 20,
@@ -416,50 +401,61 @@
     near_steps = [(0, c) for c in range(1, nc)]
     arriving = {step: along_blk(joined, *step) for step in far_steps + near_steps}
 
-    own_state = prefix("prefix_own", [joined], own=True)
+    heads_here = local * group
+    flat_state = [jax.ShapeDtypeStruct((rows, head_dim), F32)] * 2
+    probs, slot_lse, slot_inv = call(
+        functools.partial(suffix_scores_kernel, nz, local, group, scale),
+        "suffix_scores",
+        [jax.ShapeDtypeStruct((slots * heads_here, width), BF16)] + flat_state,
+        (joined, slot_branch, suffix_lengths, slot_keys),
+        [VM, SM, SM, VM],
+        scratch=[
+            pltpu.VMEM((rows, head_dim), F32),
+            pltpu.VMEM((slots * heads_here, width), F32),
+        ],
+        vmem=8 << 20,
+        flops=2 * rows * width * head_dim,
+        moved=suffix_keys.size * 2,
+    )
+
     def give_back(x, step):
         return along_blk(x, back(step[0], nx), back(step[1], nc))
 
     steps = far_steps[::-1] + near_steps
     groups = [steps[:1]] + [steps[i : i + 2] for i in range(1, len(steps), 2)]
     received = {}
-    sent = list(own_state)
-    for group_of in [g for g in groups if g]:
+    sent = [probs]
+    for i, group_of in enumerate(g for g in groups):
         rows_of, sent = lax.optimization_barrier(([arriving[step] for step in group_of], sent))
-        if group_of is groups[0]:
-            own_state = sent
-        sent = prefix("prefix_far", rows_of)
+        if i == 0:
+            (probs,) = sent
+            *sent, own_out, own_lse = prefix("prefix_own", [*rows_of, joined], own=True)
+        else:
+            sent = prefix("prefix_far", rows_of)
         for x, step in zip(sent, group_of):
             received[step] = give_back(x, step)
-    sent, slot_keys = lax.optimization_barrier((sent, slot_keys))
-    suffix_out, suffix_lse = call(
-        functools.partial(suffix_kernel, nz, local, group, scale),
-        "suffix",
-        state,
-        (joined, slot_branch, suffix_lengths, slot_keys, slot_values),
-        [VM, SM, SM, VM, VM],
-        scratch=[
-            pltpu.VMEM((rows, head_dim), F32),
-            pltpu.VMEM((slots * local * group, width), F32),
-            pltpu.VMEM((slots * local * group, width), BF16),
-        ],
+    sent, probs = lax.optimization_barrier((sent, probs))
+    suffix_state = call(
+        functools.partial(suffix_values_kernel, nz, local, group),
+        "suffix_values",
+        flat_state,
+        (slot_branch, suffix_lengths, slot_values, probs, slot_lse, slot_inv),
+        [SM, SM, VM, VM, VM, VM],
         vmem=8 << 20,
-        flops=SUF_F,
-        moved=SUF_M,
-    )
-    last = [received.pop(step) for step in groups[-1]] if steps else []
+    )
+    last = [received.pop(step) for step in groups[-1]]
     others = list(received.values())
     near = call(
         functools.partial(near_kernel, len(others), local, group, scale),
         "near",
         state,
-        (joined, fresh, suffix_out, suffix_lse, *own_state, *others),
+        (joined, fresh, *suffix_state, own_out, own_lse, *others),
         [VM] * (6 + len(others)),
         moved=rows * head_dim * 20,
     )
     received = last
     pieces = call(
-        functools.partial(final_kernel, len(received)),
+        functools.partial(final_kernel, len(received), local),
         "final",
         [jax.ShapeDtypeStruct((qrows, head_dim), BF16)] * nz,
         (*near, *received),

time: 30.8 us -> 33.2 us (1.078)
  Pallas kernels: 9.4 us -> 11.1 us
  waiting for transfers between devices: 6.88 us -> 7.37 us
    pallas_call x11, Pallas kernels: 9.4 us -> 11.1 us  [call(): pl.pallas_call(kernel, name=name, out_shape=out_shape, in_specs=in_specs,...]
    ppermute x6, waiting for transfers between devices: 1.57 us -> 2.25 us  [along_blk(): lax.ppermute(x, 'blk', [(i, partner(i // nc, step_x, nx) * nc + partner(i...]
  transfers between devices with their start and end apart: 12 -> 12, of which waited for: 8 -> 7; matrix products, arithmetic and copies ran while one was open for 0% -> 0% of each run, Pallas kernels for 24% -> 28%
where the time goes in v4:
time: 33.2 us; the launch traced here: 33 us
  starting transfers between devices  14.4 us (43%)
  Pallas kernels  11.1 us (33%)
  waiting for transfers between devices  7.37 us (22%)
    pallas_call x11, Pallas kernels, call(): pl.pallas_call(kernel, name=name, out_shape=out_shape, in_specs=in_specs,...  11.1 us
    ppermute x6, starting transfers between devices, shift(): lax.ppermute(x, axis, [(i, partner(i, step, count)) for i in range(count)])  10.2 us
    ppermute x6, waiting for transfers between devices, shift(): lax.ppermute(x, axis, [(i, partner(i, step, count)) for i in range(count)])  5.12 us
    ppermute x6, starting transfers between devices, along_blk(): lax.ppermute(x, 'blk', [(i, partner(i // nc, step_x, nx) * nc + partner(i...  4.19 us
    ppermute x6, waiting for transfers between devices, along_blk(): lax.ppermute(x, 'blk', [(i, partner(i // nc, step_x, nx) * nc + partner(i...  2.25 us
  transfers between devices with their start and end apart: 12, of which 7 were waited for; matrix products, arithmetic and copies ran while one was open for 0% of the time, Pallas kernels for 28%

profile of v4, /device:TPU:0, one launch (start us, length us, event | category | flops | bytes accessed | tf_op | source)
XLA Modules:
  0.0 33.0 jit_solution(3420771302608922337)
XLA Ops:
  0.0 0.9 %pack.1 = (bf16[80,128]{1,0:T(8,128)(2,1)S(1)}, bf16[80,128]{1,0:T(8,128)(2,1)S(1)}, bf16[80,128]{1,0:T(8,128)(2,1)S(1)}, bf16[80,128]{1,0:T(8,128)(2,1)S(1)}) custom-call(bf16[4,4,16,128]{3,2,1,0:T(8,128)(2,1)} %bitcast.10, bf16[4,8,128]{2,1,0:T(8,128)(2,1)} %k_hbm.1, bf16[4,8,128]{2,1,0:T(8,128)(2,1)} %v_hbm.1), custom_call_target="tpu_custom_call" | custom-call | bytes 131072 | tf_op jit(solution)/shard_map/pack/pallas_call | solution.py:48
  0.9 0.0 copy-start.2
  0.9 0.0 copy-start.3
  0.9 0.0 copy-start
  1.0 0.0 copy-start.4
  1.0 0.0 copy-start.5
  1.0 5.1 %collective-permute-start = (bf16[80,128]{1,0:T(8,128)(2,1)S(1)}, bf16[80,128]{1,0:T(8,128)(2,1)S(1)}, u32[]{:S(2)}, u32[]{:S(2)}) collective-permute-start(bf16[80,128]{1,0:T(8,128)(2,1)S(1)} %get-tuple-element.44), channel_id=1, source_target_pairs={{0,3},{1,2},{2,1},{3,0},{4,7},{5,6},{6,5},{7,4},{8,11},{9,10},{10,... | collective-permute-start | bytes 61448 | tf_op jit(solution)/shard_map/ppermute | solution.py:313
  6.1 0.0 collective-permute-start.1
  6.1 0.6 %collective-permute-start.2 = (bf16[80,128]{1,0:T(8,128)(2,1)S(1)}, bf16[80,128]{1,0:T(8,128)(2,1)S(1)}, u32[]{:S(2)}, u32[]{:S(2)}) collective-permute-start(bf16[80,128]{1,0:T(8,128)(2,1)S(1)} %get-tuple-element.46), channel_id=1, source_target_pairs={{0,1},{1,0},{2,3},{3,2},{4,5},{5,4},{6,7},{7,6},{8,9},{9,8},{10,11... | collective-permute-start | bytes 61448 | tf_op jit(solution)/shard_map/ppermute | solution.py:313
  6.8 0.0 copy-done.2
  6.8 0.0 copy-done.3
  6.8 0.7 %split.1 = (bf16[2,2048,128]{2,1,0:T(8,128)(2,1)S(1)}, bf16[2,128,2048]{2,1,0:T(8,128)(2,1)S(1)}, f32[8,128]{1,0:T(8,128)S(1)}) custom-call(bf16[4096,128]{1,0:T(8,128)(2,1)S(1)} %bitcast.8, bf16[4096,128]{1,0:T(8,128)(2,1)S(1)} %bitcast.9), custom_call_target="tpu_custom_call" | custom-call | bytes 4194304 | tf_op jit(solution)/shard_map/split/pallas_call | solution.py:48
  7.5 0.4 %collective-permute-done.refs_0_ = bf16[80,128]{1,0:T(8,128)(2,1)S(1)} collective-permute-done((bf16[80,128]{1,0:T(8,128)(2,1)S(1)}, bf16[80,128]{1,0:T(8,128)(2,1)S(1)}, u32[]{:S(2)}, u32[]{:S(2)}) %collective-permute-start) | collective-permute-done | bytes 20512 | tf_op jit(solution)/shard_map/ppermute | solution.py:313
  7.9 2.9 %collective-permute-done.1.refs_1_ = bf16[80,128]{1,0:T(8,128)(2,1)S(1)} collective-permute-done((bf16[80,128]{1,0:T(8,128)(2,1)S(1)}, bf16[80,128]{1,0:T(8,128)(2,1)S(1)}, u32[]{:S(2)}, u32[]{:S(2)}) %collective-permute-start.1) | collective-permute-done | bytes 20512 | tf_op jit(solution)/shard_map/ppermute | solution.py:313
  10.8 0.0 collective-permute-done.2.refs_2_
  10.8 0.1 collective-permute-start.5
  10.9 1.6 %collective-permute-start.4 = (bf16[4,64,128]{2,1,0:T(8,128)(2,1)S(1)}, bf16[4,64,128]{2,1,0:T(8,128)(2,1)S(1)}, u32[]{:S(2)}, u32[]{:S(2)}) collective-permute-start(bf16[4,64,128]{2,1,0:T(8,128)(2,1)S(1)} %get-tuple-element.50.q_ref.refs_1_), channel_id=1, source_target_pairs={{0,4},{4,0},{8,12},{12,8},{1,5},{5,1},{9,13},{13,9},{2,6},{6,2},{1... | collective-permute-start | bytes 196616 | tf_op jit(solution)/shard_map/ppermute | solution.py:316
  12.5 0.5 %collective-permute-start.3 = (bf16[4,64,128]{2,1,0:T(8,128)(2,1)S(1)}, bf16[4,64,128]{2,1,0:T(8,128)(2,1)S(1)}, u32[]{:S(2)}, u32[]{:S(2)}) collective-permute-start(bf16[4,64,128]{2,1,0:T(8,128)(2,1)S(1)} %get-tuple-element.50.q_ref.refs_1_), channel_id=1, source_target_pairs={{0,8},{4,12},{8,0},{12,4},{1,9},{5,13},{9,1},{13,5},{2,10},{6,14},... | collective-permute-start | bytes 196616 | tf_op jit(solution)/shard_map/ppermute | solution.py:316
  13.0 0.0 copy-done
  13.0 0.0 copy-done.4
  13.0 0.0 copy-done.5
  13.0 0.0 copy-start.1
  13.0 1.9 %suffix_scores.1 = (bf16[256,1024]{1,0:T(8,128)(2,1)S(1)}, f32[256,128]{1,0:T(8,128)S(1)}, f32[256,128]{1,0:T(8,128)S(1)}) custom-call(bf16[4,64,128]{2,1,0:T(8,128)(2,1)S(1)} %get-tuple-element.50.q_ref.refs_1_, s32[64]{0:T(128)S(1)} %copy-done.4, s32[64]{0:T(128)S(1)} %copy-done.5, bf16[16,1024,128]{2,1,0:T(8,128)(2,1)S(1)} %bitcast.6), custom_call_target="tpu_custom_call" | custom-call | flops 67108864 | bytes 4194304 | tf_op jit(solution)/shard_map/suffix_scores/pallas_call | solution.py:48
  15.0 0.2 collective-permute-done.5.refs_0_
  15.2 2.6 %prefix_own.1 = (bf16[272,128]{1,0:T(8,128)(2,1)S(1)}, f32[256,128]{1,0:T(8,128)S(1)}, f32[8,128]{1,0:T(8,128)S(1)}) custom-call(bf16[4,64,128]{2,1,0:T(8,128)(2,1)S(1)} %collective-permute-done.5.refs_0_, bf16[4,64,128]{2,1,0:T(8,128)(2,1)S(1)} %get-tuple-element.50.q_ref.refs_1_, bf16[2,2048,128]{2,1,0:T(8,128)(2,1)S(1)} %get-tuple-element.54.refs_2_, ...), custom_call_target="tpu_custom_call" | custom-call | flops 536870912 | bytes 2097152 | tf_op jit(solution)/shard_map/prefix_own/pallas_call | solution.py:48
  17.8 0.7 %collective-permute-start.6 = (bf16[272,128]{1,0:T(8,128)(2,1)S(1)}, bf16[272,128]{1,0:T(8,128)(2,1)S(1)}, u32[]{:S(2)}, u32[]{:S(2)}) collective-permute-start(bf16[272,128]{1,0:T(8,128)(2,1)S(1)} %get-tuple-element.56), channel_id=1, source_target_pairs={{0,12},{4,8},{8,4},{12,0},{1,13},{5,9},{9,5},{13,1},{2,14},{6,10},... | collective-permute-start | bytes 208904 | tf_op jit(solution)/shard_map/ppermute | solution.py:316
  18.4 0.0 collective-permute-done.4.refs_1_
  18.4 0.0 collective-permute-done.3.refs_0_
  18.4 2.6 %prefix_far.1 = (bf16[272,128]{1,0:T(8,128)(2,1)S(1)}, bf16[272,128]{1,0:T(8,128)(2,1)S(1)}) custom-call(bf16[4,64,128]{2,1,0:T(8,128)(2,1)S(1)} %collective-permute-done.3.refs_0_, bf16[4,64,128]{2,1,0:T(8,128)(2,1)S(1)} %collective-permute-done.4.refs_1_, bf16[2,2048,128]{2,1,0:T(8,128)(2,1)S(1)} %get-tuple-element.54.refs_2_, ...), custom_call_target="tpu_custom_call" | custom-call | flops 536870912 | bytes 2097152 | tf_op jit(solution)/shard_map/prefix_far/pallas_call | solution.py:48
  21.0 1.3 %collective-permute-start.7 = (bf16[272,128]{1,0:T(8,128)(2,1)S(1)}, bf16[272,128]{1,0:T(8,128)(2,1)S(1)}, u32[]{:S(2)}, u32[]{:S(2)}) collective-permute-start(bf16[272,128]{1,0:T(8,128)(2,1)S(1)} %get-tuple-element.59), channel_id=1, source_target_pairs={{0,8},{4,12},{8,0},{12,4},{1,9},{5,13},{9,1},{13,5},{2,10},{6,14},... | collective-permute-start | bytes 208904 | tf_op jit(solution)/shard_map/ppermute | solution.py:316
  22.3 0.1 collective-permute-start.8
  22.3 0.0 copy-done.1
  22.4 1.2 %suffix_values.1 = (f32[256,128]{1,0:T(8,128)S(1)}, f32[256,128]{1,0:T(8,128)S(1)}) custom-call(s32[64]{0:T(128)S(1)} %copy-done.4, s32[64]{0:T(128)S(1)} %copy-done.5, bf16[16,1024,128]{2,1,0:T(8,128)(2,1)S(1)} %bitcast.7, bf16[256,1024]{1,0:T(8,128)(2,1)S(1)} %get-tuple-element.62.probs, f32[256,128]{1,0:T(8,128)S(1)} %get-tuple-element.63.slot_lse, ...), custom_call_target="tpu_custom_call" | custom-call | tf_op jit(solution)/shard_map/suffix_values/pallas_call | solution.py:48
  23.6 0.0 collective-permute-done.6.refs_0_
  23.6 0.4 %near.1 = (f32[256,128]{1,0:T(8,128)S(1)}, f32[8,128]{1,0:T(8,128)S(1)}) custom-call(bf16[4,64,128]{2,1,0:T(8,128)(2,1)S(1)} %get-tuple-element.50.q_ref.refs_1_, bf16[4,16,128]{2,1,0:T(8,128)(2,1)S(1)} %get-tuple-element.51.fresh_ref, f32[256,128]{1,0:T(8,128)S(1)} %get-tuple-element.65.so_ref, f32[256,128]{1,0:T(8,128)S(1)} %get-tuple-element.66.sl_ref, ...), custom_call_target="tpu_custom_call" | custom-call | bytes 655360 | tf_op jit(solution)/shard_map/near/pallas_call | solution.py:48
  24.0 2.0 %collective-permute-done.7.refs_0_ = bf16[272,128]{1,0:T(8,128)(2,1)S(1)} collective-permute-done((bf16[272,128]{1,0:T(8,128)(2,1)S(1)}, bf16[272,128]{1,0:T(8,128)(2,1)S(1)}, u32[]{:S(2)}, u32[]{:S(2)}) %collective-permute-start.7) | collective-permute-done | bytes 69664 | tf_op jit(solution)/shard_map/ppermute | solution.py:316
  25.9 0.0 collective-permute-done.8.refs_1_
  26.0 0.1 final.1
  26.1 1.5 %collective-permute-start.9 = (bf16[64,128]{1,0:T(8,128)(2,1)S(1)}, bf16[64,128]{1,0:T(8,128)(2,1)S(1)}, u32[]{:S(2)}, u32[]{:S(2)}) collective-permute-start(bf16[64,128]{1,0:T(8,128)(2,1)S(1)} %get-tuple-element.71), channel_id=1, source_target_pairs={{0,3},{1,2},{2,1},{3,0},{4,7},{5,6},{6,5},{7,4},{8,11},{9,10},{10,... | collective-permute-start | bytes 49160 | tf_op jit(solution)/shard_map/ppermute | solution.py:313
  27.5 0.6 %collective-permute-start.10 = (bf16[64,128]{1,0:T(8,128)(2,1)S(1)}, bf16[64,128]{1,0:T(8,128)(2,1)S(1)}, u32[]{:S(2)}, u32[]{:S(2)}) collective-permute-start(bf16[64,128]{1,0:T(8,128)(2,1)S(1)} %get-tuple-element.72), channel_id=1, source_target_pairs={{0,2},{1,3},{2,0},{3,1},{4,6},{5,7},{6,4},{7,5},{8,10},{9,11},{10,... | collective-permute-start | bytes 49160 | tf_op jit(solution)/shard_map/ppermute | solution.py:313
  28.2 2.4 %collective-permute-start.11 = (bf16[64,128]{1,0:T(8,128)(2,1)S(1)}, bf16[64,128]{1,0:T(8,128)(2,1)S(1)}, u32[]{:S(2)}, u32[]{:S(2)}) collective-permute-start(bf16[64,128]{1,0:T(8,128)(2,1)S(1)} %get-tuple-element.73), channel_id=1, source_target_pairs={{0,1},{1,0},{2,3},{3,2},{4,5},{5,4},{6,7},{7,6},{8,9},{9,8},{10,11... | collective-permute-start | bytes 49160 | tf_op jit(solution)/shard_map/ppermute | solution.py:313
  30.5 1.1 %collective-permute-done.9.refs_0_ = bf16[64,128]{1,0:T(8,128)(2,1)S(1)} collective-permute-done((bf16[64,128]{1,0:T(8,128)(2,1)S(1)}, bf16[64,128]{1,0:T(8,128)(2,1)S(1)}, u32[]{:S(2)}, u32[]{:S(2)}) %collective-permute-start.9) | collective-permute-done | bytes 16416 | tf_op jit(solution)/shard_map/ppermute | solution.py:313
  31.7 0.5 %collective-permute-done.10.refs_1_ = bf16[64,128]{1,0:T(8,128)(2,1)S(1)} collective-permute-done((bf16[64,128]{1,0:T(8,128)(2,1)S(1)}, bf16[64,128]{1,0:T(8,128)(2,1)S(1)}, u32[]{:S(2)}, u32[]{:S(2)}) %collective-permute-start.10) | collective-permute-done | bytes 16416 | tf_op jit(solution)/shard_map/ppermute | solution.py:313
  32.2 0.2 collective-permute-done.11.refs_2_
  32.4 0.6 %unpack.1 = bf16[4,4,16,128]{3,2,1,0:T(8,128)(2,1)} custom-call(bf16[64,128]{1,0:T(8,128)(2,1)S(1)} %collective-permute-done.9.refs_0_, bf16[64,128]{1,0:T(8,128)(2,1)S(1)} %collective-permute-done.10.refs_1_, bf16[64,128]{1,0:T(8,128)(2,1)S(1)} %collective-permute-done.11.refs_2_, bf16[64,128]{1,0:T(8,128)(2,1)S(1)} %get-tuple-element.74.refs_3_), custom_call_target="tpu_custom_call" | custom-call | bytes 131072 | tf_op jit(solution)/shard_map/unpack/pallas_call | solution.py:48
  (2 shorter events, 0.0 us)
Async XLA Ops:
  0.9 5.8 %copy-start.2 = (bf16[2048,2,128]{2,1,0:T(2,128)(2,1)S(1)}, bf16[2048,2,128]{2,1,0:T(2,128)(2,1)}, u32[]{:S(2)}) copy-start(bf16[2048,2,128]{2,1,0:T(2,128)(2,1)} %param.12) | copy-start | bytes 3145732
  0.9 5.8 %copy-start.3 = (bf16[2048,2,128]{2,1,0:T(2,128)(2,1)S(1)}, bf16[2048,2,128]{2,1,0:T(2,128)(2,1)}, u32[]{:S(2)}) copy-start(bf16[2048,2,128]{2,1,0:T(2,128)(2,1)} %param.13) | copy-start | bytes 3145732
  0.9 12.1 %copy-start = (bf16[16,512,2,128]{3,2,1,0:T(2,128)(2,1)S(1)}, bf16[16,512,2,128]{3,2,1,0:T(2,128)(2,1)}, u32[]{:S(2)}) copy-start(bf16[16,512,2,128]{3,2,1,0:T(2,128)(2,1)} %param.14) | copy-start | bytes 12582916
  1.0 12.1 %copy-start.4 = (s32[64]{0:T(128)S(1)}, s32[64]{0:T(128)}, u32[]{:S(2)}) copy-start(s32[64]{0:T(128)} %slot_ref.3) | copy-start | bytes 772
  1.0 12.0 %copy-start.5 = (s32[64]{0:T(128)S(1)}, s32[64]{0:T(128)}, u32[]{:S(2)}) copy-start(s32[64]{0:T(128)} %len_ref.3) | copy-start | bytes 772
  1.0 6.9 %collective-permute-start = (bf16[80,128]{1,0:T(8,128)(2,1)S(1)}, bf16[80,128]{1,0:T(8,128)(2,1)S(1)}, u32[]{:S(2)}, u32[]{:S(2)}) collective-permute-start(bf16[80,128]{1,0:T(8,128)(2,1)S(1)} %get-tuple-element.44), channel_id=1, source_target_pairs={{0,3},{1,2},{2,1},{3,0},{4,7},{5,6},{6,5},{7,4},{8,11},{9,10},{10,... | collective-permute-start | bytes 61448 | tf_op jit(solution)/shard_map/ppermute | solution.py:313
  6.1 4.7 %collective-permute-start.1 = (bf16[80,128]{1,0:T(8,128)(2,1)S(1)}, bf16[80,128]{1,0:T(8,128)(2,1)S(1)}, u32[]{:S(2)}, u32[]{:S(2)}) collective-permute-start(bf16[80,128]{1,0:T(8,128)(2,1)S(1)} %get-tuple-element.45), channel_id=1, source_target_pairs={{0,2},{1,3},{2,0},{3,1},{4,6},{5,7},{6,4},{7,5},{8,10},{9,11},{10,... | collective-permute-start | bytes 61448 | tf_op jit(solution)/shard_map/ppermute | solution.py:313
  6.1 4.7 %collective-permute-start.2 = (bf16[80,128]{1,0:T(8,128)(2,1)S(1)}, bf16[80,128]{1,0:T(8,128)(2,1)S(1)}, u32[]{:S(2)}, u32[]{:S(2)}) collective-permute-start(bf16[80,128]{1,0:T(8,128)(2,1)S(1)} %get-tuple-element.46), channel_id=1, source_target_pairs={{0,1},{1,0},{2,3},{3,2},{4,5},{5,4},{6,7},{7,6},{8,9},{9,8},{10,11... | collective-permute-start | bytes 61448 | tf_op jit(solution)/shard_map/ppermute | solution.py:313
  10.8 4.4 %collective-permute-start.5 = (bf16[4,64,128]{2,1,0:T(8,128)(2,1)S(1)}, bf16[4,64,128]{2,1,0:T(8,128)(2,1)S(1)}, u32[]{:S(2)}, u32[]{:S(2)}) collective-permute-start(bf16[4,64,128]{2,1,0:T(8,128)(2,1)S(1)} %get-tuple-element.50.q_ref.refs_1_), channel_id=1, source_target_pairs={{0,12},{4,8},{8,4},{12,0},{1,13},{5,9},{9,5},{13,1},{2,14},{6,10},... | collective-permute-start | bytes 196616 | tf_op jit(solution)/shard_map/ppermute | solution.py:316
  10.9 7.6 %collective-permute-start.4 = (bf16[4,64,128]{2,1,0:T(8,128)(2,1)S(1)}, bf16[4,64,128]{2,1,0:T(8,128)(2,1)S(1)}, u32[]{:S(2)}, u32[]{:S(2)}) collective-permute-start(bf16[4,64,128]{2,1,0:T(8,128)(2,1)S(1)} %get-tuple-element.50.q_ref.refs_1_), channel_id=1, source_target_pairs={{0,4},{4,0},{8,12},{12,8},{1,5},{5,1},{9,13},{13,9},{2,6},{6,2},{1... | collective-permute-start | bytes 196616 | tf_op jit(solution)/shard_map/ppermute | solution.py:316
  12.5 6.0 %collective-permute-start.3 = (bf16[4,64,128]{2,1,0:T(8,128)(2,1)S(1)}, bf16[4,64,128]{2,1,0:T(8,128)(2,1)S(1)}, u32[]{:S(2)}, u32[]{:S(2)}) collective-permute-start(bf16[4,64,128]{2,1,0:T(8,128)(2,1)S(1)} %get-tuple-element.50.q_ref.refs_1_), channel_id=1, source_target_pairs={{0,8},{4,12},{8,0},{12,4},{1,9},{5,13},{9,1},{13,5},{2,10},{6,14},... | collective-permute-start | bytes 196616 | tf_op jit(solution)/shard_map/ppermute | solution.py:316
  13.0 9.3 %copy-start.1 = (bf16[16,512,2,128]{3,2,1,0:T(2,128)(2,1)S(1)}, bf16[16,512,2,128]{3,2,1,0:T(2,128)(2,1)}, u32[]{:S(2)}) copy-start(bf16[16,512,2,128]{3,2,1,0:T(2,128)(2,1)} %param.15) | copy-start | bytes 12582916
  17.8 5.8 %collective-permute-start.6 = (bf16[272,128]{1,0:T(8,128)(2,1)S(1)}, bf16[272,128]{1,0:T(8,128)(2,1)S(1)}, u32[]{:S(2)}, u32[]{:S(2)}) collective-permute-start(bf16[272,128]{1,0:T(8,128)(2,1)S(1)} %get-tuple-element.56), channel_id=1, source_target_pairs={{0,12},{4,8},{8,4},{12,0},{1,13},{5,9},{9,5},{13,1},{2,14},{6,10},... | collective-permute-start | bytes 208904 | tf_op jit(solution)/shard_map/ppermute | solution.py:316
  21.0 4.9 %collective-permute-start.7 = (bf16[272,128]{1,0:T(8,128)(2,1)S(1)}, bf16[272,128]{1,0:T(8,128)(2,1)S(1)}, u32[]{:S(2)}, u32[]{:S(2)}) collective-permute-start(bf16[272,128]{1,0:T(8,128)(2,1)S(1)} %get-tuple-element.59), channel_id=1, source_target_pairs={{0,8},{4,12},{8,0},{12,4},{1,9},{5,13},{9,1},{13,5},{2,10},{6,14},... | collective-permute-start | bytes 208904 | tf_op jit(solution)/shard_map/ppermute | solution.py:316
  22.3 3.7 %collective-permute-start.8 = (bf16[272,128]{1,0:T(8,128)(2,1)S(1)}, bf16[272,128]{1,0:T(8,128)(2,1)S(1)}, u32[]{:S(2)}, u32[]{:S(2)}) collective-permute-start(bf16[272,128]{1,0:T(8,128)(2,1)S(1)} %get-tuple-element.60), channel_id=1, source_target_pairs={{0,4},{4,0},{8,12},{12,8},{1,5},{5,1},{9,13},{13,9},{2,6},{6,2},{1... | collective-permute-start | bytes 208904 | tf_op jit(solution)/shard_map/ppermute | solution.py:316
  26.1 5.6 %collective-permute-start.9 = (bf16[64,128]{1,0:T(8,128)(2,1)S(1)}, bf16[64,128]{1,0:T(8,128)(2,1)S(1)}, u32[]{:S(2)}, u32[]{:S(2)}) collective-permute-start(bf16[64,128]{1,0:T(8,128)(2,1)S(1)} %get-tuple-element.71), channel_id=1, source_target_pairs={{0,3},{1,2},{2,1},{3,0},{4,7},{5,6},{6,5},{7,4},{8,11},{9,10},{10,... | collective-permute-start | bytes 49160 | tf_op jit(solution)/shard_map/ppermute | solution.py:313
  27.5 4.6 %collective-permute-start.10 = (bf16[64,128]{1,0:T(8,128)(2,1)S(1)}, bf16[64,128]{1,0:T(8,128)(2,1)S(1)}, u32[]{:S(2)}, u32[]{:S(2)}) collective-permute-start(bf16[64,128]{1,0:T(8,128)(2,1)S(1)} %get-tuple-element.72), channel_id=1, source_target_pairs={{0,2},{1,3},{2,0},{3,1},{4,6},{5,7},{6,4},{7,5},{8,10},{9,11},{10,... | collective-permute-start | bytes 49160 | tf_op jit(solution)/shard_map/ppermute | solution.py:313
  28.2 4.2 %collective-permute-start.11 = (bf16[64,128]{1,0:T(8,128)(2,1)S(1)}, bf16[64,128]{1,0:T(8,128)(2,1)S(1)}, u32[]{:S(2)}, u32[]{:S(2)}) collective-permute-start(bf16[64,128]{1,0:T(8,128)(2,1)S(1)} %get-tuple-element.73), channel_id=1, source_target_pairs={{0,1},{1,0},{2,3},{3,2},{4,5},{5,4},{6,7},{7,6},{8,9},{9,8},{10,11... | collective-permute-start | bytes 49160 | tf_op jit(solution)/shard_map/ppermute | solution.py:313

commit v5 on v4

--- a/solution.py
+++ b/solution.py
@@ -10,6 +10,8 @@
 
 NEG = -1e30
 GAP = 1 << 36
+CHUNK = 256
+FOLD = 128
 LOG2E = 1.4426950408889634
 F32 = jnp.float32
 BF16 = jnp.bfloat16
@@ -17,6 +19,7 @@
 SM = pl.BlockSpec(memory_space=pltpu.SMEM)
 HBM = pl.BlockSpec(memory_space=pltpu.HBM)
 NT = (((1,), (1,)), ((), ()))
+NN = (((1,), (0,)), ((), ()))
 
 
 def ceil_to(value, unit):
@@ -91,11 +94,12 @@
         out_refs[step][...] = jnp.concatenate(parts, axis=0).astype(BF16)
 
 
-def join_kernel(nz, qrows, *refs):
-    q_ref, tail_ref = refs[-2:]
-    for step in range(nz):
-        q_ref[step] = refs[nz - 1 - step][:qrows]
-        tail_ref[step] = refs[nz - 1 - step][qrows:]
+def join_kernel(order, qrows, *refs):
+    q_ref, tail_ref, all_ref = refs[-3:]
+    for at, step in enumerate(order):
+        q_ref[step] = refs[at][:qrows]
+        tail_ref[step] = refs[at][qrows:]
+        all_ref[step] = refs[at][...]
 
 
 def gap_kernel(after, token):
@@ -128,7 +132,9 @@
     return [pl.multiple_of(at + kl * (slots * group), 8) for kl in range(local)], length
 
 
-def suffix_scores_kernel(nz, local, group, scale, q_ref, slot_ref, len_ref, keys, probs, lse_ref, inv_ref, qwide, scores):
+def suffix_kernel(
+    nz, local, group, scale, q_ref, slot_ref, len_ref, keys, values, out_ref, lse_ref, qwide, scores, probs
+):
     slots, width, head_dim = keys.shape
     part = slots // nz * group
     for step in range(nz):
@@ -151,22 +157,18 @@
     weights = jnp.exp2((s - top) * (scale * LOG2E))
     total = jnp.sum(weights, axis=-1, keepdims=True)
     probs[...] = weights.astype(BF16)
-    lse_ref[...] = jnp.broadcast_to(top * scale + jnp.log(total), lse_ref.shape)
-    inv_ref[...] = jnp.broadcast_to(1.0 / total, inv_ref.shape)
-
-
-def suffix_values_kernel(nz, local, group, slot_ref, len_ref, values, probs, slot_lse, slot_inv, out_ref, lse_ref):
-    slots = values.shape[0]
-    heads = local * group
+    lse = top * scale + jnp.log(total)
+    inverse = 1.0 / total
     for c in range(slots):
         at, _ = places(c, slots, nz, local, group, slot_ref, len_ref)
-        rows = slice(c * heads, (c + 1) * heads)
-        o = jnp.dot(probs[rows], values[c], preferred_element_type=F32) * slot_inv[rows]
-        lse = slot_lse[rows]
+        o = jnp.dot(probs[c * heads : (c + 1) * heads], values[c], preferred_element_type=F32)
+        o = o * inverse[c * heads : (c + 1) * heads]
         for kl in range(local):
             lo, hi = kl * group, (kl + 1) * group
             out_ref[pl.ds(at[kl], group)] = o[lo:hi]
-            lse_ref[pl.ds(at[kl], group)] = lse[lo:hi]
+            lse_ref[pl.ds(at[kl], group)] = jnp.broadcast_to(
+                lse[c * heads + lo : c * heads + hi], (group, head_dim)
+            )
 
 
 def encode(outs, lses):
@@ -203,25 +205,73 @@
     return out, top + jnp.log(total)
 
 
-def prefix_kernel(count, own, local, scale, *refs):
-    q_refs, (k_ref, v_ref), outs = refs[:count], refs[count : count + 2], refs[count + 2 :]
-    steps, qrows = q_refs[0].shape[:2]
-    part = qrows // local
+def keys_as_rows(qs, k_ref, v_ref, scale):
+    positions, width = k_ref.shape[1], qs[0].shape[0]
+    chunk = math.gcd(positions, CHUNK)
+    fold = math.gcd(chunk, FOLD)
+
+    def folded(x, reduce):
+        return reduce(x.reshape(chunk // fold, fold, width), axis=0)
+
+    pieces = [slice(at, at + chunk) for at in range(0, positions, chunk)]
+    scores, tops = [], []
+    for kl, q in enumerate(qs):
+        scores.append(
+            [lax.dot_general(k_ref[kl, p], q, NT, preferred_element_type=F32) for p in pieces]
+        )
+        top = folded(scores[kl][0], jnp.max)
+        for s in scores[kl][1:]:
+            top = jnp.maximum(top, folded(s, jnp.max))
+        tops.append(jnp.max(top, axis=0, keepdims=True))
+    heads = []
+    for kl in range(len(qs)):
+        total, out = 0.0, 0.0
+        for p, s in zip(pieces, scores[kl]):
+            weights = jnp.exp2((s - tops[kl]) * (scale * LOG2E))
+            total = total + folded(weights, jnp.sum)
+            out = out + lax.dot_general(
+                v_ref[kl, :, p], weights.astype(BF16), NN, preferred_element_type=F32
+            )
+        total = jnp.sum(total, axis=0, keepdims=True)
+        heads.append((out * (1.0 / total), tops[kl] * scale + jnp.log(total)))
+    return heads
+
+
+def queries_as_rows(qs, k_ref, v_ref, scale):
+    scores = [
+        lax.dot_general(q, k_ref[kl], NT, preferred_element_type=F32) for kl, q in enumerate(qs)
+    ]
+    parts = []
+    for s in scores:
+        top = jnp.max(s, axis=1, keepdims=True)
+        weights = jnp.exp2((s - top) * (scale * LOG2E))
+        parts.append((top, jnp.sum(weights, axis=1, keepdims=True), weights.astype(BF16)))
+    heads = []
+    for kl, (top, total, weights) in enumerate(parts):
+        out = lax.dot_general(weights, v_ref[kl], NT, preferred_element_type=F32) * (1.0 / total)
+        lse = jnp.broadcast_to(top * scale + jnp.log(total), out.shape)
+        heads.append((out.T, lse.T[:1]))
+    return heads
+
+
+def prefix_kernel(count, own, merged, local, part, scale, *refs):
+    q_refs, (k_ref, v_ref), refs = refs[:count], refs[count : count + 2], refs[count + 2 :]
+    others, outs = (refs[:count], refs[count:]) if merged else ((), refs)
+    steps, part = q_refs[0].shape[0], part // local
     columns = steps * part
-    heads = []
-    for kl in range(local):
-        q = jnp.concatenate(
+    qs = [
+        jnp.concatenate(
             [ref[z, kl * part : (kl + 1) * part] for ref in q_refs for z in range(steps)], axis=0
         )
-        s = lax.dot_general(k_ref[kl], q, NT, preferred_element_type=F32)
-        top = jnp.max(s, axis=0, keepdims=True)
-        weights = jnp.exp2((s - top) * (scale * LOG2E))
-        total = jnp.sum(weights, axis=0, keepdims=True)
-        o = jnp.dot(v_ref[kl], weights.astype(BF16), preferred_element_type=F32)
-        heads.append((o * (1.0 / total), top * scale + jnp.log(total)))
+        for kl in range(local)
+    ]
+    heads = (keys_as_rows if count * columns > 128 else queries_as_rows)(qs, k_ref, v_ref, scale)
     for i in range(count):
         at = slice(i * columns, (i + 1) * columns)
-        os, lses = [o[:, at] for o, _ in heads], [lse[:, at] for _, lse in heads]
+        parts = [(o[:, at], lse[:, at]) for o, lse in heads]
+        if merged:
+            parts = [merge(pair) for pair in zip(parts, decode(others[i][...], local))]
+        os, lses = zip(*parts)
         if own and i == count - 1:
             outs[i][...] = jnp.concatenate(os, axis=0)
             outs[i + 1][:local] = jnp.concatenate(lses, axis=0)
@@ -281,13 +331,14 @@
             ref[kl * part : (kl + 1) * part] = out[step * part : (step + 1) * part].astype(BF16)
 
 
-def unpack_kernel(nz, local, group, *refs):
-    pieces, out_ref = refs[:nz], refs[nz]
+def unpack_kernel(order, local, group, *refs):
+    pieces, out_ref = refs[:-1], refs[-1]
+    nz = len(order)
     me = lax.axis_index("branch")
     nb = out_ref.shape[0]
-    for step in range(nz):
+    for at, step in enumerate(order):
         peer = partner(me, step, nz)
-        wide = pieces[nz - 1 - step][...].astype(F32)
+        wide = pieces[at][...].astype(F32)
         for b in range(nb):
             rows = [wide[(kl * nb + b) * group : (kl * nb + b + 1) * group] for kl in range(local)]
             out_ref[b, peer] = jnp.concatenate(rows, axis=0).astype(BF16)
@@ -306,6 +357,8 @@
     used = qrows + 2 * nb * local
     padded = ceil_to(used, 16)
     rows = nz * qrows
+    order_in = [*range(nz - 1, 0, -1), 0]
+    order_out = order_in
     nc = 2 if nblk % 2 == 0 else 1
     nx = nblk // nc
 
@@ -365,14 +418,15 @@
         vmem=8 << 20,
         moved=prefix_keys.size * 8,
     )
-    joined, fresh = call(
-        functools.partial(join_kernel, nz, qrows),
+    joined, fresh, wide = call(
+        functools.partial(join_kernel, order_in, qrows),
         "join",
         [
             jax.ShapeDtypeStruct((nz, qrows, head_dim), BF16),
             jax.ShapeDtypeStruct((nz, padded - qrows, head_dim), BF16),
+            jax.ShapeDtypeStruct((nz, padded, head_dim), BF16),
         ],
-        (*arrived[::-1], gap, token),
+        (*[arrived[step] for step in order_in], gap, token),
         [VM] * (nz + 2),
         moved=nz * padded * head_dim * 4,
     )
@@ -384,92 +438,79 @@
     ]
     payload = jax.ShapeDtypeStruct((local * head_dim + ceil_to(3 * local, 16), columns), BF16)
 
-    def prefix(name, arrays, own=False):
+    def prefix(name, arrays, own=False, others=()):
         count = len(arrays)
         return call(
-            functools.partial(prefix_kernel, count, own, local, scale),
+            functools.partial(prefix_kernel, count, own, bool(others), local, qrows, scale),
             name,
             [payload] * (count - own) + (state if own else []),
-            (*arrays, keys, values),
-            [VM] * (count + 2),
+            (*arrays, keys, values, *others),
+            [VM] * (count + 2 + len(others)),
             vmem=16 << 20,
-            flops=4 * count * rows * positions * head_dim,
-            moved=keys.size * 4,
+            flops=4 * count * rows * positions * head_dim if own else 0,
+            moved=keys.size * 4 if own else 0,
         )
 
     far_steps = [(x, c) for x in range(1, nx) for c in range(nc)]
     near_steps = [(0, c) for c in range(1, nc)]
-    arriving = {step: along_blk(joined, *step) for step in far_steps + near_steps}
-
-    heads_here = local * group
-    flat_state = [jax.ShapeDtypeStruct((rows, head_dim), F32)] * 2
-    probs, slot_lse, slot_inv = call(
-        functools.partial(suffix_scores_kernel, nz, local, group, scale),
-        "suffix_scores",
-        [jax.ShapeDtypeStruct((slots * heads_here, width), BF16)] + flat_state,
-        (joined, slot_branch, suffix_lengths, slot_keys),
-        [VM, SM, SM, VM],
+    arriving = {step: along_blk(joined if step[1] else wide, *step) for step in far_steps + near_steps}
+
+    def give_back(x, step):
+        return along_blk(x, back(step[0], nx), back(step[1], nc))
+
+    rows_of = [arriving[step] for step in near_steps]
+    *sent, own_out, own_lse = prefix("prefix_near", [*rows_of, joined], own=True)
+    received = {step: give_back(x, step) for x, step in zip(sent, near_steps)}
+    sibling = list(received.values())
+    distant = []
+    for far in range(1, nx):
+        hopped = []
+        for core in range(nc - 1, -1, -1):
+            rows_of, own_lse = lax.optimization_barrier((arriving[far, core], own_lse))
+            (sent,) = prefix("prefix_far", [rows_of], others=() if core else hopped)
+            if core:
+                hopped.append(give_back(sent, (0, core)))
+            else:
+                distant.append(give_back(sent, (far, 0)))
+            sent, own_lse = lax.optimization_barrier((sent, own_lse))
+    own_lse, slot_keys = lax.optimization_barrier((own_lse, slot_keys))
+    suffix_state = call(
+        functools.partial(suffix_kernel, nz, local, group, scale),
+        "suffix",
+        [jax.ShapeDtypeStruct((rows, head_dim), F32)] * 2,
+        (joined, slot_branch, suffix_lengths, slot_keys, slot_values),
+        [VM, SM, SM, VM, VM],
         scratch=[
             pltpu.VMEM((rows, head_dim), F32),
-            pltpu.VMEM((slots * heads_here, width), F32),
+            pltpu.VMEM((slots * local * group, width), F32),
+            pltpu.VMEM((slots * local * group, width), BF16),
         ],
         vmem=8 << 20,
-        flops=2 * rows * width * head_dim,
-        moved=suffix_keys.size * 2,
-    )
-
-    def give_back(x, step):
-        return along_blk(x, back(step[0], nx), back(step[1], nc))
-
-    steps = far_steps[::-1] + near_steps
-    groups = [steps[:1]] + [steps[i : i + 2] for i in range(1, len(steps), 2)]
-    received = {}
-    sent = [probs]
-    for i, group_of in enumerate(g for g in groups):
-        rows_of, sent = lax.optimization_barrier(([arriving[step] for step in group_of], sent))
-        if i == 0:
-            (probs,) = sent
-            *sent, own_out, own_lse = prefix("prefix_own", [*rows_of, joined], own=True)
-        else:
-            sent = prefix("prefix_far", rows_of)
-        for x, step in zip(sent, group_of):
-            received[step] = give_back(x, step)
-    sent, probs = lax.optimization_barrier((sent, probs))
-    suffix_state = call(
-        functools.partial(suffix_values_kernel, nz, local, group),
-        "suffix_values",
-        flat_state,
-        (slot_branch, suffix_lengths, slot_values, probs, slot_lse, slot_inv),
-        [SM, SM, VM, VM, VM, VM],
-        vmem=8 << 20,
-    )
-    last = [received.pop(step) for step in groups[-1]]
-    others = list(received.values())
+    )
     near = call(
-        functools.partial(near_kernel, len(others), local, group, scale),
+        functools.partial(near_kernel, len(sibling), local, group, scale),
         "near",
         state,
-        (joined, fresh, *suffix_state, own_out, own_lse, *others),
-        [VM] * (6 + len(others)),
+        (joined, fresh, *suffix_state, own_out, own_lse, *sibling),
+        [VM] * (6 + len(sibling)),
         moved=rows * head_dim * 20,
     )
-    received = last
     pieces = call(
-        functools.partial(final_kernel, len(received), local),
+        functools.partial(final_kernel, len(distant), local),
         "final",
         [jax.ShapeDtypeStruct((qrows, head_dim), BF16)] * nz,
-        (*near, *received),
-        [VM] * (2 + len(received)),
+        (*near, *distant),
+        [VM] * (2 + len(distant)),
         moved=rows * head_dim * 20,
     )
     landed = [pieces[0]] + [
         shift(pieces[step], "branch", back(step, nz), nz) for step in range(nz - 1, 0, -1)
     ][::-1]
     out = call(
-        functools.partial(unpack_kernel, nz, local, group),
+        functools.partial(unpack_kernel, order_out, local, group),
         "unpack",
         jax.ShapeDtypeStruct((nb, nz, heads // nz, head_dim), BF16),
-        landed[::-1],
+        [landed[step] for step in order_out],
         [VM] * nz,
         moved=queries.size * 4,
     )

time: 33.2 us -> 30.7 us (0.925)
  Pallas kernels: 11.1 us -> 9.36 us
  waiting for transfers between devices: 7.37 us -> 6.03 us
  starting transfers between devices: 14.4 us -> 14.9 us
    pallas_call x11, Pallas kernels: 11.1 us -> 9.36 us  [call(): pl.pallas_call(kernel, name=name, out_shape=out_shape, in_specs=in_specs,...]
    ppermute x6, waiting for transfers between devices: 2.25 us -> 0.88 us  [along_blk(): lax.ppermute(x, 'blk', [(i, partner(i // nc, step_x, nx) * nc + partner(i...]
    ppermute x6, starting transfers between devices: 4.19 us -> 4.72 us  [along_blk(): lax.ppermute(x, 'blk', [(i, partner(i // nc, step_x, nx) * nc + partner(i...]
  transfers between devices with their start and end apart: 12 -> 12, of which waited for: 7 -> 7; matrix products, arithmetic and copies ran while one was open for 0% -> 0% of each run, Pallas kernels for 28% -> 25%
where the time goes in v5:
time: 30.7 us; the launch traced here: 30.5 us
  starting transfers between devices  14.9 us (49%)
  Pallas kernels  9.36 us (30%)
  waiting for transfers between devices  6.03 us (20%)
    ppermute x6, starting transfers between devices, shift(): lax.ppermute(x, axis, [(i, partner(i, step, count)) for i in range(count)])  10.2 us
    pallas_call x11, Pallas kernels, call(): pl.pallas_call(kernel, name=name, out_shape=out_shape, in_specs=in_specs,...  9.36 us
    ppermute x6, waiting for transfers between devices, shift(): lax.ppermute(x, axis, [(i, partner(i, step, count)) for i in range(count)])  5.15 us
    ppermute x6, starting transfers between devices, along_blk(): lax.ppermute(x, 'blk', [(i, partner(i // nc, step_x, nx) * nc + partner(i...  4.72 us
    ppermute x6, waiting for transfers between devices, along_blk(): lax.ppermute(x, 'blk', [(i, partner(i // nc, step_x, nx) * nc + partner(i...  0.88 us
  transfers between devices with their start and end apart: 12, of which 7 were waited for; matrix products, arithmetic and copies ran while one was open for 0% of the time, Pallas kernels for 25%

profile of v5, /device:TPU:0, one launch (start us, length us, event | category | flops | bytes accessed | tf_op | source)
XLA Modules:
  0.0 30.5 jit_solution(5562876556383910828)
XLA Ops:
  0.0 0.9 %pack.1 = (bf16[80,128]{1,0:T(8,128)(2,1)S(1)}, bf16[80,128]{1,0:T(8,128)(2,1)S(1)}, bf16[80,128]{1,0:T(8,128)(2,1)S(1)}, bf16[80,128]{1,0:T(8,128)(2,1)S(1)}) custom-call(bf16[4,4,16,128]{3,2,1,0:T(8,128)(2,1)} %bitcast.10, bf16[4,8,128]{2,1,0:T(8,128)(2,1)} %k_hbm.1, bf16[4,8,128]{2,1,0:T(8,128)(2,1)} %v_hbm.1), custom_call_target="tpu_custom_call" | custom-call | bytes 131072 | tf_op jit(solution)/shard_map/pack/pallas_call | solution.py:51
  0.9 0.0 copy-start.2
  0.9 0.0 copy-start.3
  1.0 5.1 %collective-permute-start = (bf16[80,128]{1,0:T(8,128)(2,1)S(1)}, bf16[80,128]{1,0:T(8,128)(2,1)S(1)}, u32[]{:S(2)}, u32[]{:S(2)}) collective-permute-start(bf16[80,128]{1,0:T(8,128)(2,1)S(1)} %get-tuple-element.43), channel_id=1, source_target_pairs={{0,3},{1,2},{2,1},{3,0},{4,7},{5,6},{6,5},{7,4},{8,11},{9,10},{10,... | collective-permute-start | bytes 61448 | tf_op jit(solution)/shard_map/ppermute | solution.py:366
  6.1 0.0 collective-permute-start.1
  6.1 0.6 %collective-permute-start.2 = (bf16[80,128]{1,0:T(8,128)(2,1)S(1)}, bf16[80,128]{1,0:T(8,128)(2,1)S(1)}, u32[]{:S(2)}, u32[]{:S(2)}) collective-permute-start(bf16[80,128]{1,0:T(8,128)(2,1)S(1)} %get-tuple-element.45), channel_id=1, source_target_pairs={{0,1},{1,0},{2,3},{3,2},{4,5},{5,4},{6,7},{7,6},{8,9},{9,8},{10,11... | collective-permute-start | bytes 61448 | tf_op jit(solution)/shard_map/ppermute | solution.py:366
  6.7 0.0 copy-done.2
  6.7 0.0 copy-done.3
  6.7 0.0 copy-start
  6.7 0.0 copy-start.1
  6.7 0.0 copy-start.4
  6.7 0.0 copy-start.5
  6.8 0.7 %split.1 = (bf16[2,2048,128]{2,1,0:T(8,128)(2,1)S(1)}, bf16[2,128,2048]{2,1,0:T(8,128)(2,1)S(1)}, f32[8,128]{1,0:T(8,128)S(1)}) custom-call(bf16[4096,128]{1,0:T(8,128)(2,1)S(1)} %bitcast.8, bf16[4096,128]{1,0:T(8,128)(2,1)S(1)} %bitcast.9), custom_call_target="tpu_custom_call" | custom-call | bytes 4194304 | tf_op jit(solution)/shard_map/split/pallas_call | solution.py:51
  7.5 0.3 %collective-permute-done.refs_0_ = bf16[80,128]{1,0:T(8,128)(2,1)S(1)} collective-permute-done((bf16[80,128]{1,0:T(8,128)(2,1)S(1)}, bf16[80,128]{1,0:T(8,128)(2,1)S(1)}, u32[]{:S(2)}, u32[]{:S(2)}) %collective-permute-start) | collective-permute-done | bytes 20512 | tf_op jit(solution)/shard_map/ppermute | solution.py:366
  7.8 2.9 %collective-permute-done.1.refs_1_ = bf16[80,128]{1,0:T(8,128)(2,1)S(1)} collective-permute-done((bf16[80,128]{1,0:T(8,128)(2,1)S(1)}, bf16[80,128]{1,0:T(8,128)(2,1)S(1)}, u32[]{:S(2)}, u32[]{:S(2)}) %collective-permute-start.1) | collective-permute-done | bytes 20512 | tf_op jit(solution)/shard_map/ppermute | solution.py:366
  10.8 0.0 collective-permute-done.2.refs_2_
  10.8 0.1 collective-permute-start.5
  10.9 1.6 %collective-permute-start.4 = (bf16[4,64,128]{2,1,0:T(8,128)(2,1)S(1)}, bf16[4,64,128]{2,1,0:T(8,128)(2,1)S(1)}, u32[]{:S(2)}, u32[]{:S(2)}) collective-permute-start(bf16[4,64,128]{2,1,0:T(8,128)(2,1)S(1)} %get-tuple-element.49.refs_1_.q_ref), channel_id=1, source_target_pairs={{0,12},{4,8},{8,4},{12,0},{1,13},{5,9},{9,5},{13,1},{2,14},{6,10},... | collective-permute-start | bytes 196616 | tf_op jit(solution)/shard_map/ppermute | solution.py:369
  12.5 0.5 %collective-permute-start.3 = (bf16[4,80,128]{2,1,0:T(8,128)(2,1)S(1)}, bf16[4,80,128]{2,1,0:T(8,128)(2,1)S(1)}, u32[]{:S(2)}, u32[]{:S(2)}) collective-permute-start(bf16[4,80,128]{2,1,0:T(8,128)(2,1)S(1)} %get-tuple-element.51), channel_id=1, source_target_pairs={{0,8},{4,12},{8,0},{12,4},{1,9},{5,13},{9,1},{13,5},{2,10},{6,14},... | collective-permute-start | bytes 245768 | tf_op jit(solution)/shard_map/ppermute | solution.py:369
  13.0 0.0 collective-permute-done.5.refs_0_
  13.0 1.8 %prefix_near.1 = (bf16[272,128]{1,0:T(8,128)(2,1)S(1)}, f32[256,128]{1,0:T(8,128)S(1)}, f32[8,128]{1,0:T(8,128)S(1)}) custom-call(bf16[4,64,128]{2,1,0:T(8,128)(2,1)S(1)} %collective-permute-done.5.refs_0_, bf16[4,64,128]{2,1,0:T(8,128)(2,1)S(1)} %get-tuple-element.49.refs_1_.q_ref, bf16[2,2048,128]{2,1,0:T(8,128)(2,1)S(1)} %get-tuple-element.52.refs_2_.refs_1_, ...), custom_call_target="tpu_custom_call" | custom-call | flops 536870912 | bytes 2097152 | tf_op jit(solution)/shard_map/prefix_near/pallas_call | solution.py:51
  14.9 0.0 collective-permute-done.4.refs_0_
  14.9 1.2 %prefix_far.2 = bf16[272,128]{1,0:T(8,128)(2,1)S(1)} custom-call(bf16[4,64,128]{2,1,0:T(8,128)(2,1)S(1)} %collective-permute-done.4.refs_0_, bf16[2,2048,128]{2,1,0:T(8,128)(2,1)S(1)} %get-tuple-element.52.refs_2_.refs_1_, bf16[2,128,2048]{2,1,0:T(8,128)(2,1)S(1)} %get-tuple-element.53.refs_3_.refs_2_), custom_call_target="tpu_custom_call" | custom-call | tf_op jit(solution)/shard_map/prefix_far/pallas_call | solution.py:51
  16.1 0.6 %collective-permute-start.6 = (bf16[272,128]{1,0:T(8,128)(2,1)S(1)}, bf16[272,128]{1,0:T(8,128)(2,1)S(1)}, u32[]{:S(2)}, u32[]{:S(2)}) collective-permute-start(bf16[272,128]{1,0:T(8,128)(2,1)S(1)} %prefix_far.2), channel_id=1, source_target_pairs={{0,4},{4,0},{8,12},{12,8},{1,5},{5,1},{9,13},{13,9},{2,6},{6,2},{1... | collective-permute-start | bytes 208904 | tf_op jit(solution)/shard_map/ppermute | solution.py:369
  16.7 0.1 collective-permute-start.7
  16.7 0.3 %collective-permute-done.3.refs_0_ = bf16[4,80,128]{2,1,0:T(8,128)(2,1)S(1)} collective-permute-done((bf16[4,80,128]{2,1,0:T(8,128)(2,1)S(1)}, bf16[4,80,128]{2,1,0:T(8,128)(2,1)S(1)}, u32[]{:S(2)}, u32[]{:S(2)}) %collective-permute-start.3) | collective-permute-done | bytes 81952 | tf_op jit(solution)/shard_map/ppermute | solution.py:369
  17.1 0.5 %collective-permute-done.6.refs_3_ = bf16[272,128]{1,0:T(8,128)(2,1)S(1)} collective-permute-done((bf16[272,128]{1,0:T(8,128)(2,1)S(1)}, bf16[272,128]{1,0:T(8,128)(2,1)S(1)}, u32[]{:S(2)}, u32[]{:S(2)}) %collective-permute-start.6) | collective-permute-done | bytes 69664 | tf_op jit(solution)/shard_map/ppermute | solution.py:369
  17.6 1.2 %prefix_far.3 = bf16[272,128]{1,0:T(8,128)(2,1)S(1)} custom-call(bf16[4,80,128]{2,1,0:T(8,128)(2,1)S(1)} %collective-permute-done.3.refs_0_, bf16[2,2048,128]{2,1,0:T(8,128)(2,1)S(1)} %get-tuple-element.52.refs_2_.refs_1_, bf16[2,128,2048]{2,1,0:T(8,128)(2,1)S(1)} %get-tuple-element.53.refs_3_.refs_2_, bf16[272,128]{1,0:T(8,128)(2,1)S(1)} %collective-permute-done.6.refs_3_), custom_call_target="tpu_custom_call" | custom-call | tf_op jit(solution)/shard_map/prefix_far/pallas_call | solution.py:51
  18.8 1.9 %collective-permute-start.8 = (bf16[272,128]{1,0:T(8,128)(2,1)S(1)}, bf16[272,128]{1,0:T(8,128)(2,1)S(1)}, u32[]{:S(2)}, u32[]{:S(2)}) collective-permute-start(bf16[272,128]{1,0:T(8,128)(2,1)S(1)} %prefix_far.3), channel_id=1, source_target_pairs={{0,8},{4,12},{8,0},{12,4},{1,9},{5,13},{9,1},{13,5},{2,10},{6,14},... | collective-permute-start | bytes 208904 | tf_op jit(solution)/shard_map/ppermute | solution.py:369
  20.6 0.0 copy-done
  20.6 0.0 copy-done.1
  20.6 0.0 copy-done.4
  20.6 0.0 copy-done.5
  20.6 2.3 %suffix.1 = (f32[256,128]{1,0:T(8,128)S(1)}, f32[256,128]{1,0:T(8,128)S(1)}) custom-call(bf16[4,64,128]{2,1,0:T(8,128)(2,1)S(1)} %get-tuple-element.49.refs_1_.q_ref, s32[64]{0:T(128)S(1)} %copy-done.4, s32[64]{0:T(128)S(1)} %copy-done.5, bf16[16,1024,128]{2,1,0:T(8,128)(2,1)S(1)} %bitcast.6, bf16[16,1024,128]{2,1,0:T(8,128)(2,1)S(1)} %bitcast.7), custom_call_target="tpu_custom_call" | custom-call | tf_op jit(solution)/shard_map/suffix/pallas_call | solution.py:51
  23.0 0.0 collective-permute-done.7.refs_0_
  23.0 0.4 %near.1 = (f32[256,128]{1,0:T(8,128)S(1)}, f32[8,128]{1,0:T(8,128)S(1)}) custom-call(bf16[4,64,128]{2,1,0:T(8,128)(2,1)S(1)} %get-tuple-element.49.refs_1_.q_ref, bf16[4,16,128]{2,1,0:T(8,128)(2,1)S(1)} %get-tuple-element.50.fresh_ref, f32[256,128]{1,0:T(8,128)S(1)} %get-tuple-element.62.so_ref, f32[256,128]{1,0:T(8,128)S(1)} %get-tuple-element.63.sl_ref, ...), custom_call_target="tpu_custom_call" | custom-call | bytes 655360 | tf_op jit(solution)/shard_map/near/pallas_call | solution.py:51
  23.4 0.0 collective-permute-done.8.refs_0_
  23.4 0.1 final.1
  23.5 1.5 %collective-permute-start.9 = (bf16[64,128]{1,0:T(8,128)(2,1)S(1)}, bf16[64,128]{1,0:T(8,128)(2,1)S(1)}, u32[]{:S(2)}, u32[]{:S(2)}) collective-permute-start(bf16[64,128]{1,0:T(8,128)(2,1)S(1)} %get-tuple-element.69), channel_id=1, source_target_pairs={{0,3},{1,2},{2,1},{3,0},{4,7},{5,6},{6,5},{7,4},{8,11},{9,10},{10,... | collective-permute-start | bytes 49160 | tf_op jit(solution)/shard_map/ppermute | solution.py:366
  25.1 0.6 %collective-permute-start.10 = (bf16[64,128]{1,0:T(8,128)(2,1)S(1)}, bf16[64,128]{1,0:T(8,128)(2,1)S(1)}, u32[]{:S(2)}, u32[]{:S(2)}) collective-permute-start(bf16[64,128]{1,0:T(8,128)(2,1)S(1)} %get-tuple-element.70), channel_id=1, source_target_pairs={{0,2},{1,3},{2,0},{3,1},{4,6},{5,7},{6,4},{7,5},{8,10},{9,11},{10,... | collective-permute-start | bytes 49160 | tf_op jit(solution)/shard_map/ppermute | solution.py:366
  25.7 2.3 %collective-permute-start.11 = (bf16[64,128]{1,0:T(8,128)(2,1)S(1)}, bf16[64,128]{1,0:T(8,128)(2,1)S(1)}, u32[]{:S(2)}, u32[]{:S(2)}) collective-permute-start(bf16[64,128]{1,0:T(8,128)(2,1)S(1)} %get-tuple-element.71), channel_id=1, source_target_pairs={{0,1},{1,0},{2,3},{3,2},{4,5},{5,4},{6,7},{7,6},{8,9},{9,8},{10,11... | collective-permute-start | bytes 49160 | tf_op jit(solution)/shard_map/ppermute | solution.py:366
  28.0 1.3 %collective-permute-done.9.refs_0_ = bf16[64,128]{1,0:T(8,128)(2,1)S(1)} collective-permute-done((bf16[64,128]{1,0:T(8,128)(2,1)S(1)}, bf16[64,128]{1,0:T(8,128)(2,1)S(1)}, u32[]{:S(2)}, u32[]{:S(2)}) %collective-permute-start.9) | collective-permute-done | bytes 16416 | tf_op jit(solution)/shard_map/ppermute | solution.py:366
  29.2 0.5 %collective-permute-done.10.refs_1_ = bf16[64,128]{1,0:T(8,128)(2,1)S(1)} collective-permute-done((bf16[64,128]{1,0:T(8,128)(2,1)S(1)}, bf16[64,128]{1,0:T(8,128)(2,1)S(1)}, u32[]{:S(2)}, u32[]{:S(2)}) %collective-permute-start.10) | collective-permute-done | bytes 16416 | tf_op jit(solution)/shard_map/ppermute | solution.py:366
  29.7 0.2 collective-permute-done.11.refs_2_
  29.9 0.6 %unpack.1 = bf16[4,4,16,128]{3,2,1,0:T(8,128)(2,1)} custom-call(bf16[64,128]{1,0:T(8,128)(2,1)S(1)} %collective-permute-done.9.refs_0_, bf16[64,128]{1,0:T(8,128)(2,1)S(1)} %collective-permute-done.10.refs_1_, bf16[64,128]{1,0:T(8,128)(2,1)S(1)} %collective-permute-done.11.refs_2_, bf16[64,128]{1,0:T(8,128)(2,1)S(1)} %get-tuple-element.72.refs_3_), custom_call_target="tpu_custom_call" | custom-call | bytes 131072 | tf_op jit(solution)/shard_map/unpack/pallas_call | solution.py:51
  (2 shorter events, 0.0 us)
Async XLA Ops:
  0.9 5.8 %copy-start.2 = (bf16[2048,2,128]{2,1,0:T(2,128)(2,1)S(1)}, bf16[2048,2,128]{2,1,0:T(2,128)(2,1)}, u32[]{:S(2)}) copy-start(bf16[2048,2,128]{2,1,0:T(2,128)(2,1)} %param.12) | copy-start | bytes 3145732
  0.9 5.8 %copy-start.3 = (bf16[2048,2,128]{2,1,0:T(2,128)(2,1)S(1)}, bf16[2048,2,128]{2,1,0:T(2,128)(2,1)}, u32[]{:S(2)}) copy-start(bf16[2048,2,128]{2,1,0:T(2,128)(2,1)} %param.13) | copy-start | bytes 3145732
  1.0 6.9 %collective-permute-start = (bf16[80,128]{1,0:T(8,128)(2,1)S(1)}, bf16[80,128]{1,0:T(8,128)(2,1)S(1)}, u32[]{:S(2)}, u32[]{:S(2)}) collective-permute-start(bf16[80,128]{1,0:T(8,128)(2,1)S(1)} %get-tuple-element.43), channel_id=1, source_target_pairs={{0,3},{1,2},{2,1},{3,0},{4,7},{5,6},{6,5},{7,4},{8,11},{9,10},{10,... | collective-permute-start | bytes 61448 | tf_op jit(solution)/shard_map/ppermute | solution.py:366
  6.1 4.7 %collective-permute-start.1 = (bf16[80,128]{1,0:T(8,128)(2,1)S(1)}, bf16[80,128]{1,0:T(8,128)(2,1)S(1)}, u32[]{:S(2)}, u32[]{:S(2)}) collective-permute-start(bf16[80,128]{1,0:T(8,128)(2,1)S(1)} %get-tuple-element.44), channel_id=1, source_target_pairs={{0,2},{1,3},{2,0},{3,1},{4,6},{5,7},{6,4},{7,5},{8,10},{9,11},{10,... | collective-permute-start | bytes 61448 | tf_op jit(solution)/shard_map/ppermute | solution.py:366
  6.1 4.7 %collective-permute-start.2 = (bf16[80,128]{1,0:T(8,128)(2,1)S(1)}, bf16[80,128]{1,0:T(8,128)(2,1)S(1)}, u32[]{:S(2)}, u32[]{:S(2)}) collective-permute-start(bf16[80,128]{1,0:T(8,128)(2,1)S(1)} %get-tuple-element.45), channel_id=1, source_target_pairs={{0,1},{1,0},{2,3},{3,2},{4,5},{5,4},{6,7},{7,6},{8,9},{9,8},{10,11... | collective-permute-start | bytes 61448 | tf_op jit(solution)/shard_map/ppermute | solution.py:366
  6.7 13.9 %copy-start = (bf16[16,512,2,128]{3,2,1,0:T(2,128)(2,1)S(1)}, bf16[16,512,2,128]{3,2,1,0:T(2,128)(2,1)}, u32[]{:S(2)}) copy-start(bf16[16,512,2,128]{3,2,1,0:T(2,128)(2,1)} %param.14) | copy-start | bytes 12582916
  6.7 13.9 %copy-start.1 = (bf16[16,512,2,128]{3,2,1,0:T(2,128)(2,1)S(1)}, bf16[16,512,2,128]{3,2,1,0:T(2,128)(2,1)}, u32[]{:S(2)}) copy-start(bf16[16,512,2,128]{3,2,1,0:T(2,128)(2,1)} %param.15) | copy-start | bytes 12582916
  6.7 13.9 %copy-start.4 = (s32[64]{0:T(128)S(1)}, s32[64]{0:T(128)}, u32[]{:S(2)}) copy-start(s32[64]{0:T(128)} %slot_ref.1) | copy-start | bytes 772
  6.7 13.9 %copy-start.5 = (s32[64]{0:T(128)S(1)}, s32[64]{0:T(128)}, u32[]{:S(2)}) copy-start(s32[64]{0:T(128)} %len_ref.1) | copy-start | bytes 772
  10.8 2.2 %collective-permute-start.5 = (bf16[4,64,128]{2,1,0:T(8,128)(2,1)S(1)}, bf16[4,64,128]{2,1,0:T(8,128)(2,1)S(1)}, u32[]{:S(2)}, u32[]{:S(2)}) collective-permute-start(bf16[4,64,128]{2,1,0:T(8,128)(2,1)S(1)} %get-tuple-element.49.refs_1_.q_ref), channel_id=1, source_target_pairs={{0,4},{4,0},{8,12},{12,8},{1,5},{5,1},{9,13},{13,9},{2,6},{6,2},{1... | collective-permute-start | bytes 196616 | tf_op jit(solution)/shard_map/ppermute | solution.py:369
  10.9 4.0 %collective-permute-start.4 = (bf16[4,64,128]{2,1,0:T(8,128)(2,1)S(1)}, bf16[4,64,128]{2,1,0:T(8,128)(2,1)S(1)}, u32[]{:S(2)}, u32[]{:S(2)}) collective-permute-start(bf16[4,64,128]{2,1,0:T(8,128)(2,1)S(1)} %get-tuple-element.49.refs_1_.q_ref), channel_id=1, source_target_pairs={{0,12},{4,8},{8,4},{12,0},{1,13},{5,9},{9,5},{13,1},{2,14},{6,10},... | collective-permute-start | bytes 196616 | tf_op jit(solution)/shard_map/ppermute | solution.py:369
  12.5 4.6 %collective-permute-start.3 = (bf16[4,80,128]{2,1,0:T(8,128)(2,1)S(1)}, bf16[4,80,128]{2,1,0:T(8,128)(2,1)S(1)}, u32[]{:S(2)}, u32[]{:S(2)}) collective-permute-start(bf16[4,80,128]{2,1,0:T(8,128)(2,1)S(1)} %get-tuple-element.51), channel_id=1, source_target_pairs={{0,8},{4,12},{8,0},{12,4},{1,9},{5,13},{9,1},{13,5},{2,10},{6,14},... | collective-permute-start | bytes 245768 | tf_op jit(solution)/shard_map/ppermute | solution.py:369
  16.1 1.5 %collective-permute-start.6 = (bf16[272,128]{1,0:T(8,128)(2,1)S(1)}, bf16[272,128]{1,0:T(8,128)(2,1)S(1)}, u32[]{:S(2)}, u32[]{:S(2)}) collective-permute-start(bf16[272,128]{1,0:T(8,128)(2,1)S(1)} %prefix_far.2), channel_id=1, source_target_pairs={{0,4},{4,0},{8,12},{12,8},{1,5},{5,1},{9,13},{13,9},{2,6},{6,2},{1... | collective-permute-start | bytes 208904 | tf_op jit(solution)/shard_map/ppermute | solution.py:369
  16.7 6.3 %collective-permute-start.7 = (bf16[272,128]{1,0:T(8,128)(2,1)S(1)}, bf16[272,128]{1,0:T(8,128)(2,1)S(1)}, u32[]{:S(2)}, u32[]{:S(2)}) collective-permute-start(bf16[272,128]{1,0:T(8,128)(2,1)S(1)} %get-tuple-element.66), channel_id=1, source_target_pairs={{0,4},{4,0},{8,12},{12,8},{1,5},{5,1},{9,13},{13,9},{2,6},{6,2},{1... | collective-permute-start | bytes 208904 | tf_op jit(solution)/shard_map/ppermute | solution.py:369
  18.8 4.6 %collective-permute-start.8 = (bf16[272,128]{1,0:T(8,128)(2,1)S(1)}, bf16[272,128]{1,0:T(8,128)(2,1)S(1)}, u32[]{:S(2)}, u32[]{:S(2)}) collective-permute-start(bf16[272,128]{1,0:T(8,128)(2,1)S(1)} %prefix_far.3), channel_id=1, source_target_pairs={{0,8},{4,12},{8,0},{12,4},{1,9},{5,13},{9,1},{13,5},{2,10},{6,14},... | collective-permute-start | bytes 208904 | tf_op jit(solution)/shard_map/ppermute | solution.py:369
  23.5 5.7 %collective-permute-start.9 = (bf16[64,128]{1,0:T(8,128)(2,1)S(1)}, bf16[64,128]{1,0:T(8,128)(2,1)S(1)}, u32[]{:S(2)}, u32[]{:S(2)}) collective-permute-start(bf16[64,128]{1,0:T(8,128)(2,1)S(1)} %get-tuple-element.69), channel_id=1, source_target_pairs={{0,3},{1,2},{2,1},{3,0},{4,7},{5,6},{6,5},{7,4},{8,11},{9,10},{10,... | collective-permute-start | bytes 49160 | tf_op jit(solution)/shard_map/ppermute | solution.py:366
  25.1 4.7 %collective-permute-start.10 = (bf16[64,128]{1,0:T(8,128)(2,1)S(1)}, bf16[64,128]{1,0:T(8,128)(2,1)S(1)}, u32[]{:S(2)}, u32[]{:S(2)}) collective-permute-start(bf16[64,128]{1,0:T(8,128)(2,1)S(1)} %get-tuple-element.70), channel_id=1, source_target_pairs={{0,2},{1,3},{2,0},{3,1},{4,6},{5,7},{6,4},{7,5},{8,10},{9,11},{10,... | collective-permute-start | bytes 49160 | tf_op jit(solution)/shard_map/ppermute | solution.py:366
  25.7 4.2 %collective-permute-start.11 = (bf16[64,128]{1,0:T(8,128)(2,1)S(1)}, bf16[64,128]{1,0:T(8,128)(2,1)S(1)}, u32[]{:S(2)}, u32[]{:S(2)}) collective-permute-start(bf16[64,128]{1,0:T(8,128)(2,1)S(1)} %get-tuple-element.71), channel_id=1, source_target_pairs={{0,1},{1,0},{2,3},{3,2},{4,5},{5,4},{6,7},{7,6},{8,9},{9,8},{10,11... | collective-permute-start | bytes 49160 | tf_op jit(solution)/shard_map/ppermute | solution.py:366

commit v6 on v5

--- a/solution.py
+++ b/solution.py
@@ -10,8 +10,6 @@
 
 NEG = -1e30
 GAP = 1 << 36
-CHUNK = 256
-FOLD = 128
 LOG2E = 1.4426950408889634
 F32 = jnp.float32
 BF16 = jnp.bfloat16
@@ -19,7 +17,6 @@
 SM = pl.BlockSpec(memory_space=pltpu.SMEM)
 HBM = pl.BlockSpec(memory_space=pltpu.HBM)
 NT = (((1,), (1,)), ((), ()))
-NN = (((1,), (0,)), ((), ()))
 
 
 def ceil_to(value, unit):
@@ -115,10 +112,7 @@
             wide[...] = src[at * chunk : (at + 1) * chunk].astype(F32)
             for kl in range(local):
                 head = wide[pl.ds(kl, rows, stride=local)] if local > 1 else wide[...]
-                if dst is pvo:
-                    dst[kl, :, at * rows : (at + 1) * rows] = head.T.astype(BF16)
-                else:
-                    dst[kl, at * rows : (at + 1) * rows] = head.astype(BF16)
+                dst[kl, at * rows : (at + 1) * rows] = head.astype(BF16)
 
 
 def places(c, slots, nz, local, group, slot_ref, len_ref):
@@ -205,39 +199,7 @@
     return out, top + jnp.log(total)
 
 
-def keys_as_rows(qs, k_ref, v_ref, scale):
-    positions, width = k_ref.shape[1], qs[0].shape[0]
-    chunk = math.gcd(positions, CHUNK)
-    fold = math.gcd(chunk, FOLD)
-
-    def folded(x, reduce):
-        return reduce(x.reshape(chunk // fold, fold, width), axis=0)
-
-    pieces = [slice(at, at + chunk) for at in range(0, positions, chunk)]
-    scores, tops = [], []
-    for kl, q in enumerate(qs):
-        scores.append(
-            [lax.dot_general(k_ref[kl, p], q, NT, preferred_element_type=F32) for p in pieces]
-        )
-        top = folded(scores[kl][0], jnp.max)
-        for s in scores[kl][1:]:
-            top = jnp.maximum(top, folded(s, jnp.max))
-        tops.append(jnp.max(top, axis=0, keepdims=True))
-    heads = []
-    for kl in range(len(qs)):
-        total, out = 0.0, 0.0
-        for p, s in zip(pieces, scores[kl]):
-            weights = jnp.exp2((s - tops[kl]) * (scale * LOG2E))
-            total = total + folded(weights, jnp.sum)
-            out = out + lax.dot_general(
-                v_ref[kl, :, p], weights.astype(BF16), NN, preferred_element_type=F32
-            )
-        total = jnp.sum(total, axis=0, keepdims=True)
-        heads.append((out * (1.0 / total), tops[kl] * scale + jnp.log(total)))
-    return heads
-
-
-def queries_as_rows(qs, k_ref, v_ref, scale):
+def attend(qs, k_ref, v_ref, scale):
     scores = [
         lax.dot_general(q, k_ref[kl], NT, preferred_element_type=F32) for kl, q in enumerate(qs)
     ]
@@ -248,9 +210,9 @@
         parts.append((top, jnp.sum(weights, axis=1, keepdims=True), weights.astype(BF16)))
     heads = []
     for kl, (top, total, weights) in enumerate(parts):
-        out = lax.dot_general(weights, v_ref[kl], NT, preferred_element_type=F32) * (1.0 / total)
+        out = jnp.dot(weights, v_ref[kl], preferred_element_type=F32) * (1.0 / total)
         lse = jnp.broadcast_to(top * scale + jnp.log(total), out.shape)
-        heads.append((out.T, lse.T[:1]))
+        heads.append((out.T, lse.T))
     return heads
 
 
@@ -265,10 +227,10 @@
         )
         for kl in range(local)
     ]
-    heads = (keys_as_rows if count * columns > 128 else queries_as_rows)(qs, k_ref, v_ref, scale)
+    heads = attend(qs, k_ref, v_ref, scale)
     for i in range(count):
         at = slice(i * columns, (i + 1) * columns)
-        parts = [(o[:, at], lse[:, at]) for o, lse in heads]
+        parts = [(o[:, at], lse[:1, at]) for o, lse in heads]
         if merged:
             parts = [merge(pair) for pair in zip(parts, decode(others[i][...], local))]
         os, lses = zip(*parts)
@@ -357,8 +319,7 @@
     used = qrows + 2 * nb * local
     padded = ceil_to(used, 16)
     rows = nz * qrows
-    order_in = [*range(nz - 1, 0, -1), 0]
-    order_out = order_in
+    order = [*range(nz - 1, 0, -1), 0]
     nc = 2 if nblk % 2 == 0 else 1
     nx = nblk // nc
 
@@ -407,11 +368,7 @@
     keys, values, token = call(
         functools.partial(split_kernel, local),
         "split",
-        [
-            pltpu.VMEM((local, positions, head_dim), BF16),
-            pltpu.VMEM((local, head_dim, positions), BF16),
-            pltpu.VMEM((8, head_dim), F32),
-        ],
+        [pltpu.VMEM((local, positions, head_dim), BF16)] * 2 + [pltpu.VMEM((8, head_dim), F32)],
         (prefix_keys.reshape(flat), prefix_values.reshape(flat)),
         [VM] * 2,
         scratch=[pltpu.VMEM((chunk, head_dim), F32)],
@@ -419,14 +376,14 @@
         moved=prefix_keys.size * 8,
     )
     joined, fresh, wide = call(
-        functools.partial(join_kernel, order_in, qrows),
+        functools.partial(join_kernel, order, qrows),
         "join",
         [
             jax.ShapeDtypeStruct((nz, qrows, head_dim), BF16),
             jax.ShapeDtypeStruct((nz, padded - qrows, head_dim), BF16),
             jax.ShapeDtypeStruct((nz, padded, head_dim), BF16),
         ],
-        (*[arrived[step] for step in order_in], gap, token),
+        (*[arrived[step] for step in order], gap, token),
         [VM] * (nz + 2),
         moved=nz * padded * head_dim * 4,
     )
@@ -507,10 +464,10 @@
         shift(pieces[step], "branch", back(step, nz), nz) for step in range(nz - 1, 0, -1)
     ][::-1]
     out = call(
-        functools.partial(unpack_kernel, order_out, local, group),
+        functools.partial(unpack_kernel, order, local, group),
         "unpack",
         jax.ShapeDtypeStruct((nb, nz, heads // nz, head_dim), BF16),
-        [landed[step] for step in order_out],
+        [landed[step] for step in order],
         [VM] * nz,
         moved=queries.size * 4,
     )

time: 30.7 us -> 30.4 us (level)
  Pallas kernels: 9.36 us -> 8.76 us
  waiting for transfers between devices: 6.03 us -> 6.4 us
    pallas_call x11, Pallas kernels: 9.36 us -> 8.76 us  [call(): pl.pallas_call(kernel, name=name, out_shape=out_shape, in_specs=in_specs,...]
  transfers between devices with their start and end apart: 12 -> 12, of which waited for: 7 -> 8; matrix products, arithmetic and copies ran while one was open for 0% -> 0% of each run, Pallas kernels for 25% -> 23%
where the time goes in v6:
time: 30.4 us; the launch traced here: 30.3 us
  starting transfers between devices  14.9 us (49%)
  Pallas kernels  8.76 us (29%)
  waiting for transfers between devices  6.4 us (21%)
    ppermute x6, starting transfers between devices, shift(): lax.ppermute(x, axis, [(i, partner(i, step, count)) for i in range(count)])  10.2 us
    pallas_call x11, Pallas kernels, call(): pl.pallas_call(kernel, name=name, out_shape=out_shape, in_specs=in_specs,...  8.76 us
    ppermute x6, waiting for transfers between devices, shift(): lax.ppermute(x, axis, [(i, partner(i, step, count)) for i in range(count)])  5.38 us
    ppermute x6, starting transfers between devices, along_blk(): lax.ppermute(x, 'blk', [(i, partner(i // nc, step_x, nx) * nc + partner(i...  4.72 us
    ppermute x6, waiting for transfers between devices, along_blk(): lax.ppermute(x, 'blk', [(i, partner(i // nc, step_x, nx) * nc + partner(i...  1.01 us
  transfers between devices with their start and end apart: 12, of which 8 were waited for; matrix products, arithmetic and copies ran while one was open for 0% of the time, Pallas kernels for 23%

profile of v6, /device:TPU:0, one launch (start us, length us, event | category | flops | bytes accessed | tf_op | source)
XLA Modules:
  0.0 30.3 jit_solution(11525975876410342400)
XLA Ops:
  0.0 0.9 %pack.1 = (bf16[80,128]{1,0:T(8,128)(2,1)S(1)}, bf16[80,128]{1,0:T(8,128)(2,1)S(1)}, bf16[80,128]{1,0:T(8,128)(2,1)S(1)}, bf16[80,128]{1,0:T(8,128)(2,1)S(1)}) custom-call(bf16[4,4,16,128]{3,2,1,0:T(8,128)(2,1)} %bitcast.10, bf16[4,8,128]{2,1,0:T(8,128)(2,1)} %k_hbm.1, bf16[4,8,128]{2,1,0:T(8,128)(2,1)} %v_hbm.1), custom_call_target="tpu_custom_call" | custom-call | bytes 131072 | tf_op jit(solution)/shard_map/pack/pallas_call | solution.py:48
  0.9 0.0 copy-start.2
  0.9 0.0 copy-start.3
  1.0 5.1 %collective-permute-start = (bf16[80,128]{1,0:T(8,128)(2,1)S(1)}, bf16[80,128]{1,0:T(8,128)(2,1)S(1)}, u32[]{:S(2)}, u32[]{:S(2)}) collective-permute-start(bf16[80,128]{1,0:T(8,128)(2,1)S(1)} %get-tuple-element.43), channel_id=1, source_target_pairs={{0,3},{1,2},{2,1},{3,0},{4,7},{5,6},{6,5},{7,4},{8,11},{9,10},{10,... | collective-permute-start | bytes 61448 | tf_op jit(solution)/shard_map/ppermute | solution.py:327
  6.1 0.0 collective-permute-start.1
  6.1 0.6 %collective-permute-start.2 = (bf16[80,128]{1,0:T(8,128)(2,1)S(1)}, bf16[80,128]{1,0:T(8,128)(2,1)S(1)}, u32[]{:S(2)}, u32[]{:S(2)}) collective-permute-start(bf16[80,128]{1,0:T(8,128)(2,1)S(1)} %get-tuple-element.45), channel_id=1, source_target_pairs={{0,1},{1,0},{2,3},{3,2},{4,5},{5,4},{6,7},{7,6},{8,9},{9,8},{10,11... | collective-permute-start | bytes 61448 | tf_op jit(solution)/shard_map/ppermute | solution.py:327
  6.7 0.0 copy-done.2
  6.7 0.0 copy-done.3
  6.7 0.0 copy-start
  6.7 0.0 copy-start.1
  6.7 0.0 copy-start.4
  6.7 0.0 copy-start.5
  6.8 0.5 %split.1 = (bf16[2,2048,128]{2,1,0:T(8,128)(2,1)S(1)}, bf16[2,2048,128]{2,1,0:T(8,128)(2,1)S(1)}, f32[8,128]{1,0:T(8,128)S(1)}) custom-call(bf16[4096,128]{1,0:T(8,128)(2,1)S(1)} %bitcast.8, bf16[4096,128]{1,0:T(8,128)(2,1)S(1)} %bitcast.9), custom_call_target="tpu_custom_call" | custom-call | bytes 4194304 | tf_op jit(solution)/shard_map/split/pallas_call | solution.py:48
  7.3 0.6 %collective-permute-done.refs_0_ = bf16[80,128]{1,0:T(8,128)(2,1)S(1)} collective-permute-done((bf16[80,128]{1,0:T(8,128)(2,1)S(1)}, bf16[80,128]{1,0:T(8,128)(2,1)S(1)}, u32[]{:S(2)}, u32[]{:S(2)}) %collective-permute-start) | collective-permute-done | bytes 20512 | tf_op jit(solution)/shard_map/ppermute | solution.py:327
  7.8 2.9 %collective-permute-done.1.refs_1_ = bf16[80,128]{1,0:T(8,128)(2,1)S(1)} collective-permute-done((bf16[80,128]{1,0:T(8,128)(2,1)S(1)}, bf16[80,128]{1,0:T(8,128)(2,1)S(1)}, u32[]{:S(2)}, u32[]{:S(2)}) %collective-permute-start.1) | collective-permute-done | bytes 20512 | tf_op jit(solution)/shard_map/ppermute | solution.py:327
  10.8 0.0 collective-permute-done.2.refs_2_
  10.8 0.1 collective-permute-start.5
  10.9 1.6 %collective-permute-start.4 = (bf16[4,64,128]{2,1,0:T(8,128)(2,1)S(1)}, bf16[4,64,128]{2,1,0:T(8,128)(2,1)S(1)}, u32[]{:S(2)}, u32[]{:S(2)}) collective-permute-start(bf16[4,64,128]{2,1,0:T(8,128)(2,1)S(1)} %get-tuple-element.49.refs_1_.q_ref), channel_id=1, source_target_pairs={{0,12},{4,8},{8,4},{12,0},{1,13},{5,9},{9,5},{13,1},{2,14},{6,10},... | collective-permute-start | bytes 196616 | tf_op jit(solution)/shard_map/ppermute | solution.py:330
  12.5 0.5 %collective-permute-start.3 = (bf16[4,80,128]{2,1,0:T(8,128)(2,1)S(1)}, bf16[4,80,128]{2,1,0:T(8,128)(2,1)S(1)}, u32[]{:S(2)}, u32[]{:S(2)}) collective-permute-start(bf16[4,80,128]{2,1,0:T(8,128)(2,1)S(1)} %get-tuple-element.51), channel_id=1, source_target_pairs={{0,8},{4,12},{8,0},{12,4},{1,9},{5,13},{9,1},{13,5},{2,10},{6,14},... | collective-permute-start | bytes 245768 | tf_op jit(solution)/shard_map/ppermute | solution.py:330
  13.0 0.0 collective-permute-done.5.refs_0_
  13.0 1.7 %prefix_near.1 = (bf16[272,128]{1,0:T(8,128)(2,1)S(1)}, f32[256,128]{1,0:T(8,128)S(1)}, f32[8,128]{1,0:T(8,128)S(1)}) custom-call(bf16[4,64,128]{2,1,0:T(8,128)(2,1)S(1)} %collective-permute-done.5.refs_0_, bf16[4,64,128]{2,1,0:T(8,128)(2,1)S(1)} %get-tuple-element.49.refs_1_.q_ref, bf16[2,2048,128]{2,1,0:T(8,128)(2,1)S(1)} %get-tuple-element.52.refs_2_.refs_1_, ...), custom_call_target="tpu_custom_call" | custom-call | flops 536870912 | bytes 2097152 | tf_op jit(solution)/shard_map/prefix_near/pallas_call | solution.py:48
  14.7 0.2 collective-permute-done.4.refs_0_
  14.9 1.1 %prefix_far.2 = bf16[272,128]{1,0:T(8,128)(2,1)S(1)} custom-call(bf16[4,64,128]{2,1,0:T(8,128)(2,1)S(1)} %collective-permute-done.4.refs_0_, bf16[2,2048,128]{2,1,0:T(8,128)(2,1)S(1)} %get-tuple-element.52.refs_2_.refs_1_, bf16[2,2048,128]{2,1,0:T(8,128)(2,1)S(1)} %get-tuple-element.53.refs_3_.refs_2_), custom_call_target="tpu_custom_call" | custom-call | tf_op jit(solution)/shard_map/prefix_far/pallas_call | solution.py:48
  16.0 0.6 %collective-permute-start.6 = (bf16[272,128]{1,0:T(8,128)(2,1)S(1)}, bf16[272,128]{1,0:T(8,128)(2,1)S(1)}, u32[]{:S(2)}, u32[]{:S(2)}) collective-permute-start(bf16[272,128]{1,0:T(8,128)(2,1)S(1)} %prefix_far.2), channel_id=1, source_target_pairs={{0,4},{4,0},{8,12},{12,8},{1,5},{5,1},{9,13},{13,9},{2,6},{6,2},{1... | collective-permute-start | bytes 208904 | tf_op jit(solution)/shard_map/ppermute | solution.py:330
  16.5 0.1 collective-permute-start.7
  16.6 0.5 %collective-permute-done.3.refs_0_ = bf16[4,80,128]{2,1,0:T(8,128)(2,1)S(1)} collective-permute-done((bf16[4,80,128]{2,1,0:T(8,128)(2,1)S(1)}, bf16[4,80,128]{2,1,0:T(8,128)(2,1)S(1)}, u32[]{:S(2)}, u32[]{:S(2)}) %collective-permute-start.3) | collective-permute-done | bytes 81952 | tf_op jit(solution)/shard_map/ppermute | solution.py:330
  17.1 0.4 %collective-permute-done.6.refs_3_ = bf16[272,128]{1,0:T(8,128)(2,1)S(1)} collective-permute-done((bf16[272,128]{1,0:T(8,128)(2,1)S(1)}, bf16[272,128]{1,0:T(8,128)(2,1)S(1)}, u32[]{:S(2)}, u32[]{:S(2)}) %collective-permute-start.6) | collective-permute-done | bytes 69664 | tf_op jit(solution)/shard_map/ppermute | solution.py:330
  17.4 1.1 %prefix_far.3 = bf16[272,128]{1,0:T(8,128)(2,1)S(1)} custom-call(bf16[4,80,128]{2,1,0:T(8,128)(2,1)S(1)} %collective-permute-done.3.refs_0_, bf16[2,2048,128]{2,1,0:T(8,128)(2,1)S(1)} %get-tuple-element.52.refs_2_.refs_1_, bf16[2,2048,128]{2,1,0:T(8,128)(2,1)S(1)} %get-tuple-element.53.refs_3_.refs_2_, bf16[272,128]{1,0:T(8,128)(2,1)S(1)} %collective-permute-done.6.refs_3_), custom_call_target="tpu_custom_call" | custom-call | tf_op jit(solution)/shard_map/prefix_far/pallas_call | solution.py:48
  18.5 1.9 %collective-permute-start.8 = (bf16[272,128]{1,0:T(8,128)(2,1)S(1)}, bf16[272,128]{1,0:T(8,128)(2,1)S(1)}, u32[]{:S(2)}, u32[]{:S(2)}) collective-permute-start(bf16[272,128]{1,0:T(8,128)(2,1)S(1)} %prefix_far.3), channel_id=1, source_target_pairs={{0,8},{4,12},{8,0},{12,4},{1,9},{5,13},{9,1},{13,5},{2,10},{6,14},... | collective-permute-start | bytes 208904 | tf_op jit(solution)/shard_map/ppermute | solution.py:330
  20.4 0.0 copy-done
  20.4 0.0 copy-done.1
  20.4 0.0 copy-done.4
  20.4 0.0 copy-done.5
  20.4 2.3 %suffix.1 = (f32[256,128]{1,0:T(8,128)S(1)}, f32[256,128]{1,0:T(8,128)S(1)}) custom-call(bf16[4,64,128]{2,1,0:T(8,128)(2,1)S(1)} %get-tuple-element.49.refs_1_.q_ref, s32[64]{0:T(128)S(1)} %copy-done.4, s32[64]{0:T(128)S(1)} %copy-done.5, bf16[16,1024,128]{2,1,0:T(8,128)(2,1)S(1)} %bitcast.6, bf16[16,1024,128]{2,1,0:T(8,128)(2,1)S(1)} %bitcast.7), custom_call_target="tpu_custom_call" | custom-call | tf_op jit(solution)/shard_map/suffix/pallas_call | solution.py:48
  22.7 0.0 collective-permute-done.7.refs_0_
  22.7 0.4 %near.1 = (f32[256,128]{1,0:T(8,128)S(1)}, f32[8,128]{1,0:T(8,128)S(1)}) custom-call(bf16[4,64,128]{2,1,0:T(8,128)(2,1)S(1)} %get-tuple-element.49.refs_1_.q_ref, bf16[4,16,128]{2,1,0:T(8,128)(2,1)S(1)} %get-tuple-element.50.fresh_ref, f32[256,128]{1,0:T(8,128)S(1)} %get-tuple-element.62.so_ref, f32[256,128]{1,0:T(8,128)S(1)} %get-tuple-element.63.sl_ref, ...), custom_call_target="tpu_custom_call" | custom-call | bytes 655360 | tf_op jit(solution)/shard_map/near/pallas_call | solution.py:48
  23.1 0.0 collective-permute-done.8.refs_0_
  23.1 0.1 final.1
  23.3 1.5 %collective-permute-start.9 = (bf16[64,128]{1,0:T(8,128)(2,1)S(1)}, bf16[64,128]{1,0:T(8,128)(2,1)S(1)}, u32[]{:S(2)}, u32[]{:S(2)}) collective-permute-start(bf16[64,128]{1,0:T(8,128)(2,1)S(1)} %get-tuple-element.69), channel_id=1, source_target_pairs={{0,3},{1,2},{2,1},{3,0},{4,7},{5,6},{6,5},{7,4},{8,11},{9,10},{10,... | collective-permute-start | bytes 49160 | tf_op jit(solution)/shard_map/ppermute | solution.py:327
  24.8 0.6 %collective-permute-start.10 = (bf16[64,128]{1,0:T(8,128)(2,1)S(1)}, bf16[64,128]{1,0:T(8,128)(2,1)S(1)}, u32[]{:S(2)}, u32[]{:S(2)}) collective-permute-start(bf16[64,128]{1,0:T(8,128)(2,1)S(1)} %get-tuple-element.70), channel_id=1, source_target_pairs={{0,2},{1,3},{2,0},{3,1},{4,6},{5,7},{6,4},{7,5},{8,10},{9,11},{10,... | collective-permute-start | bytes 49160 | tf_op jit(solution)/shard_map/ppermute | solution.py:327
  25.4 2.3 %collective-permute-start.11 = (bf16[64,128]{1,0:T(8,128)(2,1)S(1)}, bf16[64,128]{1,0:T(8,128)(2,1)S(1)}, u32[]{:S(2)}, u32[]{:S(2)}) collective-permute-start(bf16[64,128]{1,0:T(8,128)(2,1)S(1)} %get-tuple-element.71), channel_id=1, source_target_pairs={{0,1},{1,0},{2,3},{3,2},{4,5},{5,4},{6,7},{7,6},{8,9},{9,8},{10,11... | collective-permute-start | bytes 49160 | tf_op jit(solution)/shard_map/ppermute | solution.py:327
  27.7 1.3 %collective-permute-done.9.refs_0_ = bf16[64,128]{1,0:T(8,128)(2,1)S(1)} collective-permute-done((bf16[64,128]{1,0:T(8,128)(2,1)S(1)}, bf16[64,128]{1,0:T(8,128)(2,1)S(1)}, u32[]{:S(2)}, u32[]{:S(2)}) %collective-permute-start.9) | collective-permute-done | bytes 16416 | tf_op jit(solution)/shard_map/ppermute | solution.py:327
  29.0 0.5 %collective-permute-done.10.refs_1_ = bf16[64,128]{1,0:T(8,128)(2,1)S(1)} collective-permute-done((bf16[64,128]{1,0:T(8,128)(2,1)S(1)}, bf16[64,128]{1,0:T(8,128)(2,1)S(1)}, u32[]{:S(2)}, u32[]{:S(2)}) %collective-permute-start.10) | collective-permute-done | bytes 16416 | tf_op jit(solution)/shard_map/ppermute | solution.py:327
  29.5 0.2 collective-permute-done.11.refs_2_
  29.6 0.6 %unpack.1 = bf16[4,4,16,128]{3,2,1,0:T(8,128)(2,1)} custom-call(bf16[64,128]{1,0:T(8,128)(2,1)S(1)} %collective-permute-done.9.refs_0_, bf16[64,128]{1,0:T(8,128)(2,1)S(1)} %collective-permute-done.10.refs_1_, bf16[64,128]{1,0:T(8,128)(2,1)S(1)} %collective-permute-done.11.refs_2_, bf16[64,128]{1,0:T(8,128)(2,1)S(1)} %get-tuple-element.72.refs_3_), custom_call_target="tpu_custom_call" | custom-call | bytes 131072 | tf_op jit(solution)/shard_map/unpack/pallas_call | solution.py:48
  (2 shorter events, 0.0 us)
Async XLA Ops:
  0.9 5.8 %copy-start.2 = (bf16[2048,2,128]{2,1,0:T(2,128)(2,1)S(1)}, bf16[2048,2,128]{2,1,0:T(2,128)(2,1)}, u32[]{:S(2)}) copy-start(bf16[2048,2,128]{2,1,0:T(2,128)(2,1)} %param.12) | copy-start | bytes 3145732
  0.9 5.8 %copy-start.3 = (bf16[2048,2,128]{2,1,0:T(2,128)(2,1)S(1)}, bf16[2048,2,128]{2,1,0:T(2,128)(2,1)}, u32[]{:S(2)}) copy-start(bf16[2048,2,128]{2,1,0:T(2,128)(2,1)} %param.13) | copy-start | bytes 3145732
  1.0 6.9 %collective-permute-start = (bf16[80,128]{1,0:T(8,128)(2,1)S(1)}, bf16[80,128]{1,0:T(8,128)(2,1)S(1)}, u32[]{:S(2)}, u32[]{:S(2)}) collective-permute-start(bf16[80,128]{1,0:T(8,128)(2,1)S(1)} %get-tuple-element.43), channel_id=1, source_target_pairs={{0,3},{1,2},{2,1},{3,0},{4,7},{5,6},{6,5},{7,4},{8,11},{9,10},{10,... | collective-permute-start | bytes 61448 | tf_op jit(solution)/shard_map/ppermute | solution.py:327
  6.1 4.7 %collective-permute-start.1 = (bf16[80,128]{1,0:T(8,128)(2,1)S(1)}, bf16[80,128]{1,0:T(8,128)(2,1)S(1)}, u32[]{:S(2)}, u32[]{:S(2)}) collective-permute-start(bf16[80,128]{1,0:T(8,128)(2,1)S(1)} %get-tuple-element.44), channel_id=1, source_target_pairs={{0,2},{1,3},{2,0},{3,1},{4,6},{5,7},{6,4},{7,5},{8,10},{9,11},{10,... | collective-permute-start | bytes 61448 | tf_op jit(solution)/shard_map/ppermute | solution.py:327
  6.1 4.7 %collective-permute-start.2 = (bf16[80,128]{1,0:T(8,128)(2,1)S(1)}, bf16[80,128]{1,0:T(8,128)(2,1)S(1)}, u32[]{:S(2)}, u32[]{:S(2)}) collective-permute-start(bf16[80,128]{1,0:T(8,128)(2,1)S(1)} %get-tuple-element.45), channel_id=1, source_target_pairs={{0,1},{1,0},{2,3},{3,2},{4,5},{5,4},{6,7},{7,6},{8,9},{9,8},{10,11... | collective-permute-start | bytes 61448 | tf_op jit(solution)/shard_map/ppermute | solution.py:327
  6.7 13.7 %copy-start = (bf16[16,512,2,128]{3,2,1,0:T(2,128)(2,1)S(1)}, bf16[16,512,2,128]{3,2,1,0:T(2,128)(2,1)}, u32[]{:S(2)}) copy-start(bf16[16,512,2,128]{3,2,1,0:T(2,128)(2,1)} %param.14) | copy-start | bytes 12582916
  6.7 13.7 %copy-start.1 = (bf16[16,512,2,128]{3,2,1,0:T(2,128)(2,1)S(1)}, bf16[16,512,2,128]{3,2,1,0:T(2,128)(2,1)}, u32[]{:S(2)}) copy-start(bf16[16,512,2,128]{3,2,1,0:T(2,128)(2,1)} %param.15) | copy-start | bytes 12582916
  6.7 13.6 %copy-start.4 = (s32[64]{0:T(128)S(1)}, s32[64]{0:T(128)}, u32[]{:S(2)}) copy-start(s32[64]{0:T(128)} %slot_ref.1) | copy-start | bytes 772
  6.7 13.6 %copy-start.5 = (s32[64]{0:T(128)S(1)}, s32[64]{0:T(128)}, u32[]{:S(2)}) copy-start(s32[64]{0:T(128)} %len_ref.1) | copy-start | bytes 772
  10.8 2.2 %collective-permute-start.5 = (bf16[4,64,128]{2,1,0:T(8,128)(2,1)S(1)}, bf16[4,64,128]{2,1,0:T(8,128)(2,1)S(1)}, u32[]{:S(2)}, u32[]{:S(2)}) collective-permute-start(bf16[4,64,128]{2,1,0:T(8,128)(2,1)S(1)} %get-tuple-element.49.refs_1_.q_ref), channel_id=1, source_target_pairs={{0,4},{4,0},{8,12},{12,8},{1,5},{5,1},{9,13},{13,9},{2,6},{6,2},{1... | collective-permute-start | bytes 196616 | tf_op jit(solution)/shard_map/ppermute | solution.py:330
  10.9 4.0 %collective-permute-start.4 = (bf16[4,64,128]{2,1,0:T(8,128)(2,1)S(1)}, bf16[4,64,128]{2,1,0:T(8,128)(2,1)S(1)}, u32[]{:S(2)}, u32[]{:S(2)}) collective-permute-start(bf16[4,64,128]{2,1,0:T(8,128)(2,1)S(1)} %get-tuple-element.49.refs_1_.q_ref), channel_id=1, source_target_pairs={{0,12},{4,8},{8,4},{12,0},{1,13},{5,9},{9,5},{13,1},{2,14},{6,10},... | collective-permute-start | bytes 196616 | tf_op jit(solution)/shard_map/ppermute | solution.py:330
  12.5 4.6 %collective-permute-start.3 = (bf16[4,80,128]{2,1,0:T(8,128)(2,1)S(1)}, bf16[4,80,128]{2,1,0:T(8,128)(2,1)S(1)}, u32[]{:S(2)}, u32[]{:S(2)}) collective-permute-start(bf16[4,80,128]{2,1,0:T(8,128)(2,1)S(1)} %get-tuple-element.51), channel_id=1, source_target_pairs={{0,8},{4,12},{8,0},{12,4},{1,9},{5,13},{9,1},{13,5},{2,10},{6,14},... | collective-permute-start | bytes 245768 | tf_op jit(solution)/shard_map/ppermute | solution.py:330
  16.0 1.5 %collective-permute-start.6 = (bf16[272,128]{1,0:T(8,128)(2,1)S(1)}, bf16[272,128]{1,0:T(8,128)(2,1)S(1)}, u32[]{:S(2)}, u32[]{:S(2)}) collective-permute-start(bf16[272,128]{1,0:T(8,128)(2,1)S(1)} %prefix_far.2), channel_id=1, source_target_pairs={{0,4},{4,0},{8,12},{12,8},{1,5},{5,1},{9,13},{13,9},{2,6},{6,2},{1... | collective-permute-start | bytes 208904 | tf_op jit(solution)/shard_map/ppermute | solution.py:330
  16.5 6.2 %collective-permute-start.7 = (bf16[272,128]{1,0:T(8,128)(2,1)S(1)}, bf16[272,128]{1,0:T(8,128)(2,1)S(1)}, u32[]{:S(2)}, u32[]{:S(2)}) collective-permute-start(bf16[272,128]{1,0:T(8,128)(2,1)S(1)} %get-tuple-element.66), channel_id=1, source_target_pairs={{0,4},{4,0},{8,12},{12,8},{1,5},{5,1},{9,13},{13,9},{2,6},{6,2},{1... | collective-permute-start | bytes 208904 | tf_op jit(solution)/shard_map/ppermute | solution.py:330
  18.5 4.6 %collective-permute-start.8 = (bf16[272,128]{1,0:T(8,128)(2,1)S(1)}, bf16[272,128]{1,0:T(8,128)(2,1)S(1)}, u32[]{:S(2)}, u32[]{:S(2)}) collective-permute-start(bf16[272,128]{1,0:T(8,128)(2,1)S(1)} %prefix_far.3), channel_id=1, source_target_pairs={{0,8},{4,12},{8,0},{12,4},{1,9},{5,13},{9,1},{13,5},{2,10},{6,14},... | collective-permute-start | bytes 208904 | tf_op jit(solution)/shard_map/ppermute | solution.py:330
  23.3 5.7 %collective-permute-start.9 = (bf16[64,128]{1,0:T(8,128)(2,1)S(1)}, bf16[64,128]{1,0:T(8,128)(2,1)S(1)}, u32[]{:S(2)}, u32[]{:S(2)}) collective-permute-start(bf16[64,128]{1,0:T(8,128)(2,1)S(1)} %get-tuple-element.69), channel_id=1, source_target_pairs={{0,3},{1,2},{2,1},{3,0},{4,7},{5,6},{6,5},{7,4},{8,11},{9,10},{10,... | collective-permute-start | bytes 49160 | tf_op jit(solution)/shard_map/ppermute | solution.py:327
  24.8 4.7 %collective-permute-start.10 = (bf16[64,128]{1,0:T(8,128)(2,1)S(1)}, bf16[64,128]{1,0:T(8,128)(2,1)S(1)}, u32[]{:S(2)}, u32[]{:S(2)}) collective-permute-start(bf16[64,128]{1,0:T(8,128)(2,1)S(1)} %get-tuple-element.70), channel_id=1, source_target_pairs={{0,2},{1,3},{2,0},{3,1},{4,6},{5,7},{6,4},{7,5},{8,10},{9,11},{10,... | collective-permute-start | bytes 49160 | tf_op jit(solution)/shard_map/ppermute | solution.py:327
  25.4 4.2 %collective-permute-start.11 = (bf16[64,128]{1,0:T(8,128)(2,1)S(1)}, bf16[64,128]{1,0:T(8,128)(2,1)S(1)}, u32[]{:S(2)}, u32[]{:S(2)}) collective-permute-start(bf16[64,128]{1,0:T(8,128)(2,1)S(1)} %get-tuple-element.71), channel_id=1, source_target_pairs={{0,1},{1,0},{2,3},{3,2},{4,5},{5,4},{6,7},{7,6},{8,9},{9,8},{10,11... | collective-permute-start | bytes 49160 | tf_op jit(solution)/shard_map/ppermute | solution.py:327

commit v7 on v6

--- a/solution.py
+++ b/solution.py
@@ -92,11 +92,10 @@
 
 
 def join_kernel(order, qrows, *refs):
-    q_ref, tail_ref, all_ref = refs[-3:]
+    q_ref, tail_ref = refs[-2:]
     for at, step in enumerate(order):
         q_ref[step] = refs[at][:qrows]
         tail_ref[step] = refs[at][qrows:]
-        all_ref[step] = refs[at][...]
 
 
 def gap_kernel(after, token):
@@ -216,9 +215,8 @@
     return heads
 
 
-def prefix_kernel(count, own, merged, local, part, scale, *refs):
-    q_refs, (k_ref, v_ref), refs = refs[:count], refs[count : count + 2], refs[count + 2 :]
-    others, outs = (refs[:count], refs[count:]) if merged else ((), refs)
+def prefix_kernel(count, own, local, part, scale, *refs):
+    q_refs, (k_ref, v_ref), outs = refs[:count], refs[count : count + 2], refs[count + 2 :]
     steps, part = q_refs[0].shape[0], part // local
     columns = steps * part
     qs = [
@@ -230,15 +228,21 @@
     heads = attend(qs, k_ref, v_ref, scale)
     for i in range(count):
         at = slice(i * columns, (i + 1) * columns)
-        parts = [(o[:, at], lse[:1, at]) for o, lse in heads]
-        if merged:
-            parts = [merge(pair) for pair in zip(parts, decode(others[i][...], local))]
-        os, lses = zip(*parts)
+        os, lses = zip(*((o[:, at], lse[:1, at]) for o, lse in heads))
         if own and i == count - 1:
             outs[i][...] = jnp.concatenate(os, axis=0)
             outs[i + 1][:local] = jnp.concatenate(lses, axis=0)
         else:
             outs[i][...] = encode(os, lses)
+
+
+def join_partials_kernel(local, o_ref, lse_ref, other_ref, out_ref):
+    size = o_ref.shape[0] // local
+    parts = [
+        merge([(o_ref[kl * size : (kl + 1) * size], lse_ref[kl : kl + 1]), other])
+        for kl, other in enumerate(decode(other_ref[...], local))
+    ]
+    out_ref[...] = encode(*zip(*parts))
 
 
 def near_kernel(count, local, group, scale, q_ref, fresh_ref, so_ref, sl_ref, po_ref, pl_ref, *refs):
@@ -375,13 +379,12 @@
         vmem=8 << 20,
         moved=prefix_keys.size * 8,
     )
-    joined, fresh, wide = call(
+    joined, fresh = call(
         functools.partial(join_kernel, order, qrows),
         "join",
         [
             jax.ShapeDtypeStruct((nz, qrows, head_dim), BF16),
             jax.ShapeDtypeStruct((nz, padded - qrows, head_dim), BF16),
-            jax.ShapeDtypeStruct((nz, padded, head_dim), BF16),
         ],
         (*[arrived[step] for step in order], gap, token),
         [VM] * (nz + 2),
@@ -395,22 +398,23 @@
     ]
     payload = jax.ShapeDtypeStruct((local * head_dim + ceil_to(3 * local, 16), columns), BF16)
 
-    def prefix(name, arrays, own=False, others=()):
+    def prefix(name, arrays, own=False):
         count = len(arrays)
         return call(
-            functools.partial(prefix_kernel, count, own, bool(others), local, qrows, scale),
+            functools.partial(prefix_kernel, count, own, local, qrows, scale),
             name,
             [payload] * (count - own) + (state if own else []),
-            (*arrays, keys, values, *others),
-            [VM] * (count + 2 + len(others)),
+            (*arrays, keys, values),
+            [VM] * (count + 2),
             vmem=16 << 20,
-            flops=4 * count * rows * positions * head_dim if own else 0,
-            moved=keys.size * 4 if own else 0,
+            flops=4 * count * rows * positions * head_dim,
+            moved=keys.size * 4,
         )
 
-    far_steps = [(x, c) for x in range(1, nx) for c in range(nc)]
     near_steps = [(0, c) for c in range(1, nc)]
-    arriving = {step: along_blk(joined if step[1] else wide, *step) for step in far_steps + near_steps}
+    arriving = {
+        step: along_blk(joined, *step) for step in [(x, nc - 1) for x in range(1, nx)] + near_steps
+    }
 
     def give_back(x, step):
         return along_blk(x, back(step[0], nx), back(step[1], nc))
@@ -421,15 +425,24 @@
     sibling = list(received.values())
     distant = []
     for far in range(1, nx):
-        hopped = []
-        for core in range(nc - 1, -1, -1):
-            rows_of, own_lse = lax.optimization_barrier((arriving[far, core], own_lse))
-            (sent,) = prefix("prefix_far", [rows_of], others=() if core else hopped)
-            if core:
-                hopped.append(give_back(sent, (0, core)))
-            else:
-                distant.append(give_back(sent, (far, 0)))
-            sent, own_lse = lax.optimization_barrier((sent, own_lse))
+        rows_of, own_lse = lax.optimization_barrier((arriving[far, nc - 1], own_lse))
+        (sent,) = prefix("prefix_far", [rows_of])
+        if nc > 1:
+            hopped = give_back(sent, (0, 1))
+            rows_of, own_lse = lax.optimization_barrier(
+                (along_blk(arriving[far, nc - 1], 0, 1), own_lse)
+            )
+            rows_of, sent = lax.optimization_barrier((rows_of, sent))
+            partial = prefix("prefix_x", [rows_of], own=True)
+            sent = call(
+                functools.partial(join_partials_kernel, local),
+                "join_partials",
+                payload,
+                (*partial, hopped),
+                [VM] * 3,
+            )
+        distant.append(give_back(sent, (far, 0)))
+        sent, own_lse = lax.optimization_barrier((sent, own_lse))
     own_lse, slot_keys = lax.optimization_barrier((own_lse, slot_keys))
     suffix_state = call(
         functools.partial(suffix_kernel, nz, local, group, scale),

time: 30.4 us -> 29.5 us (0.970)
  starting transfers between devices: 14.9 us -> 14.4 us
  waiting for transfers between devices: 6.4 us -> 5.96 us
    ppermute x6, starting transfers between devices: 4.72 us -> 4.2 us  [along_blk(): lax.ppermute(x, 'blk', [(i, partner(i // nc, step_x, nx) * nc + partner(i...]
    ppermute x6, waiting for transfers between devices: 1.01 us -> 0.64 us  [along_blk(): lax.ppermute(x, 'blk', [(i, partner(i // nc, step_x, nx) * nc + partner(i...]
    pallas_call x11 -> x12, Pallas kernels: 8.76 us -> 8.79 us  [call(): pl.pallas_call(kernel, name=name, out_shape=out_shape, in_specs=in_specs,...]
  transfers between devices with their start and end apart: 12 -> 12, of which waited for: 8 -> 7; matrix products, arithmetic and copies ran while one was open for 0% -> 0% of each run, Pallas kernels for 23% -> 24%
where the time goes in v7:
time: 29.5 us; the launch traced here: 29.3 us
  starting transfers between devices  14.4 us (49%)
  Pallas kernels  8.79 us (30%)
  waiting for transfers between devices  5.96 us (20%)
    ppermute x6, starting transfers between devices, shift(): lax.ppermute(x, axis, [(i, partner(i, step, count)) for i in range(count)])  10.2 us
    pallas_call x12, Pallas kernels, call(): pl.pallas_call(kernel, name=name, out_shape=out_shape, in_specs=in_specs,...  8.79 us
    ppermute x6, waiting for transfers between devices, shift(): lax.ppermute(x, axis, [(i, partner(i, step, count)) for i in range(count)])  5.32 us
    ppermute x6, starting transfers between devices, along_blk(): lax.ppermute(x, 'blk', [(i, partner(i // nc, step_x, nx) * nc + partner(i...  4.2 us
    ppermute x6, waiting for transfers between devices, along_blk(): lax.ppermute(x, 'blk', [(i, partner(i // nc, step_x, nx) * nc + partner(i...  0.64 us
  transfers between devices with their start and end apart: 12, of which 7 were waited for; matrix products, arithmetic and copies ran while one was open for 0% of the time, Pallas kernels for 24%

profile of v7, /device:TPU:0, one launch (start us, length us, event | category | flops | bytes accessed | tf_op | source)
XLA Modules:
  0.0 29.3 jit_solution(1768184754219330701)
XLA Ops:
  0.0 0.9 %pack.1 = (bf16[80,128]{1,0:T(8,128)(2,1)S(1)}, bf16[80,128]{1,0:T(8,128)(2,1)S(1)}, bf16[80,128]{1,0:T(8,128)(2,1)S(1)}, bf16[80,128]{1,0:T(8,128)(2,1)S(1)}) custom-call(bf16[4,4,16,128]{3,2,1,0:T(8,128)(2,1)} %bitcast.10, bf16[4,8,128]{2,1,0:T(8,128)(2,1)} %k_hbm.1, bf16[4,8,128]{2,1,0:T(8,128)(2,1)} %v_hbm.1), custom_call_target="tpu_custom_call" | custom-call | bytes 131072 | tf_op jit(solution)/shard_map/pack/pallas_call | solution.py:48
  0.9 0.0 copy-start.2
  0.9 0.0 copy-start.3
  1.0 5.1 %collective-permute-start = (bf16[80,128]{1,0:T(8,128)(2,1)S(1)}, bf16[80,128]{1,0:T(8,128)(2,1)S(1)}, u32[]{:S(2)}, u32[]{:S(2)}) collective-permute-start(bf16[80,128]{1,0:T(8,128)(2,1)S(1)} %get-tuple-element.44), channel_id=1, source_target_pairs={{0,3},{1,2},{2,1},{3,0},{4,7},{5,6},{6,5},{7,4},{8,11},{9,10},{10,... | collective-permute-start | bytes 61448 | tf_op jit(solution)/shard_map/ppermute | solution.py:331
  6.1 0.0 collective-permute-start.1
  6.1 0.6 %collective-permute-start.2 = (bf16[80,128]{1,0:T(8,128)(2,1)S(1)}, bf16[80,128]{1,0:T(8,128)(2,1)S(1)}, u32[]{:S(2)}, u32[]{:S(2)}) collective-permute-start(bf16[80,128]{1,0:T(8,128)(2,1)S(1)} %get-tuple-element.46), channel_id=1, source_target_pairs={{0,1},{1,0},{2,3},{3,2},{4,5},{5,4},{6,7},{7,6},{8,9},{9,8},{10,11... | collective-permute-start | bytes 61448 | tf_op jit(solution)/shard_map/ppermute | solution.py:331
  6.7 0.0 copy-done.2
  6.7 0.0 copy-done.3
  6.7 0.0 copy-start
  6.7 0.0 copy-start.1
  6.7 0.0 copy-start.4
  6.7 0.0 copy-start.5
  6.8 0.5 %split.1 = (bf16[2,2048,128]{2,1,0:T(8,128)(2,1)S(1)}, bf16[2,2048,128]{2,1,0:T(8,128)(2,1)S(1)}, f32[8,128]{1,0:T(8,128)S(1)}) custom-call(bf16[4096,128]{1,0:T(8,128)(2,1)S(1)} %bitcast.8, bf16[4096,128]{1,0:T(8,128)(2,1)S(1)} %bitcast.9), custom_call_target="tpu_custom_call" | custom-call | bytes 4194304 | tf_op jit(solution)/shard_map/split/pallas_call | solution.py:48
  7.3 0.6 %collective-permute-done.refs_0_ = bf16[80,128]{1,0:T(8,128)(2,1)S(1)} collective-permute-done((bf16[80,128]{1,0:T(8,128)(2,1)S(1)}, bf16[80,128]{1,0:T(8,128)(2,1)S(1)}, u32[]{:S(2)}, u32[]{:S(2)}) %collective-permute-start) | collective-permute-done | bytes 20512 | tf_op jit(solution)/shard_map/ppermute | solution.py:331
  7.8 2.9 %collective-permute-done.1.refs_1_ = bf16[80,128]{1,0:T(8,128)(2,1)S(1)} collective-permute-done((bf16[80,128]{1,0:T(8,128)(2,1)S(1)}, bf16[80,128]{1,0:T(8,128)(2,1)S(1)}, u32[]{:S(2)}, u32[]{:S(2)}) %collective-permute-start.1) | collective-permute-done | bytes 20512 | tf_op jit(solution)/shard_map/ppermute | solution.py:331
  10.8 0.0 collective-permute-done.2.refs_2_
  10.8 0.1 collective-permute-start.5
  10.8 1.6 %collective-permute-start.3 = (bf16[4,64,128]{2,1,0:T(8,128)(2,1)S(1)}, bf16[4,64,128]{2,1,0:T(8,128)(2,1)S(1)}, u32[]{:S(2)}, u32[]{:S(2)}) collective-permute-start(bf16[4,64,128]{2,1,0:T(8,128)(2,1)S(1)} %get-tuple-element.50.refs_1_.q_ref), channel_id=1, source_target_pairs={{0,12},{4,8},{8,4},{12,0},{1,13},{5,9},{9,5},{13,1},{2,14},{6,10},... | collective-permute-start | bytes 196616 | tf_op jit(solution)/shard_map/ppermute | solution.py:334
  12.5 0.0 collective-permute-done.5.refs_0_
  12.5 1.7 %prefix_near.1 = (bf16[272,128]{1,0:T(8,128)(2,1)S(1)}, f32[256,128]{1,0:T(8,128)S(1)}, f32[8,128]{1,0:T(8,128)S(1)}) custom-call(bf16[4,64,128]{2,1,0:T(8,128)(2,1)S(1)} %collective-permute-done.5.refs_0_, bf16[4,64,128]{2,1,0:T(8,128)(2,1)S(1)} %get-tuple-element.50.refs_1_.q_ref, bf16[2,2048,128]{2,1,0:T(8,128)(2,1)S(1)} %get-tuple-element.52.refs_2_.refs_1_, ...), custom_call_target="tpu_custom_call" | custom-call | flops 536870912 | bytes 2097152 | tf_op jit(solution)/shard_map/prefix_near/pallas_call | solution.py:48
  14.2 0.6 %collective-permute-done.3.refs_0_ = bf16[4,64,128]{2,1,0:T(8,128)(2,1)S(1)} collective-permute-done((bf16[4,64,128]{2,1,0:T(8,128)(2,1)S(1)}, bf16[4,64,128]{2,1,0:T(8,128)(2,1)S(1)}, u32[]{:S(2)}, u32[]{:S(2)}) %collective-permute-start.3) | collective-permute-done | bytes 65568 | tf_op jit(solution)/shard_map/ppermute | solution.py:334
  14.7 0.4 %collective-permute-start.4 = (bf16[4,64,128]{2,1,0:T(8,128)(2,1)S(1)}, bf16[4,64,128]{2,1,0:T(8,128)(2,1)S(1)}, u32[]{:S(2)}, u32[]{:S(2)}) collective-permute-start(bf16[4,64,128]{2,1,0:T(8,128)(2,1)S(1)} %collective-permute-done.3.refs_0_), channel_id=1, source_target_pairs={{0,4},{4,0},{8,12},{12,8},{1,5},{5,1},{9,13},{13,9},{2,6},{6,2},{1... | collective-permute-start | bytes 196616 | tf_op jit(solution)/shard_map/ppermute | solution.py:334
  15.1 1.1 %prefix_far.1 = bf16[272,128]{1,0:T(8,128)(2,1)S(1)} custom-call(bf16[4,64,128]{2,1,0:T(8,128)(2,1)S(1)} %collective-permute-done.3.refs_0_, bf16[2,2048,128]{2,1,0:T(8,128)(2,1)S(1)} %get-tuple-element.52.refs_2_.refs_1_, bf16[2,2048,128]{2,1,0:T(8,128)(2,1)S(1)} %get-tuple-element.53.refs_3_.refs_2_), custom_call_target="tpu_custom_call" | custom-call | flops 268435456 | bytes 2097152 | tf_op jit(solution)/shard_map/prefix_far/pallas_call | solution.py:48
  16.2 0.2 collective-permute-start.6
  16.4 0.4 %collective-permute-start.7 = (bf16[272,128]{1,0:T(8,128)(2,1)S(1)}, bf16[272,128]{1,0:T(8,128)(2,1)S(1)}, u32[]{:S(2)}, u32[]{:S(2)}) collective-permute-start(bf16[272,128]{1,0:T(8,128)(2,1)S(1)} %get-tuple-element.68), channel_id=1, source_target_pairs={{0,4},{4,0},{8,12},{12,8},{1,5},{5,1},{9,13},{13,9},{2,6},{6,2},{1... | collective-permute-start | bytes 208904 | tf_op jit(solution)/shard_map/ppermute | solution.py:334
  16.8 0.0 collective-permute-done.4.refs_0_
  16.8 1.1 %prefix_x.1 = (f32[256,128]{1,0:T(8,128)S(1)}, f32[8,128]{1,0:T(8,128)S(1)}) custom-call(bf16[4,64,128]{2,1,0:T(8,128)(2,1)S(1)} %collective-permute-done.4.refs_0_, bf16[2,2048,128]{2,1,0:T(8,128)(2,1)S(1)} %get-tuple-element.52.refs_2_.refs_1_, bf16[2,2048,128]{2,1,0:T(8,128)(2,1)S(1)} %get-tuple-element.53.refs_3_.refs_2_), custom_call_target="tpu_custom_call" | custom-call | flops 268435456 | bytes 2097152 | tf_op jit(solution)/shard_map/prefix_x/pallas_call | solution.py:48
  17.8 0.0 collective-permute-done.6.other_ref
  17.8 0.1 join_partials.1
  17.9 1.6 %collective-permute-start.8 = (bf16[272,128]{1,0:T(8,128)(2,1)S(1)}, bf16[272,128]{1,0:T(8,128)(2,1)S(1)}, u32[]{:S(2)}, u32[]{:S(2)}) collective-permute-start(bf16[272,128]{1,0:T(8,128)(2,1)S(1)} %join_partials.1), channel_id=1, source_target_pairs={{0,8},{4,12},{8,0},{12,4},{1,9},{5,13},{9,1},{13,5},{2,10},{6,14},... | collective-permute-start | bytes 208904 | tf_op jit(solution)/shard_map/ppermute | solution.py:334
  19.4 0.0 copy-done
  19.5 0.0 copy-done.1
  19.5 0.0 copy-done.4
  19.5 0.0 copy-done.5
  19.5 2.3 %suffix.1 = (f32[256,128]{1,0:T(8,128)S(1)}, f32[256,128]{1,0:T(8,128)S(1)}) custom-call(bf16[4,64,128]{2,1,0:T(8,128)(2,1)S(1)} %get-tuple-element.50.refs_1_.q_ref, s32[64]{0:T(128)S(1)} %copy-done.4, s32[64]{0:T(128)S(1)} %copy-done.5, bf16[16,1024,128]{2,1,0:T(8,128)(2,1)S(1)} %bitcast.6, bf16[16,1024,128]{2,1,0:T(8,128)(2,1)S(1)} %bitcast.7), custom_call_target="tpu_custom_call" | custom-call | tf_op jit(solution)/shard_map/suffix/pallas_call | solution.py:48
  21.8 0.0 collective-permute-done.7.refs_0_
  21.8 0.4 %near.1 = (f32[256,128]{1,0:T(8,128)S(1)}, f32[8,128]{1,0:T(8,128)S(1)}) custom-call(bf16[4,64,128]{2,1,0:T(8,128)(2,1)S(1)} %get-tuple-element.50.refs_1_.q_ref, bf16[4,16,128]{2,1,0:T(8,128)(2,1)S(1)} %get-tuple-element.51.fresh_ref, f32[256,128]{1,0:T(8,128)S(1)} %get-tuple-element.64.so_ref, f32[256,128]{1,0:T(8,128)S(1)} %get-tuple-element.65.sl_ref, ...), custom_call_target="tpu_custom_call" | custom-call | bytes 655360 | tf_op jit(solution)/shard_map/near/pallas_call | solution.py:48
  22.2 0.1 collective-permute-done.8.refs_0_
  22.3 0.1 final.1
  22.4 1.5 %collective-permute-start.9 = (bf16[64,128]{1,0:T(8,128)(2,1)S(1)}, bf16[64,128]{1,0:T(8,128)(2,1)S(1)}, u32[]{:S(2)}, u32[]{:S(2)}) collective-permute-start(bf16[64,128]{1,0:T(8,128)(2,1)S(1)} %get-tuple-element.71), channel_id=1, source_target_pairs={{0,3},{1,2},{2,1},{3,0},{4,7},{5,6},{6,5},{7,4},{8,11},{9,10},{10,... | collective-permute-start | bytes 49160 | tf_op jit(solution)/shard_map/ppermute | solution.py:331
  23.9 0.6 %collective-permute-start.10 = (bf16[64,128]{1,0:T(8,128)(2,1)S(1)}, bf16[64,128]{1,0:T(8,128)(2,1)S(1)}, u32[]{:S(2)}, u32[]{:S(2)}) collective-permute-start(bf16[64,128]{1,0:T(8,128)(2,1)S(1)} %get-tuple-element.72), channel_id=1, source_target_pairs={{0,2},{1,3},{2,0},{3,1},{4,6},{5,7},{6,4},{7,5},{8,10},{9,11},{10,... | collective-permute-start | bytes 49160 | tf_op jit(solution)/shard_map/ppermute | solution.py:331
  24.5 2.4 %collective-permute-start.11 = (bf16[64,128]{1,0:T(8,128)(2,1)S(1)}, bf16[64,128]{1,0:T(8,128)(2,1)S(1)}, u32[]{:S(2)}, u32[]{:S(2)}) collective-permute-start(bf16[64,128]{1,0:T(8,128)(2,1)S(1)} %get-tuple-element.73), channel_id=1, source_target_pairs={{0,1},{1,0},{2,3},{3,2},{4,5},{5,4},{6,7},{7,6},{8,9},{9,8},{10,11... | collective-permute-start | bytes 49160 | tf_op jit(solution)/shard_map/ppermute | solution.py:331
  26.9 1.1 %collective-permute-done.9.refs_0_ = bf16[64,128]{1,0:T(8,128)(2,1)S(1)} collective-permute-done((bf16[64,128]{1,0:T(8,128)(2,1)S(1)}, bf16[64,128]{1,0:T(8,128)(2,1)S(1)}, u32[]{:S(2)}, u32[]{:S(2)}) %collective-permute-start.9) | collective-permute-done | bytes 16416 | tf_op jit(solution)/shard_map/ppermute | solution.py:331
  28.0 0.5 %collective-permute-done.10.refs_1_ = bf16[64,128]{1,0:T(8,128)(2,1)S(1)} collective-permute-done((bf16[64,128]{1,0:T(8,128)(2,1)S(1)}, bf16[64,128]{1,0:T(8,128)(2,1)S(1)}, u32[]{:S(2)}, u32[]{:S(2)}) %collective-permute-start.10) | collective-permute-done | bytes 16416 | tf_op jit(solution)/shard_map/ppermute | solution.py:331
  28.5 0.2 collective-permute-done.11.refs_2_
  28.7 0.6 %unpack.1 = bf16[4,4,16,128]{3,2,1,0:T(8,128)(2,1)} custom-call(bf16[64,128]{1,0:T(8,128)(2,1)S(1)} %collective-permute-done.9.refs_0_, bf16[64,128]{1,0:T(8,128)(2,1)S(1)} %collective-permute-done.10.refs_1_, bf16[64,128]{1,0:T(8,128)(2,1)S(1)} %collective-permute-done.11.refs_2_, bf16[64,128]{1,0:T(8,128)(2,1)S(1)} %get-tuple-element.74.refs_3_), custom_call_target="tpu_custom_call" | custom-call | bytes 131072 | tf_op jit(solution)/shard_map/unpack/pallas_call | solution.py:48
  (2 shorter events, 0.0 us)
Async XLA Ops:
  0.9 5.8 %copy-start.2 = (bf16[2048,2,128]{2,1,0:T(2,128)(2,1)S(1)}, bf16[2048,2,128]{2,1,0:T(2,128)(2,1)}, u32[]{:S(2)}) copy-start(bf16[2048,2,128]{2,1,0:T(2,128)(2,1)} %param.12) | copy-start | bytes 3145732
  0.9 5.8 %copy-start.3 = (bf16[2048,2,128]{2,1,0:T(2,128)(2,1)S(1)}, bf16[2048,2,128]{2,1,0:T(2,128)(2,1)}, u32[]{:S(2)}) copy-start(bf16[2048,2,128]{2,1,0:T(2,128)(2,1)} %param.13) | copy-start | bytes 3145732
  1.0 6.9 %collective-permute-start = (bf16[80,128]{1,0:T(8,128)(2,1)S(1)}, bf16[80,128]{1,0:T(8,128)(2,1)S(1)}, u32[]{:S(2)}, u32[]{:S(2)}) collective-permute-start(bf16[80,128]{1,0:T(8,128)(2,1)S(1)} %get-tuple-element.44), channel_id=1, source_target_pairs={{0,3},{1,2},{2,1},{3,0},{4,7},{5,6},{6,5},{7,4},{8,11},{9,10},{10,... | collective-permute-start | bytes 61448 | tf_op jit(solution)/shard_map/ppermute | solution.py:331
  6.1 4.7 %collective-permute-start.1 = (bf16[80,128]{1,0:T(8,128)(2,1)S(1)}, bf16[80,128]{1,0:T(8,128)(2,1)S(1)}, u32[]{:S(2)}, u32[]{:S(2)}) collective-permute-start(bf16[80,128]{1,0:T(8,128)(2,1)S(1)} %get-tuple-element.45), channel_id=1, source_target_pairs={{0,2},{1,3},{2,0},{3,1},{4,6},{5,7},{6,4},{7,5},{8,10},{9,11},{10,... | collective-permute-start | bytes 61448 | tf_op jit(solution)/shard_map/ppermute | solution.py:331
  6.1 4.7 %collective-permute-start.2 = (bf16[80,128]{1,0:T(8,128)(2,1)S(1)}, bf16[80,128]{1,0:T(8,128)(2,1)S(1)}, u32[]{:S(2)}, u32[]{:S(2)}) collective-permute-start(bf16[80,128]{1,0:T(8,128)(2,1)S(1)} %get-tuple-element.46), channel_id=1, source_target_pairs={{0,1},{1,0},{2,3},{3,2},{4,5},{5,4},{6,7},{7,6},{8,9},{9,8},{10,11... | collective-permute-start | bytes 61448 | tf_op jit(solution)/shard_map/ppermute | solution.py:331
  6.7 12.7 %copy-start = (bf16[16,512,2,128]{3,2,1,0:T(2,128)(2,1)S(1)}, bf16[16,512,2,128]{3,2,1,0:T(2,128)(2,1)}, u32[]{:S(2)}) copy-start(bf16[16,512,2,128]{3,2,1,0:T(2,128)(2,1)} %param.14) | copy-start | bytes 12582916
  6.7 12.7 %copy-start.1 = (bf16[16,512,2,128]{3,2,1,0:T(2,128)(2,1)S(1)}, bf16[16,512,2,128]{3,2,1,0:T(2,128)(2,1)}, u32[]{:S(2)}) copy-start(bf16[16,512,2,128]{3,2,1,0:T(2,128)(2,1)} %param.15) | copy-start | bytes 12582916
  6.7 12.7 %copy-start.4 = (s32[64]{0:T(128)S(1)}, s32[64]{0:T(128)}, u32[]{:S(2)}) copy-start(s32[64]{0:T(128)} %slot_ref.1) | copy-start | bytes 772
  6.7 12.7 %copy-start.5 = (s32[64]{0:T(128)S(1)}, s32[64]{0:T(128)}, u32[]{:S(2)}) copy-start(s32[64]{0:T(128)} %len_ref.1) | copy-start | bytes 772
  10.8 1.7 %collective-permute-start.5 = (bf16[4,64,128]{2,1,0:T(8,128)(2,1)S(1)}, bf16[4,64,128]{2,1,0:T(8,128)(2,1)S(1)}, u32[]{:S(2)}, u32[]{:S(2)}) collective-permute-start(bf16[4,64,128]{2,1,0:T(8,128)(2,1)S(1)} %get-tuple-element.50.refs_1_.q_ref), channel_id=1, source_target_pairs={{0,4},{4,0},{8,12},{12,8},{1,5},{5,1},{9,13},{13,9},{2,6},{6,2},{1... | collective-permute-start | bytes 196616 | tf_op jit(solution)/shard_map/ppermute | solution.py:334
  10.8 3.9 %collective-permute-start.3 = (bf16[4,64,128]{2,1,0:T(8,128)(2,1)S(1)}, bf16[4,64,128]{2,1,0:T(8,128)(2,1)S(1)}, u32[]{:S(2)}, u32[]{:S(2)}) collective-permute-start(bf16[4,64,128]{2,1,0:T(8,128)(2,1)S(1)} %get-tuple-element.50.refs_1_.q_ref), channel_id=1, source_target_pairs={{0,12},{4,8},{8,4},{12,0},{1,13},{5,9},{9,5},{13,1},{2,14},{6,10},... | collective-permute-start | bytes 196616 | tf_op jit(solution)/shard_map/ppermute | solution.py:334
  14.7 2.0 %collective-permute-start.4 = (bf16[4,64,128]{2,1,0:T(8,128)(2,1)S(1)}, bf16[4,64,128]{2,1,0:T(8,128)(2,1)S(1)}, u32[]{:S(2)}, u32[]{:S(2)}) collective-permute-start(bf16[4,64,128]{2,1,0:T(8,128)(2,1)S(1)} %collective-permute-done.3.refs_0_), channel_id=1, source_target_pairs={{0,4},{4,0},{8,12},{12,8},{1,5},{5,1},{9,13},{13,9},{2,6},{6,2},{1... | collective-permute-start | bytes 196616 | tf_op jit(solution)/shard_map/ppermute | solution.py:334
  16.2 1.6 %collective-permute-start.6 = (bf16[272,128]{1,0:T(8,128)(2,1)S(1)}, bf16[272,128]{1,0:T(8,128)(2,1)S(1)}, u32[]{:S(2)}, u32[]{:S(2)}) collective-permute-start(bf16[272,128]{1,0:T(8,128)(2,1)S(1)} %prefix_far.1), channel_id=1, source_target_pairs={{0,4},{4,0},{8,12},{12,8},{1,5},{5,1},{9,13},{13,9},{2,6},{6,2},{1... | collective-permute-start | bytes 208904 | tf_op jit(solution)/shard_map/ppermute | solution.py:334
  16.4 5.4 %collective-permute-start.7 = (bf16[272,128]{1,0:T(8,128)(2,1)S(1)}, bf16[272,128]{1,0:T(8,128)(2,1)S(1)}, u32[]{:S(2)}, u32[]{:S(2)}) collective-permute-start(bf16[272,128]{1,0:T(8,128)(2,1)S(1)} %get-tuple-element.68), channel_id=1, source_target_pairs={{0,4},{4,0},{8,12},{12,8},{1,5},{5,1},{9,13},{13,9},{2,6},{6,2},{1... | collective-permute-start | bytes 208904 | tf_op jit(solution)/shard_map/ppermute | solution.py:334
  17.9 4.4 %collective-permute-start.8 = (bf16[272,128]{1,0:T(8,128)(2,1)S(1)}, bf16[272,128]{1,0:T(8,128)(2,1)S(1)}, u32[]{:S(2)}, u32[]{:S(2)}) collective-permute-start(bf16[272,128]{1,0:T(8,128)(2,1)S(1)} %join_partials.1), channel_id=1, source_target_pairs={{0,8},{4,12},{8,0},{12,4},{1,9},{5,13},{9,1},{13,5},{2,10},{6,14},... | collective-permute-start | bytes 208904 | tf_op jit(solution)/shard_map/ppermute | solution.py:334
  22.4 5.6 %collective-permute-start.9 = (bf16[64,128]{1,0:T(8,128)(2,1)S(1)}, bf16[64,128]{1,0:T(8,128)(2,1)S(1)}, u32[]{:S(2)}, u32[]{:S(2)}) collective-permute-start(bf16[64,128]{1,0:T(8,128)(2,1)S(1)} %get-tuple-element.71), channel_id=1, source_target_pairs={{0,3},{1,2},{2,1},{3,0},{4,7},{5,6},{6,5},{7,4},{8,11},{9,10},{10,... | collective-permute-start | bytes 49160 | tf_op jit(solution)/shard_map/ppermute | solution.py:331
  23.9 4.6 %collective-permute-start.10 = (bf16[64,128]{1,0:T(8,128)(2,1)S(1)}, bf16[64,128]{1,0:T(8,128)(2,1)S(1)}, u32[]{:S(2)}, u32[]{:S(2)}) collective-permute-start(bf16[64,128]{1,0:T(8,128)(2,1)S(1)} %get-tuple-element.72), channel_id=1, source_target_pairs={{0,2},{1,3},{2,0},{3,1},{4,6},{5,7},{6,4},{7,5},{8,10},{9,11},{10,... | collective-permute-start | bytes 49160 | tf_op jit(solution)/shard_map/ppermute | solution.py:331
  24.5 4.2 %collective-permute-start.11 = (bf16[64,128]{1,0:T(8,128)(2,1)S(1)}, bf16[64,128]{1,0:T(8,128)(2,1)S(1)}, u32[]{:S(2)}, u32[]{:S(2)}) collective-permute-start(bf16[64,128]{1,0:T(8,128)(2,1)S(1)} %get-tuple-element.73), channel_id=1, source_target_pairs={{0,1},{1,0},{2,3},{3,2},{4,5},{5,4},{6,7},{7,6},{8,9},{9,8},{10,11... | collective-permute-start | bytes 49160 | tf_op jit(solution)/shard_map/ppermute | solution.py:331

commit v8 on v7

--- a/solution.py
+++ b/solution.py
@@ -215,8 +215,9 @@
     return heads
 
 
-def prefix_kernel(count, own, local, part, scale, *refs):
-    q_refs, (k_ref, v_ref), outs = refs[:count], refs[count : count + 2], refs[count + 2 :]
+def prefix_kernel(count, own, extra, local, part, scale, *refs):
+    q_refs, (k_ref, v_ref), refs = refs[:count], refs[count : count + 2], refs[count + 2 :]
+    extras, outs = refs[:extra], refs[extra:]
     steps, part = q_refs[0].shape[0], part // local
     columns = steps * part
     qs = [
@@ -232,6 +233,10 @@
         if own and i == count - 1:
             outs[i][...] = jnp.concatenate(os, axis=0)
             outs[i + 1][:local] = jnp.concatenate(lses, axis=0)
+        elif extra:
+            size = extras[0].shape[0]
+            outs[i][:size] = encode(os, lses)
+            outs[i][size:] = extras[0][...]
         else:
             outs[i][...] = encode(os, lses)
 
@@ -240,19 +245,19 @@
     size = o_ref.shape[0] // local
     parts = [
         merge([(o_ref[kl * size : (kl + 1) * size], lse_ref[kl : kl + 1]), other])
-        for kl, other in enumerate(decode(other_ref[...], local))
+        for kl, other in enumerate(decode(other_ref[: out_ref.shape[0]], local))
     ]
     out_ref[...] = encode(*zip(*parts))
 
 
-def near_kernel(count, local, group, scale, q_ref, fresh_ref, so_ref, sl_ref, po_ref, pl_ref, *refs):
+def near_kernel(count, size, local, group, scale, q_ref, fresh_ref, so_ref, sl_ref, po_ref, pl_ref, *refs):
     others, (out_ref, lse_ref) = refs[:count], refs[count:]
     nz, qrows = q_ref.shape[:2]
     part = qrows // local
     nb = part // group
     columns = nz * part
     head_dim = so_ref.shape[1]
-    decoded = [decode(ref[...], local) for ref in others]
+    decoded = [decode(ref[ref.shape[0] - size :], local) for ref in others]
     for kl in range(local):
         scores, news = [], []
         for step in range(nz):
@@ -398,17 +403,20 @@
     ]
     payload = jax.ShapeDtypeStruct((local * head_dim + ceil_to(3 * local, 16), columns), BF16)
 
-    def prefix(name, arrays, own=False):
+    pair = jax.ShapeDtypeStruct((2 * payload.shape[0], columns), BF16)
+
+    def prefix(name, arrays, own=False, extra=(), weight=1):
         count = len(arrays)
+        sent = pair if extra else payload
         return call(
-            functools.partial(prefix_kernel, count, own, local, qrows, scale),
+            functools.partial(prefix_kernel, count, own, len(extra), local, qrows, scale),
             name,
-            [payload] * (count - own) + (state if own else []),
-            (*arrays, keys, values),
-            [VM] * (count + 2),
+            [sent] * (count - own) + (state if own else []),
+            (*arrays, keys, values, *extra),
+            [VM] * (count + 2 + len(extra)),
             vmem=16 << 20,
-            flops=4 * count * rows * positions * head_dim,
-            moved=keys.size * 4,
+            flops=4 * weight * count * rows * positions * head_dim,
+            moved=4 * weight * keys.size,
         )
 
     near_steps = [(0, c) for c in range(1, nc)]
@@ -420,20 +428,21 @@
         return along_blk(x, back(step[0], nx), back(step[1], nc))
 
     rows_of = [arriving[step] for step in near_steps]
-    *sent, own_out, own_lse = prefix("prefix_near", [*rows_of, joined], own=True)
-    received = {step: give_back(x, step) for x, step in zip(sent, near_steps)}
-    sibling = list(received.values())
+    *sibling, own_out, own_lse = prefix("prefix_near", [*rows_of, joined], own=True)
     distant = []
     for far in range(1, nx):
         rows_of, own_lse = lax.optimization_barrier((arriving[far, nc - 1], own_lse))
-        (sent,) = prefix("prefix_far", [rows_of])
+        first = nc > 1 and far == 1
+        (sent,) = prefix("prefix_far", [rows_of], extra=sibling if first else ())
         if nc > 1:
             hopped = give_back(sent, (0, 1))
+            if first:
+                sibling = [hopped]
             rows_of, own_lse = lax.optimization_barrier(
                 (along_blk(arriving[far, nc - 1], 0, 1), own_lse)
             )
             rows_of, sent = lax.optimization_barrier((rows_of, sent))
-            partial = prefix("prefix_x", [rows_of], own=True)
+            partial = prefix("prefix_x", [rows_of], own=True, weight=3)
             sent = call(
                 functools.partial(join_partials_kernel, local),
                 "join_partials",
@@ -443,6 +452,8 @@
             )
         distant.append(give_back(sent, (far, 0)))
         sent, own_lse = lax.optimization_barrier((sent, own_lse))
+    if nx == 1:
+        sibling = [give_back(x, step) for x, step in zip(sibling, near_steps)]
     own_lse, slot_keys = lax.optimization_barrier((own_lse, slot_keys))
     suffix_state = call(
         functools.partial(suffix_kernel, nz, local, group, scale),
@@ -458,7 +469,7 @@
         vmem=8 << 20,
     )
     near = call(
-        functools.partial(near_kernel, len(sibling), local, group, scale),
+        functools.partial(near_kernel, len(sibling), payload.shape[0], local, group, scale),
         "near",
         state,
         (joined, fresh, *suffix_state, own_out, own_lse, *sibling),

time: 29.5 us -> 29.3 us (level)
  starting transfers between devices: 14.4 us -> 14 us
    ppermute x6 -> x5, starting transfers between devices: 4.2 us -> 3.8 us  [along_blk(): lax.ppermute(x, 'blk', [(i, partner(i // nc, step_x, nx) * nc + partner(i...]
    ppermute x6 -> x5, waiting for transfers between devices: 0.64 us -> 0.83 us  [along_blk(): lax.ppermute(x, 'blk', [(i, partner(i // nc, step_x, nx) * nc + partner(i...]
  transfers between devices with their start and end apart: 12 -> 11, of which waited for: 7 -> 8; matrix products, arithmetic and copies ran while one was open for 0% -> 0% of each run, Pallas kernels for 24% -> 24%
where the time goes in v8:
time: 29.3 us; the launch traced here: 29.1 us
  starting transfers between devices  14 us (48%)
  Pallas kernels  8.79 us (30%)
  waiting for transfers between devices  6.14 us (21%)
    ppermute x6, starting transfers between devices, shift(): lax.ppermute(x, axis, [(i, partner(i, step, count)) for i in range(count)])  10.2 us
    pallas_call x12, Pallas kernels, call(): pl.pallas_call(kernel, name=name, out_shape=out_shape, in_specs=in_specs,...  8.79 us
    ppermute x6, waiting for transfers between devices, shift(): lax.ppermute(x, axis, [(i, partner(i, step, count)) for i in range(count)])  5.31 us
    ppermute x5, starting transfers between devices, along_blk(): lax.ppermute(x, 'blk', [(i, partner(i // nc, step_x, nx) * nc + partner(i...  3.8 us
    ppermute x5, waiting for transfers between devices, along_blk(): lax.ppermute(x, 'blk', [(i, partner(i // nc, step_x, nx) * nc + partner(i...  0.83 us
  transfers between devices with their start and end apart: 11, of which 8 were waited for; matrix products, arithmetic and copies ran while one was open for 0% of the time, Pallas kernels for 24%

profile of v8, /device:TPU:0, one launch (start us, length us, event | category | flops | bytes accessed | tf_op | source)
XLA Modules:
  0.0 29.1 jit_solution(12805285984099134000)
XLA Ops:
  0.0 0.9 %pack.1 = (bf16[80,128]{1,0:T(8,128)(2,1)S(1)}, bf16[80,128]{1,0:T(8,128)(2,1)S(1)}, bf16[80,128]{1,0:T(8,128)(2,1)S(1)}, bf16[80,128]{1,0:T(8,128)(2,1)S(1)}) custom-call(bf16[4,4,16,128]{3,2,1,0:T(8,128)(2,1)} %bitcast.10, bf16[4,8,128]{2,1,0:T(8,128)(2,1)} %k_hbm.1, bf16[4,8,128]{2,1,0:T(8,128)(2,1)} %v_hbm.1), custom_call_target="tpu_custom_call" | custom-call | bytes 131072 | tf_op jit(solution)/shard_map/pack/pallas_call | solution.py:48
  0.9 0.0 copy-start.2
  0.9 0.0 copy-start.3
  1.0 5.1 %collective-permute-start = (bf16[80,128]{1,0:T(8,128)(2,1)S(1)}, bf16[80,128]{1,0:T(8,128)(2,1)S(1)}, u32[]{:S(2)}, u32[]{:S(2)}) collective-permute-start(bf16[80,128]{1,0:T(8,128)(2,1)S(1)} %get-tuple-element.44), channel_id=1, source_target_pairs={{0,3},{1,2},{2,1},{3,0},{4,7},{5,6},{6,5},{7,4},{8,11},{9,10},{10,... | collective-permute-start | bytes 61448 | tf_op jit(solution)/shard_map/ppermute | solution.py:336
  6.1 0.0 collective-permute-start.1
  6.1 0.6 %collective-permute-start.2 = (bf16[80,128]{1,0:T(8,128)(2,1)S(1)}, bf16[80,128]{1,0:T(8,128)(2,1)S(1)}, u32[]{:S(2)}, u32[]{:S(2)}) collective-permute-start(bf16[80,128]{1,0:T(8,128)(2,1)S(1)} %get-tuple-element.46), channel_id=1, source_target_pairs={{0,1},{1,0},{2,3},{3,2},{4,5},{5,4},{6,7},{7,6},{8,9},{9,8},{10,11... | collective-permute-start | bytes 61448 | tf_op jit(solution)/shard_map/ppermute | solution.py:336
  6.7 0.0 copy-done.2
  6.7 0.0 copy-done.3
  6.7 0.0 copy-start.1
  6.7 0.5 %split.1 = (bf16[2,2048,128]{2,1,0:T(8,128)(2,1)S(1)}, bf16[2,2048,128]{2,1,0:T(8,128)(2,1)S(1)}, f32[8,128]{1,0:T(8,128)S(1)}) custom-call(bf16[4096,128]{1,0:T(8,128)(2,1)S(1)} %bitcast.8, bf16[4096,128]{1,0:T(8,128)(2,1)S(1)} %bitcast.9), custom_call_target="tpu_custom_call" | custom-call | bytes 4194304 | tf_op jit(solution)/shard_map/split/pallas_call | solution.py:48
  7.2 0.0 copy-start
  7.2 0.0 copy-start.4
  7.2 0.0 copy-start.5
  7.3 0.6 %collective-permute-done.refs_0_ = bf16[80,128]{1,0:T(8,128)(2,1)S(1)} collective-permute-done((bf16[80,128]{1,0:T(8,128)(2,1)S(1)}, bf16[80,128]{1,0:T(8,128)(2,1)S(1)}, u32[]{:S(2)}, u32[]{:S(2)}) %collective-permute-start) | collective-permute-done | bytes 20512 | tf_op jit(solution)/shard_map/ppermute | solution.py:336
  7.8 2.9 %collective-permute-done.1.refs_1_ = bf16[80,128]{1,0:T(8,128)(2,1)S(1)} collective-permute-done((bf16[80,128]{1,0:T(8,128)(2,1)S(1)}, bf16[80,128]{1,0:T(8,128)(2,1)S(1)}, u32[]{:S(2)}, u32[]{:S(2)}) %collective-permute-start.1) | collective-permute-done | bytes 20512 | tf_op jit(solution)/shard_map/ppermute | solution.py:336
  10.8 0.0 collective-permute-done.2.refs_2_
  10.8 0.1 collective-permute-start.5
  10.8 1.6 %collective-permute-start.3 = (bf16[4,64,128]{2,1,0:T(8,128)(2,1)S(1)}, bf16[4,64,128]{2,1,0:T(8,128)(2,1)S(1)}, u32[]{:S(2)}, u32[]{:S(2)}) collective-permute-start(bf16[4,64,128]{2,1,0:T(8,128)(2,1)S(1)} %get-tuple-element.50.refs_1_.q_ref), channel_id=1, source_target_pairs={{0,12},{4,8},{8,4},{12,0},{1,13},{5,9},{9,5},{13,1},{2,14},{6,10},... | collective-permute-start | bytes 196616 | tf_op jit(solution)/shard_map/ppermute | solution.py:339
  12.5 0.0 collective-permute-done.5.refs_0_
  12.5 1.7 %prefix_near.1 = (bf16[272,128]{1,0:T(8,128)(2,1)S(1)}, f32[256,128]{1,0:T(8,128)S(1)}, f32[8,128]{1,0:T(8,128)S(1)}) custom-call(bf16[4,64,128]{2,1,0:T(8,128)(2,1)S(1)} %collective-permute-done.5.refs_0_, bf16[4,64,128]{2,1,0:T(8,128)(2,1)S(1)} %get-tuple-element.50.refs_1_.q_ref, bf16[2,2048,128]{2,1,0:T(8,128)(2,1)S(1)} %get-tuple-element.52.refs_2_.refs_1_, ...), custom_call_target="tpu_custom_call" | custom-call | flops 536870912 | bytes 2097152 | tf_op jit(solution)/shard_map/prefix_near/pallas_call | solution.py:48
  14.2 0.6 %collective-permute-done.3.refs_0_ = bf16[4,64,128]{2,1,0:T(8,128)(2,1)S(1)} collective-permute-done((bf16[4,64,128]{2,1,0:T(8,128)(2,1)S(1)}, bf16[4,64,128]{2,1,0:T(8,128)(2,1)S(1)}, u32[]{:S(2)}, u32[]{:S(2)}) %collective-permute-start.3) | collective-permute-done | bytes 65568 | tf_op jit(solution)/shard_map/ppermute | solution.py:339
  14.7 0.4 %collective-permute-start.4 = (bf16[4,64,128]{2,1,0:T(8,128)(2,1)S(1)}, bf16[4,64,128]{2,1,0:T(8,128)(2,1)S(1)}, u32[]{:S(2)}, u32[]{:S(2)}) collective-permute-start(bf16[4,64,128]{2,1,0:T(8,128)(2,1)S(1)} %collective-permute-done.3.refs_0_), channel_id=1, source_target_pairs={{0,4},{4,0},{8,12},{12,8},{1,5},{5,1},{9,13},{13,9},{2,6},{6,2},{1... | collective-permute-start | bytes 196616 | tf_op jit(solution)/shard_map/ppermute | solution.py:339
  15.1 1.1 %prefix_far.1 = bf16[544,128]{1,0:T(8,128)(2,1)S(1)} custom-call(bf16[4,64,128]{2,1,0:T(8,128)(2,1)S(1)} %collective-permute-done.3.refs_0_, bf16[2,2048,128]{2,1,0:T(8,128)(2,1)S(1)} %get-tuple-element.52.refs_2_.refs_1_, bf16[2,2048,128]{2,1,0:T(8,128)(2,1)S(1)} %get-tuple-element.53.refs_3_.refs_2_, bf16[272,128]{1,0:T(8,128)(2,1)S(1)} %get-tuple-element.58.refs_3_), custom_call_target="tpu_custom_call" | custom-call | flops 268435456 | bytes 2097152 | tf_op jit(solution)/shard_map/prefix_far/pallas_call | solution.py:48
  16.2 0.2 collective-permute-start.6
  16.4 0.0 collective-permute-done.4.refs_0_
  16.4 1.1 %prefix_x.1 = (f32[256,128]{1,0:T(8,128)S(1)}, f32[8,128]{1,0:T(8,128)S(1)}) custom-call(bf16[4,64,128]{2,1,0:T(8,128)(2,1)S(1)} %collective-permute-done.4.refs_0_, bf16[2,2048,128]{2,1,0:T(8,128)(2,1)S(1)} %get-tuple-element.52.refs_2_.refs_1_, bf16[2,2048,128]{2,1,0:T(8,128)(2,1)S(1)} %get-tuple-element.53.refs_3_.refs_2_), custom_call_target="tpu_custom_call" | custom-call | flops 805306368 | bytes 6291456 | tf_op jit(solution)/shard_map/prefix_x/pallas_call | solution.py:48
  17.4 0.2 collective-permute-done.6.other_ref.refs_0_
  17.7 1.6 %collective-permute-start.7 = (bf16[272,128]{1,0:T(8,128)(2,1)S(1)}, bf16[272,128]{1,0:T(8,128)(2,1)S(1)}, u32[]{:S(2)}, u32[]{:S(2)}) collective-permute-start(bf16[272,128]{1,0:T(8,128)(2,1)S(1)} %join_partials.1), channel_id=1, source_target_pairs={{0,8},{4,12},{8,0},{12,4},{1,9},{5,13},{9,1},{13,5},{2,10},{6,14},... | collective-permute-start | bytes 208904 | tf_op jit(solution)/shard_map/ppermute | solution.py:339
  19.2 0.0 copy-done.1
  19.2 0.0 copy-done
  19.2 0.0 copy-done.4
  19.2 0.0 copy-done.5
  19.2 2.3 %suffix.1 = (f32[256,128]{1,0:T(8,128)S(1)}, f32[256,128]{1,0:T(8,128)S(1)}) custom-call(bf16[4,64,128]{2,1,0:T(8,128)(2,1)S(1)} %get-tuple-element.50.refs_1_.q_ref, s32[64]{0:T(128)S(1)} %copy-done.4, s32[64]{0:T(128)S(1)} %copy-done.5, bf16[16,1024,128]{2,1,0:T(8,128)(2,1)S(1)} %bitcast.6, bf16[16,1024,128]{2,1,0:T(8,128)(2,1)S(1)} %bitcast.7), custom_call_target="tpu_custom_call" | custom-call | tf_op jit(solution)/shard_map/suffix/pallas_call | solution.py:48
  21.6 0.4 %near.1 = (f32[256,128]{1,0:T(8,128)S(1)}, f32[8,128]{1,0:T(8,128)S(1)}) custom-call(bf16[4,64,128]{2,1,0:T(8,128)(2,1)S(1)} %get-tuple-element.50.refs_1_.q_ref, bf16[4,16,128]{2,1,0:T(8,128)(2,1)S(1)} %get-tuple-element.51.fresh_ref, f32[256,128]{1,0:T(8,128)S(1)} %get-tuple-element.65.so_ref, f32[256,128]{1,0:T(8,128)S(1)} %get-tuple-element.66.sl_ref, ...), custom_call_target="tpu_custom_call" | custom-call | bytes 655360 | tf_op jit(solution)/shard_map/near/pallas_call | solution.py:48
  22.0 0.1 collective-permute-done.7.refs_0_
  22.1 0.1 final.1
  22.2 1.5 %collective-permute-start.8 = (bf16[64,128]{1,0:T(8,128)(2,1)S(1)}, bf16[64,128]{1,0:T(8,128)(2,1)S(1)}, u32[]{:S(2)}, u32[]{:S(2)}) collective-permute-start(bf16[64,128]{1,0:T(8,128)(2,1)S(1)} %get-tuple-element.71), channel_id=1, source_target_pairs={{0,3},{1,2},{2,1},{3,0},{4,7},{5,6},{6,5},{7,4},{8,11},{9,10},{10,... | collective-permute-start | bytes 49160 | tf_op jit(solution)/shard_map/ppermute | solution.py:336
  23.6 0.6 %collective-permute-start.9 = (bf16[64,128]{1,0:T(8,128)(2,1)S(1)}, bf16[64,128]{1,0:T(8,128)(2,1)S(1)}, u32[]{:S(2)}, u32[]{:S(2)}) collective-permute-start(bf16[64,128]{1,0:T(8,128)(2,1)S(1)} %get-tuple-element.72), channel_id=1, source_target_pairs={{0,2},{1,3},{2,0},{3,1},{4,6},{5,7},{6,4},{7,5},{8,10},{9,11},{10,... | collective-permute-start | bytes 49160 | tf_op jit(solution)/shard_map/ppermute | solution.py:336
  24.3 2.4 %collective-permute-start.10 = (bf16[64,128]{1,0:T(8,128)(2,1)S(1)}, bf16[64,128]{1,0:T(8,128)(2,1)S(1)}, u32[]{:S(2)}, u32[]{:S(2)}) collective-permute-start(bf16[64,128]{1,0:T(8,128)(2,1)S(1)} %get-tuple-element.73), channel_id=1, source_target_pairs={{0,1},{1,0},{2,3},{3,2},{4,5},{5,4},{6,7},{7,6},{8,9},{9,8},{10,11... | collective-permute-start | bytes 49160 | tf_op jit(solution)/shard_map/ppermute | solution.py:336
  26.6 1.1 %collective-permute-done.8.refs_0_ = bf16[64,128]{1,0:T(8,128)(2,1)S(1)} collective-permute-done((bf16[64,128]{1,0:T(8,128)(2,1)S(1)}, bf16[64,128]{1,0:T(8,128)(2,1)S(1)}, u32[]{:S(2)}, u32[]{:S(2)}) %collective-permute-start.8) | collective-permute-done | bytes 16416 | tf_op jit(solution)/shard_map/ppermute | solution.py:336
  27.8 0.5 %collective-permute-done.9.refs_1_ = bf16[64,128]{1,0:T(8,128)(2,1)S(1)} collective-permute-done((bf16[64,128]{1,0:T(8,128)(2,1)S(1)}, bf16[64,128]{1,0:T(8,128)(2,1)S(1)}, u32[]{:S(2)}, u32[]{:S(2)}) %collective-permute-start.9) | collective-permute-done | bytes 16416 | tf_op jit(solution)/shard_map/ppermute | solution.py:336
  28.3 0.2 collective-permute-done.10.refs_2_
  28.5 0.6 %unpack.1 = bf16[4,4,16,128]{3,2,1,0:T(8,128)(2,1)} custom-call(bf16[64,128]{1,0:T(8,128)(2,1)S(1)} %collective-permute-done.8.refs_0_, bf16[64,128]{1,0:T(8,128)(2,1)S(1)} %collective-permute-done.9.refs_1_, bf16[64,128]{1,0:T(8,128)(2,1)S(1)} %collective-permute-done.10.refs_2_, bf16[64,128]{1,0:T(8,128)(2,1)S(1)} %get-tuple-element.74.refs_3_), custom_call_target="tpu_custom_call" | custom-call | bytes 131072 | tf_op jit(solution)/shard_map/unpack/pallas_call | solution.py:48
  (3 shorter events, 0.1 us)
Async XLA Ops:
  0.9 5.8 %copy-start.2 = (bf16[2048,2,128]{2,1,0:T(2,128)(2,1)S(1)}, bf16[2048,2,128]{2,1,0:T(2,128)(2,1)}, u32[]{:S(2)}) copy-start(bf16[2048,2,128]{2,1,0:T(2,128)(2,1)} %param.12) | copy-start | bytes 3145732
  0.9 5.8 %copy-start.3 = (bf16[2048,2,128]{2,1,0:T(2,128)(2,1)S(1)}, bf16[2048,2,128]{2,1,0:T(2,128)(2,1)}, u32[]{:S(2)}) copy-start(bf16[2048,2,128]{2,1,0:T(2,128)(2,1)} %param.13) | copy-start | bytes 3145732
  1.0 6.9 %collective-permute-start = (bf16[80,128]{1,0:T(8,128)(2,1)S(1)}, bf16[80,128]{1,0:T(8,128)(2,1)S(1)}, u32[]{:S(2)}, u32[]{:S(2)}) collective-permute-start(bf16[80,128]{1,0:T(8,128)(2,1)S(1)} %get-tuple-element.44), channel_id=1, source_target_pairs={{0,3},{1,2},{2,1},{3,0},{4,7},{5,6},{6,5},{7,4},{8,11},{9,10},{10,... | collective-permute-start | bytes 61448 | tf_op jit(solution)/shard_map/ppermute | solution.py:336
  6.1 4.7 %collective-permute-start.1 = (bf16[80,128]{1,0:T(8,128)(2,1)S(1)}, bf16[80,128]{1,0:T(8,128)(2,1)S(1)}, u32[]{:S(2)}, u32[]{:S(2)}) collective-permute-start(bf16[80,128]{1,0:T(8,128)(2,1)S(1)} %get-tuple-element.45), channel_id=1, source_target_pairs={{0,2},{1,3},{2,0},{3,1},{4,6},{5,7},{6,4},{7,5},{8,10},{9,11},{10,... | collective-permute-start | bytes 61448 | tf_op jit(solution)/shard_map/ppermute | solution.py:336
  6.1 4.7 %collective-permute-start.2 = (bf16[80,128]{1,0:T(8,128)(2,1)S(1)}, bf16[80,128]{1,0:T(8,128)(2,1)S(1)}, u32[]{:S(2)}, u32[]{:S(2)}) collective-permute-start(bf16[80,128]{1,0:T(8,128)(2,1)S(1)} %get-tuple-element.46), channel_id=1, source_target_pairs={{0,1},{1,0},{2,3},{3,2},{4,5},{5,4},{6,7},{7,6},{8,9},{9,8},{10,11... | collective-permute-start | bytes 61448 | tf_op jit(solution)/shard_map/ppermute | solution.py:336
  6.7 12.5 %copy-start.1 = (bf16[16,512,2,128]{3,2,1,0:T(2,128)(2,1)S(1)}, bf16[16,512,2,128]{3,2,1,0:T(2,128)(2,1)}, u32[]{:S(2)}) copy-start(bf16[16,512,2,128]{3,2,1,0:T(2,128)(2,1)} %param.15) | copy-start | bytes 12582916
  7.2 12.0 %copy-start = (bf16[16,512,2,128]{3,2,1,0:T(2,128)(2,1)S(1)}, bf16[16,512,2,128]{3,2,1,0:T(2,128)(2,1)}, u32[]{:S(2)}) copy-start(bf16[16,512,2,128]{3,2,1,0:T(2,128)(2,1)} %param.14) | copy-start | bytes 12582916
  7.2 12.0 %copy-start.4 = (s32[64]{0:T(128)S(1)}, s32[64]{0:T(128)}, u32[]{:S(2)}) copy-start(s32[64]{0:T(128)} %slot_ref.1) | copy-start | bytes 772
  7.2 12.0 %copy-start.5 = (s32[64]{0:T(128)S(1)}, s32[64]{0:T(128)}, u32[]{:S(2)}) copy-start(s32[64]{0:T(128)} %len_ref.1) | copy-start | bytes 772
  10.8 1.7 %collective-permute-start.5 = (bf16[4,64,128]{2,1,0:T(8,128)(2,1)S(1)}, bf16[4,64,128]{2,1,0:T(8,128)(2,1)S(1)}, u32[]{:S(2)}, u32[]{:S(2)}) collective-permute-start(bf16[4,64,128]{2,1,0:T(8,128)(2,1)S(1)} %get-tuple-element.50.refs_1_.q_ref), channel_id=1, source_target_pairs={{0,4},{4,0},{8,12},{12,8},{1,5},{5,1},{9,13},{13,9},{2,6},{6,2},{1... | collective-permute-start | bytes 196616 | tf_op jit(solution)/shard_map/ppermute | solution.py:339
  10.8 3.9 %collective-permute-start.3 = (bf16[4,64,128]{2,1,0:T(8,128)(2,1)S(1)}, bf16[4,64,128]{2,1,0:T(8,128)(2,1)S(1)}, u32[]{:S(2)}, u32[]{:S(2)}) collective-permute-start(bf16[4,64,128]{2,1,0:T(8,128)(2,1)S(1)} %get-tuple-element.50.refs_1_.q_ref), channel_id=1, source_target_pairs={{0,12},{4,8},{8,4},{12,0},{1,13},{5,9},{9,5},{13,1},{2,14},{6,10},... | collective-permute-start | bytes 196616 | tf_op jit(solution)/shard_map/ppermute | solution.py:339
  14.7 1.6 %collective-permute-start.4 = (bf16[4,64,128]{2,1,0:T(8,128)(2,1)S(1)}, bf16[4,64,128]{2,1,0:T(8,128)(2,1)S(1)}, u32[]{:S(2)}, u32[]{:S(2)}) collective-permute-start(bf16[4,64,128]{2,1,0:T(8,128)(2,1)S(1)} %collective-permute-done.3.refs_0_), channel_id=1, source_target_pairs={{0,4},{4,0},{8,12},{12,8},{1,5},{5,1},{9,13},{13,9},{2,6},{6,2},{1... | collective-permute-start | bytes 196616 | tf_op jit(solution)/shard_map/ppermute | solution.py:339
  16.2 1.4 %collective-permute-start.6 = (bf16[544,128]{1,0:T(8,128)(2,1)S(1)}, bf16[544,128]{1,0:T(8,128)(2,1)S(1)}, u32[]{:S(2)}, u32[]{:S(2)}) collective-permute-start(bf16[544,128]{1,0:T(8,128)(2,1)S(1)} %prefix_far.1), channel_id=1, source_target_pairs={{0,4},{4,0},{8,12},{12,8},{1,5},{5,1},{9,13},{13,9},{2,6},{6,2},{1... | collective-permute-start | bytes 417800 | tf_op jit(solution)/shard_map/ppermute | solution.py:339
  17.7 4.4 %collective-permute-start.7 = (bf16[272,128]{1,0:T(8,128)(2,1)S(1)}, bf16[272,128]{1,0:T(8,128)(2,1)S(1)}, u32[]{:S(2)}, u32[]{:S(2)}) collective-permute-start(bf16[272,128]{1,0:T(8,128)(2,1)S(1)} %join_partials.1), channel_id=1, source_target_pairs={{0,8},{4,12},{8,0},{12,4},{1,9},{5,13},{9,1},{13,5},{2,10},{6,14},... | collective-permute-start | bytes 208904 | tf_op jit(solution)/shard_map/ppermute | solution.py:339
  22.2 5.6 %collective-permute-start.8 = (bf16[64,128]{1,0:T(8,128)(2,1)S(1)}, bf16[64,128]{1,0:T(8,128)(2,1)S(1)}, u32[]{:S(2)}, u32[]{:S(2)}) collective-permute-start(bf16[64,128]{1,0:T(8,128)(2,1)S(1)} %get-tuple-element.71), channel_id=1, source_target_pairs={{0,3},{1,2},{2,1},{3,0},{4,7},{5,6},{6,5},{7,4},{8,11},{9,10},{10,... | collective-permute-start | bytes 49160 | tf_op jit(solution)/shard_map/ppermute | solution.py:336
  23.6 4.6 %collective-permute-start.9 = (bf16[64,128]{1,0:T(8,128)(2,1)S(1)}, bf16[64,128]{1,0:T(8,128)(2,1)S(1)}, u32[]{:S(2)}, u32[]{:S(2)}) collective-permute-start(bf16[64,128]{1,0:T(8,128)(2,1)S(1)} %get-tuple-element.72), channel_id=1, source_target_pairs={{0,2},{1,3},{2,0},{3,1},{4,6},{5,7},{6,4},{7,5},{8,10},{9,11},{10,... | collective-permute-start | bytes 49160 | tf_op jit(solution)/shard_map/ppermute | solution.py:336
  24.3 4.2 %collective-permute-start.10 = (bf16[64,128]{1,0:T(8,128)(2,1)S(1)}, bf16[64,128]{1,0:T(8,128)(2,1)S(1)}, u32[]{:S(2)}, u32[]{:S(2)}) collective-permute-start(bf16[64,128]{1,0:T(8,128)(2,1)S(1)} %get-tuple-element.73), channel_id=1, source_target_pairs={{0,1},{1,0},{2,3},{3,2},{4,5},{5,4},{6,7},{7,6},{8,9},{9,8},{10,11... | collective-permute-start | bytes 49160 | tf_op jit(solution)/shard_map/ppermute | solution.py:336

commit v9 on v7

--- a/solution.py
+++ b/solution.py
@@ -59,10 +59,9 @@
 
 def pack_kernel(nz, local, group, pad, q_hbm, k_hbm, v_hbm, *refs):
     out_refs, (q_ref, k_ref, v_ref, sems) = refs[:nz], refs[nz:]
-    copies = [
-        pltpu.make_async_copy(src, dst, sems.at[i])
-        for i, (src, dst) in enumerate(((q_hbm, q_ref), (k_hbm, k_ref), (v_hbm, v_ref)))
-    ]
+    pairs = [(q_hbm.at[b], q_ref.at[b]) for b in range(q_hbm.shape[0])]
+    pairs += [(k_hbm, k_ref), (v_hbm, v_ref)]
+    copies = [pltpu.make_async_copy(src, dst, sems.at[i]) for i, (src, dst) in enumerate(pairs)]
     for copy in copies:
         copy.start()
     for copy in copies:
@@ -215,13 +214,29 @@
     return heads
 
 
-def prefix_kernel(count, own, local, part, scale, *refs):
+def bundle_kernel(q_ref, payload_ref, out_ref):
+    steps, qrows = q_ref.shape[:2]
+    for z in range(steps):
+        out_ref[z * qrows : (z + 1) * qrows] = q_ref[z]
+    out_ref[steps * qrows :] = payload_ref[...]
+
+
+def prefix_kernel(count, own, steps, local, part, scale, *refs):
     q_refs, (k_ref, v_ref), outs = refs[:count], refs[count : count + 2], refs[count + 2 :]
-    steps, part = q_refs[0].shape[0], part // local
+    qrows = part
+
+    def rows_at(ref, z, lo, hi):
+        return ref[z, lo:hi] if len(ref.shape) == 3 else ref[z * qrows + lo : z * qrows + hi]
+
+    part = part // local
     columns = steps * part
     qs = [
         jnp.concatenate(
-            [ref[z, kl * part : (kl + 1) * part] for ref in q_refs for z in range(steps)], axis=0
+            [
+                rows_at(ref, z, kl * part, (kl + 1) * part)
+                for ref in q_refs
+                for z in range(steps)
+            ], axis=0
         )
         for kl in range(local)
     ]
@@ -240,19 +255,19 @@
     size = o_ref.shape[0] // local
     parts = [
         merge([(o_ref[kl * size : (kl + 1) * size], lse_ref[kl : kl + 1]), other])
-        for kl, other in enumerate(decode(other_ref[...], local))
+        for kl, other in enumerate(decode(other_ref[: out_ref.shape[0]], local))
     ]
     out_ref[...] = encode(*zip(*parts))
 
 
-def near_kernel(count, local, group, scale, q_ref, fresh_ref, so_ref, sl_ref, po_ref, pl_ref, *refs):
+def near_kernel(count, size, local, group, scale, q_ref, fresh_ref, so_ref, sl_ref, po_ref, pl_ref, *refs):
     others, (out_ref, lse_ref) = refs[:count], refs[count:]
     nz, qrows = q_ref.shape[:2]
     part = qrows // local
     nb = part // group
     columns = nz * part
     head_dim = so_ref.shape[1]
-    decoded = [decode(ref[...], local) for ref in others]
+    decoded = [decode(ref[ref.shape[0] - size :], local) for ref in others]
     for kl in range(local):
         scores, news = [], []
         for step in range(nz):
@@ -353,7 +368,7 @@
             pltpu.VMEM((nb, nz, heads // nz, head_dim), BF16),
             pltpu.VMEM(new_keys.shape, BF16),
             pltpu.VMEM(new_keys.shape, BF16),
-            pltpu.SemaphoreType.DMA((3,)),
+            pltpu.SemaphoreType.DMA((nb + 2,)),
         ],
         moved=queries.size * 4,
     )
@@ -398,17 +413,19 @@
     ]
     payload = jax.ShapeDtypeStruct((local * head_dim + ceil_to(3 * local, 16), columns), BF16)
 
+    bundle = jax.ShapeDtypeStruct((rows + payload.shape[0], head_dim), BF16)
+
     def prefix(name, arrays, own=False):
         count = len(arrays)
         return call(
-            functools.partial(prefix_kernel, count, own, local, qrows, scale),
+            functools.partial(prefix_kernel, count, own, nz, local, qrows, scale),
             name,
             [payload] * (count - own) + (state if own else []),
             (*arrays, keys, values),
             [VM] * (count + 2),
             vmem=16 << 20,
             flops=4 * count * rows * positions * head_dim,
-            moved=keys.size * 4,
+            moved=4 * keys.size,
         )
 
     near_steps = [(0, c) for c in range(1, nc)]
@@ -420,18 +437,24 @@
         return along_blk(x, back(step[0], nx), back(step[1], nc))
 
     rows_of = [arriving[step] for step in near_steps]
-    *sent, own_out, own_lse = prefix("prefix_near", [*rows_of, joined], own=True)
-    received = {step: give_back(x, step) for x, step in zip(sent, near_steps)}
-    sibling = list(received.values())
+    *sibling, own_out, own_lse = prefix("prefix_near", [*rows_of, joined], own=True)
     distant = []
+    returned = False
     for far in range(1, nx):
         rows_of, own_lse = lax.optimization_barrier((arriving[far, nc - 1], own_lse))
         (sent,) = prefix("prefix_far", [rows_of])
         if nc > 1:
             hopped = give_back(sent, (0, 1))
-            rows_of, own_lse = lax.optimization_barrier(
-                (along_blk(arriving[far, nc - 1], 0, 1), own_lse)
-            )
+            queries_of = arriving[far, nc - 1]
+            if far == 1 and columns == head_dim:
+                queries_of = call(
+                    bundle_kernel, "bundle", bundle, (queries_of, *sibling), [VM] * 2
+                )
+            queries_of = along_blk(queries_of, 0, 1)
+            if far == 1 and columns == head_dim:
+                sibling = [queries_of]
+                returned = True
+            rows_of, own_lse = lax.optimization_barrier((queries_of, own_lse))
             rows_of, sent = lax.optimization_barrier((rows_of, sent))
             partial = prefix("prefix_x", [rows_of], own=True)
             sent = call(
@@ -443,6 +466,8 @@
             )
         distant.append(give_back(sent, (far, 0)))
         sent, own_lse = lax.optimization_barrier((sent, own_lse))
+    if not returned:
+        sibling = [give_back(x, step) for x, step in zip(sibling, near_steps)]
     own_lse, slot_keys = lax.optimization_barrier((own_lse, slot_keys))
     suffix_state = call(
         functools.partial(suffix_kernel, nz, local, group, scale),
@@ -458,7 +483,7 @@
         vmem=8 << 20,
     )
     near = call(
-        functools.partial(near_kernel, len(sibling), local, group, scale),
+        functools.partial(near_kernel, len(sibling), payload.shape[0], local, group, scale),
         "near",
         state,
         (joined, fresh, *suffix_state, own_out, own_lse, *sibling),

time: 29.5 us -> 29.4 us (level)
  starting transfers between devices: 14.4 us -> 14.1 us
    ppermute x6 -> x5, starting transfers between devices: 4.2 us -> 3.87 us  [along_blk(): lax.ppermute(x, 'blk', [(i, partner(i // nc, step_x, nx) * nc + partner(i...]
    ppermute x6 -> x5, waiting for transfers between devices: 0.64 us -> 0.82 us  [along_blk(): lax.ppermute(x, 'blk', [(i, partner(i // nc, step_x, nx) * nc + partner(i...]
    pallas_call x12 -> x13, Pallas kernels: 8.79 us -> 8.76 us  [call(): pl.pallas_call(kernel, name=name, out_shape=out_shape, in_specs=in_specs,...]
  transfers between devices with their start and end apart: 12 -> 11, of which waited for: 7 -> 8; matrix products, arithmetic and copies ran while one was open for 0% -> 0% of each run, Pallas kernels for 24% -> 24%
where the time goes in v9:
time: 29.4 us; the launch traced here: 29.1 us
  starting transfers between devices  14.1 us (48%)
  Pallas kernels  8.76 us (30%)
  waiting for transfers between devices  6.13 us (21%)
    ppermute x6, starting transfers between devices, shift(): lax.ppermute(x, axis, [(i, partner(i, step, count)) for i in range(count)])  10.2 us
    pallas_call x13, Pallas kernels, call(): pl.pallas_call(kernel, name=name, out_shape=out_shape, in_specs=in_specs,...  8.76 us
    ppermute x6, waiting for transfers between devices, shift(): lax.ppermute(x, axis, [(i, partner(i, step, count)) for i in range(count)])  5.31 us
    ppermute x5, starting transfers between devices, along_blk(): lax.ppermute(x, 'blk', [(i, partner(i // nc, step_x, nx) * nc + partner(i...  3.87 us
    ppermute x5, waiting for transfers between devices, along_blk(): lax.ppermute(x, 'blk', [(i, partner(i // nc, step_x, nx) * nc + partner(i...  0.82 us
  transfers between devices with their start and end apart: 11, of which 8 were waited for; matrix products, arithmetic and copies ran while one was open for 0% of the time, Pallas kernels for 24%

profile of v9, /device:TPU:0, one launch (start us, length us, event | category | flops | bytes accessed | tf_op | source)
XLA Modules:
  0.0 29.1 jit_solution(4336744236680507593)
XLA Ops:
  0.0 0.9 %pack.1 = (bf16[80,128]{1,0:T(8,128)(2,1)S(1)}, bf16[80,128]{1,0:T(8,128)(2,1)S(1)}, bf16[80,128]{1,0:T(8,128)(2,1)S(1)}, bf16[80,128]{1,0:T(8,128)(2,1)S(1)}) custom-call(bf16[4,4,16,128]{3,2,1,0:T(8,128)(2,1)} %bitcast.10, bf16[4,8,128]{2,1,0:T(8,128)(2,1)} %k_hbm.1, bf16[4,8,128]{2,1,0:T(8,128)(2,1)} %v_hbm.1), custom_call_target="tpu_custom_call" | custom-call | bytes 131072 | tf_op jit(solution)/shard_map/pack/pallas_call | solution.py:48
  0.9 0.0 copy-start.2
  0.9 0.0 copy-start.3
  0.9 5.1 %collective-permute-start = (bf16[80,128]{1,0:T(8,128)(2,1)S(1)}, bf16[80,128]{1,0:T(8,128)(2,1)S(1)}, u32[]{:S(2)}, u32[]{:S(2)}) collective-permute-start(bf16[80,128]{1,0:T(8,128)(2,1)S(1)} %get-tuple-element.44), channel_id=1, source_target_pairs={{0,3},{1,2},{2,1},{3,0},{4,7},{5,6},{6,5},{7,4},{8,11},{9,10},{10,... | collective-permute-start | bytes 61448 | tf_op jit(solution)/shard_map/ppermute | solution.py:346
  6.0 0.0 collective-permute-start.1
  6.0 0.6 %collective-permute-start.2 = (bf16[80,128]{1,0:T(8,128)(2,1)S(1)}, bf16[80,128]{1,0:T(8,128)(2,1)S(1)}, u32[]{:S(2)}, u32[]{:S(2)}) collective-permute-start(bf16[80,128]{1,0:T(8,128)(2,1)S(1)} %get-tuple-element.46), channel_id=1, source_target_pairs={{0,1},{1,0},{2,3},{3,2},{4,5},{5,4},{6,7},{7,6},{8,9},{9,8},{10,11... | collective-permute-start | bytes 61448 | tf_op jit(solution)/shard_map/ppermute | solution.py:346
  6.7 0.0 copy-done.2
  6.7 0.0 copy-done.3
  6.7 0.0 copy-start.1
  6.7 0.5 %split.1 = (bf16[2,2048,128]{2,1,0:T(8,128)(2,1)S(1)}, bf16[2,2048,128]{2,1,0:T(8,128)(2,1)S(1)}, f32[8,128]{1,0:T(8,128)S(1)}) custom-call(bf16[4096,128]{1,0:T(8,128)(2,1)S(1)} %bitcast.8, bf16[4096,128]{1,0:T(8,128)(2,1)S(1)} %bitcast.9), custom_call_target="tpu_custom_call" | custom-call | bytes 4194304 | tf_op jit(solution)/shard_map/split/pallas_call | solution.py:48
  7.2 0.0 copy-start
  7.2 0.0 copy-start.4
  7.2 0.0 copy-start.5
  7.2 0.6 %collective-permute-done.refs_0_ = bf16[80,128]{1,0:T(8,128)(2,1)S(1)} collective-permute-done((bf16[80,128]{1,0:T(8,128)(2,1)S(1)}, bf16[80,128]{1,0:T(8,128)(2,1)S(1)}, u32[]{:S(2)}, u32[]{:S(2)}) %collective-permute-start) | collective-permute-done | bytes 20512 | tf_op jit(solution)/shard_map/ppermute | solution.py:346
  7.8 2.9 %collective-permute-done.1.refs_1_ = bf16[80,128]{1,0:T(8,128)(2,1)S(1)} collective-permute-done((bf16[80,128]{1,0:T(8,128)(2,1)S(1)}, bf16[80,128]{1,0:T(8,128)(2,1)S(1)}, u32[]{:S(2)}, u32[]{:S(2)}) %collective-permute-start.1) | collective-permute-done | bytes 20512 | tf_op jit(solution)/shard_map/ppermute | solution.py:346
  10.7 0.0 collective-permute-done.2.refs_2_
  10.7 0.1 collective-permute-start.4
  10.8 1.6 %collective-permute-start.3 = (bf16[4,64,128]{2,1,0:T(8,128)(2,1)S(1)}, bf16[4,64,128]{2,1,0:T(8,128)(2,1)S(1)}, u32[]{:S(2)}, u32[]{:S(2)}) collective-permute-start(bf16[4,64,128]{2,1,0:T(8,128)(2,1)S(1)} %get-tuple-element.50.refs_1_.q_ref), channel_id=1, source_target_pairs={{0,12},{4,8},{8,4},{12,0},{1,13},{5,9},{9,5},{13,1},{2,14},{6,10},... | collective-permute-start | bytes 196616 | tf_op jit(solution)/shard_map/ppermute | solution.py:349
  12.4 0.0 collective-permute-done.4.refs_0_
  12.4 1.7 %prefix_near.1 = (bf16[272,128]{1,0:T(8,128)(2,1)S(1)}, f32[256,128]{1,0:T(8,128)S(1)}, f32[8,128]{1,0:T(8,128)S(1)}) custom-call(bf16[4,64,128]{2,1,0:T(8,128)(2,1)S(1)} %collective-permute-done.4.refs_0_, bf16[4,64,128]{2,1,0:T(8,128)(2,1)S(1)} %get-tuple-element.50.refs_1_.q_ref, bf16[2,2048,128]{2,1,0:T(8,128)(2,1)S(1)} %get-tuple-element.52.refs_2_.refs_1_, ...), custom_call_target="tpu_custom_call" | custom-call | flops 536870912 | bytes 2097152 | tf_op jit(solution)/shard_map/prefix_near/pallas_call | solution.py:48
  14.1 0.6 %collective-permute-done.3.q_ref.refs_0_ = bf16[4,64,128]{2,1,0:T(8,128)(2,1)S(1)} collective-permute-done((bf16[4,64,128]{2,1,0:T(8,128)(2,1)S(1)}, bf16[4,64,128]{2,1,0:T(8,128)(2,1)S(1)}, u32[]{:S(2)}, u32[]{:S(2)}) %collective-permute-start.3) | collective-permute-done | bytes 65568 | tf_op jit(solution)/shard_map/ppermute | solution.py:349
  14.7 0.5 %collective-permute-start.5 = (bf16[528,128]{1,0:T(8,128)(2,1)S(1)}, bf16[528,128]{1,0:T(8,128)(2,1)S(1)}, u32[]{:S(2)}, u32[]{:S(2)}) collective-permute-start(bf16[528,128]{1,0:T(8,128)(2,1)S(1)} %bundle.1), channel_id=1, source_target_pairs={{0,4},{4,0},{8,12},{12,8},{1,5},{5,1},{9,13},{13,9},{2,6},{6,2},{1... | collective-permute-start | bytes 405512 | tf_op jit(solution)/shard_map/ppermute | solution.py:349
  15.2 1.1 %prefix_far.1 = bf16[272,128]{1,0:T(8,128)(2,1)S(1)} custom-call(bf16[4,64,128]{2,1,0:T(8,128)(2,1)S(1)} %collective-permute-done.3.q_ref.refs_0_, bf16[2,2048,128]{2,1,0:T(8,128)(2,1)S(1)} %get-tuple-element.52.refs_2_.refs_1_, bf16[2,2048,128]{2,1,0:T(8,128)(2,1)S(1)} %get-tuple-element.53.refs_3_.refs_2_), custom_call_target="tpu_custom_call" | custom-call | flops 268435456 | bytes 2097152 | tf_op jit(solution)/shard_map/prefix_far/pallas_call | solution.py:48
  16.2 0.2 collective-permute-start.6
  16.4 0.0 collective-permute-done.5.refs_0_
  16.4 1.1 %prefix_x.1 = (f32[256,128]{1,0:T(8,128)S(1)}, f32[8,128]{1,0:T(8,128)S(1)}) custom-call(bf16[528,128]{1,0:T(8,128)(2,1)S(1)} %collective-permute-done.5.refs_0_, bf16[2,2048,128]{2,1,0:T(8,128)(2,1)S(1)} %get-tuple-element.52.refs_2_.refs_1_, bf16[2,2048,128]{2,1,0:T(8,128)(2,1)S(1)} %get-tuple-element.53.refs_3_.refs_2_), custom_call_target="tpu_custom_call" | custom-call | flops 268435456 | bytes 2097152 | tf_op jit(solution)/shard_map/prefix_x/pallas_call | solution.py:48
  17.5 0.1 collective-permute-done.6.other_ref
  17.6 1.6 %collective-permute-start.7 = (bf16[272,128]{1,0:T(8,128)(2,1)S(1)}, bf16[272,128]{1,0:T(8,128)(2,1)S(1)}, u32[]{:S(2)}, u32[]{:S(2)}) collective-permute-start(bf16[272,128]{1,0:T(8,128)(2,1)S(1)} %join_partials.1), channel_id=1, source_target_pairs={{0,8},{4,12},{8,0},{12,4},{1,9},{5,13},{9,1},{13,5},{2,10},{6,14},... | collective-permute-start | bytes 208904 | tf_op jit(solution)/shard_map/ppermute | solution.py:349
  19.2 0.0 copy-done.1
  19.2 0.0 copy-done
  19.2 0.0 copy-done.4
  19.2 0.0 copy-done.5
  19.2 2.3 %suffix.1 = (f32[256,128]{1,0:T(8,128)S(1)}, f32[256,128]{1,0:T(8,128)S(1)}) custom-call(bf16[4,64,128]{2,1,0:T(8,128)(2,1)S(1)} %get-tuple-element.50.refs_1_.q_ref, s32[64]{0:T(128)S(1)} %copy-done.4, s32[64]{0:T(128)S(1)} %copy-done.5, bf16[16,1024,128]{2,1,0:T(8,128)(2,1)S(1)} %bitcast.6, bf16[16,1024,128]{2,1,0:T(8,128)(2,1)S(1)} %bitcast.7), custom_call_target="tpu_custom_call" | custom-call | tf_op jit(solution)/shard_map/suffix/pallas_call | solution.py:48
  21.5 0.4 %near.1 = (f32[256,128]{1,0:T(8,128)S(1)}, f32[8,128]{1,0:T(8,128)S(1)}) custom-call(bf16[4,64,128]{2,1,0:T(8,128)(2,1)S(1)} %get-tuple-element.50.refs_1_.q_ref, bf16[4,16,128]{2,1,0:T(8,128)(2,1)S(1)} %get-tuple-element.51.fresh_ref, f32[256,128]{1,0:T(8,128)S(1)} %get-tuple-element.65.so_ref, f32[256,128]{1,0:T(8,128)S(1)} %get-tuple-element.66.sl_ref, ...), custom_call_target="tpu_custom_call" | custom-call | bytes 655360 | tf_op jit(solution)/shard_map/near/pallas_call | solution.py:48
  21.9 0.2 collective-permute-done.7.refs_0_
  22.1 0.1 final.1
  22.2 1.5 %collective-permute-start.8 = (bf16[64,128]{1,0:T(8,128)(2,1)S(1)}, bf16[64,128]{1,0:T(8,128)(2,1)S(1)}, u32[]{:S(2)}, u32[]{:S(2)}) collective-permute-start(bf16[64,128]{1,0:T(8,128)(2,1)S(1)} %get-tuple-element.71), channel_id=1, source_target_pairs={{0,3},{1,2},{2,1},{3,0},{4,7},{5,6},{6,5},{7,4},{8,11},{9,10},{10,... | collective-permute-start | bytes 49160 | tf_op jit(solution)/shard_map/ppermute | solution.py:346
  23.7 0.6 %collective-permute-start.9 = (bf16[64,128]{1,0:T(8,128)(2,1)S(1)}, bf16[64,128]{1,0:T(8,128)(2,1)S(1)}, u32[]{:S(2)}, u32[]{:S(2)}) collective-permute-start(bf16[64,128]{1,0:T(8,128)(2,1)S(1)} %get-tuple-element.72), channel_id=1, source_target_pairs={{0,2},{1,3},{2,0},{3,1},{4,6},{5,7},{6,4},{7,5},{8,10},{9,11},{10,... | collective-permute-start | bytes 49160 | tf_op jit(solution)/shard_map/ppermute | solution.py:346
  24.3 2.4 %collective-permute-start.10 = (bf16[64,128]{1,0:T(8,128)(2,1)S(1)}, bf16[64,128]{1,0:T(8,128)(2,1)S(1)}, u32[]{:S(2)}, u32[]{:S(2)}) collective-permute-start(bf16[64,128]{1,0:T(8,128)(2,1)S(1)} %get-tuple-element.73), channel_id=1, source_target_pairs={{0,1},{1,0},{2,3},{3,2},{4,5},{5,4},{6,7},{7,6},{8,9},{9,8},{10,11... | collective-permute-start | bytes 49160 | tf_op jit(solution)/shard_map/ppermute | solution.py:346
  26.7 1.1 %collective-permute-done.8.refs_0_ = bf16[64,128]{1,0:T(8,128)(2,1)S(1)} collective-permute-done((bf16[64,128]{1,0:T(8,128)(2,1)S(1)}, bf16[64,128]{1,0:T(8,128)(2,1)S(1)}, u32[]{:S(2)}, u32[]{:S(2)}) %collective-permute-start.8) | collective-permute-done | bytes 16416 | tf_op jit(solution)/shard_map/ppermute | solution.py:346
  27.8 0.5 %collective-permute-done.9.refs_1_ = bf16[64,128]{1,0:T(8,128)(2,1)S(1)} collective-permute-done((bf16[64,128]{1,0:T(8,128)(2,1)S(1)}, bf16[64,128]{1,0:T(8,128)(2,1)S(1)}, u32[]{:S(2)}, u32[]{:S(2)}) %collective-permute-start.9) | collective-permute-done | bytes 16416 | tf_op jit(solution)/shard_map/ppermute | solution.py:346
  28.3 0.2 collective-permute-done.10.refs_2_
  28.5 0.6 %unpack.1 = bf16[4,4,16,128]{3,2,1,0:T(8,128)(2,1)} custom-call(bf16[64,128]{1,0:T(8,128)(2,1)S(1)} %collective-permute-done.8.refs_0_, bf16[64,128]{1,0:T(8,128)(2,1)S(1)} %collective-permute-done.9.refs_1_, bf16[64,128]{1,0:T(8,128)(2,1)S(1)} %collective-permute-done.10.refs_2_, bf16[64,128]{1,0:T(8,128)(2,1)S(1)} %get-tuple-element.74.refs_3_), custom_call_target="tpu_custom_call" | custom-call | bytes 131072 | tf_op jit(solution)/shard_map/unpack/pallas_call | solution.py:48
  (4 shorter events, 0.1 us)
Async XLA Ops:
  0.9 5.8 %copy-start.2 = (bf16[2048,2,128]{2,1,0:T(2,128)(2,1)S(1)}, bf16[2048,2,128]{2,1,0:T(2,128)(2,1)}, u32[]{:S(2)}) copy-start(bf16[2048,2,128]{2,1,0:T(2,128)(2,1)} %param.12) | copy-start | bytes 3145732
  0.9 5.8 %copy-start.3 = (bf16[2048,2,128]{2,1,0:T(2,128)(2,1)S(1)}, bf16[2048,2,128]{2,1,0:T(2,128)(2,1)}, u32[]{:S(2)}) copy-start(bf16[2048,2,128]{2,1,0:T(2,128)(2,1)} %param.13) | copy-start | bytes 3145732
  0.9 6.9 %collective-permute-start = (bf16[80,128]{1,0:T(8,128)(2,1)S(1)}, bf16[80,128]{1,0:T(8,128)(2,1)S(1)}, u32[]{:S(2)}, u32[]{:S(2)}) collective-permute-start(bf16[80,128]{1,0:T(8,128)(2,1)S(1)} %get-tuple-element.44), channel_id=1, source_target_pairs={{0,3},{1,2},{2,1},{3,0},{4,7},{5,6},{6,5},{7,4},{8,11},{9,10},{10,... | collective-permute-start | bytes 61448 | tf_op jit(solution)/shard_map/ppermute | solution.py:346
  6.0 4.7 %collective-permute-start.1 = (bf16[80,128]{1,0:T(8,128)(2,1)S(1)}, bf16[80,128]{1,0:T(8,128)(2,1)S(1)}, u32[]{:S(2)}, u32[]{:S(2)}) collective-permute-start(bf16[80,128]{1,0:T(8,128)(2,1)S(1)} %get-tuple-element.45), channel_id=1, source_target_pairs={{0,2},{1,3},{2,0},{3,1},{4,6},{5,7},{6,4},{7,5},{8,10},{9,11},{10,... | collective-permute-start | bytes 61448 | tf_op jit(solution)/shard_map/ppermute | solution.py:346
  6.0 4.7 %collective-permute-start.2 = (bf16[80,128]{1,0:T(8,128)(2,1)S(1)}, bf16[80,128]{1,0:T(8,128)(2,1)S(1)}, u32[]{:S(2)}, u32[]{:S(2)}) collective-permute-start(bf16[80,128]{1,0:T(8,128)(2,1)S(1)} %get-tuple-element.46), channel_id=1, source_target_pairs={{0,1},{1,0},{2,3},{3,2},{4,5},{5,4},{6,7},{7,6},{8,9},{9,8},{10,11... | collective-permute-start | bytes 61448 | tf_op jit(solution)/shard_map/ppermute | solution.py:346
  6.7 12.5 %copy-start.1 = (bf16[16,512,2,128]{3,2,1,0:T(2,128)(2,1)S(1)}, bf16[16,512,2,128]{3,2,1,0:T(2,128)(2,1)}, u32[]{:S(2)}) copy-start(bf16[16,512,2,128]{3,2,1,0:T(2,128)(2,1)} %param.15) | copy-start | bytes 12582916
  7.2 12.0 %copy-start = (bf16[16,512,2,128]{3,2,1,0:T(2,128)(2,1)S(1)}, bf16[16,512,2,128]{3,2,1,0:T(2,128)(2,1)}, u32[]{:S(2)}) copy-start(bf16[16,512,2,128]{3,2,1,0:T(2,128)(2,1)} %param.14) | copy-start | bytes 12582916
  7.2 12.0 %copy-start.4 = (s32[64]{0:T(128)S(1)}, s32[64]{0:T(128)}, u32[]{:S(2)}) copy-start(s32[64]{0:T(128)} %slot_ref.1) | copy-start | bytes 772
  7.2 12.0 %copy-start.5 = (s32[64]{0:T(128)S(1)}, s32[64]{0:T(128)}, u32[]{:S(2)}) copy-start(s32[64]{0:T(128)} %len_ref.1) | copy-start | bytes 772
  10.7 1.7 %collective-permute-start.4 = (bf16[4,64,128]{2,1,0:T(8,128)(2,1)S(1)}, bf16[4,64,128]{2,1,0:T(8,128)(2,1)S(1)}, u32[]{:S(2)}, u32[]{:S(2)}) collective-permute-start(bf16[4,64,128]{2,1,0:T(8,128)(2,1)S(1)} %get-tuple-element.50.refs_1_.q_ref), channel_id=1, source_target_pairs={{0,4},{4,0},{8,12},{12,8},{1,5},{5,1},{9,13},{13,9},{2,6},{6,2},{1... | collective-permute-start | bytes 196616 | tf_op jit(solution)/shard_map/ppermute | solution.py:349
  10.8 3.9 %collective-permute-start.3 = (bf16[4,64,128]{2,1,0:T(8,128)(2,1)S(1)}, bf16[4,64,128]{2,1,0:T(8,128)(2,1)S(1)}, u32[]{:S(2)}, u32[]{:S(2)}) collective-permute-start(bf16[4,64,128]{2,1,0:T(8,128)(2,1)S(1)} %get-tuple-element.50.refs_1_.q_ref), channel_id=1, source_target_pairs={{0,12},{4,8},{8,4},{12,0},{1,13},{5,9},{9,5},{13,1},{2,14},{6,10},... | collective-permute-start | bytes 196616 | tf_op jit(solution)/shard_map/ppermute | solution.py:349
  14.7 1.7 %collective-permute-start.5 = (bf16[528,128]{1,0:T(8,128)(2,1)S(1)}, bf16[528,128]{1,0:T(8,128)(2,1)S(1)}, u32[]{:S(2)}, u32[]{:S(2)}) collective-permute-start(bf16[528,128]{1,0:T(8,128)(2,1)S(1)} %bundle.1), channel_id=1, source_target_pairs={{0,4},{4,0},{8,12},{12,8},{1,5},{5,1},{9,13},{13,9},{2,6},{6,2},{1... | collective-permute-start | bytes 405512 | tf_op jit(solution)/shard_map/ppermute | solution.py:349
  16.2 1.3 %collective-permute-start.6 = (bf16[272,128]{1,0:T(8,128)(2,1)S(1)}, bf16[272,128]{1,0:T(8,128)(2,1)S(1)}, u32[]{:S(2)}, u32[]{:S(2)}) collective-permute-start(bf16[272,128]{1,0:T(8,128)(2,1)S(1)} %prefix_far.1), channel_id=1, source_target_pairs={{0,4},{4,0},{8,12},{12,8},{1,5},{5,1},{9,13},{13,9},{2,6},{6,2},{1... | collective-permute-start | bytes 208904 | tf_op jit(solution)/shard_map/ppermute | solution.py:349
  17.6 4.5 %collective-permute-start.7 = (bf16[272,128]{1,0:T(8,128)(2,1)S(1)}, bf16[272,128]{1,0:T(8,128)(2,1)S(1)}, u32[]{:S(2)}, u32[]{:S(2)}) collective-permute-start(bf16[272,128]{1,0:T(8,128)(2,1)S(1)} %join_partials.1), channel_id=1, source_target_pairs={{0,8},{4,12},{8,0},{12,4},{1,9},{5,13},{9,1},{13,5},{2,10},{6,14},... | collective-permute-start | bytes 208904 | tf_op jit(solution)/shard_map/ppermute | solution.py:349
  22.2 5.6 %collective-permute-start.8 = (bf16[64,128]{1,0:T(8,128)(2,1)S(1)}, bf16[64,128]{1,0:T(8,128)(2,1)S(1)}, u32[]{:S(2)}, u32[]{:S(2)}) collective-permute-start(bf16[64,128]{1,0:T(8,128)(2,1)S(1)} %get-tuple-element.71), channel_id=1, source_target_pairs={{0,3},{1,2},{2,1},{3,0},{4,7},{5,6},{6,5},{7,4},{8,11},{9,10},{10,... | collective-permute-start | bytes 49160 | tf_op jit(solution)/shard_map/ppermute | solution.py:346
  23.7 4.6 %collective-permute-start.9 = (bf16[64,128]{1,0:T(8,128)(2,1)S(1)}, bf16[64,128]{1,0:T(8,128)(2,1)S(1)}, u32[]{:S(2)}, u32[]{:S(2)}) collective-permute-start(bf16[64,128]{1,0:T(8,128)(2,1)S(1)} %get-tuple-element.72), channel_id=1, source_target_pairs={{0,2},{1,3},{2,0},{3,1},{4,6},{5,7},{6,4},{7,5},{8,10},{9,11},{10,... | collective-permute-start | bytes 49160 | tf_op jit(solution)/shard_map/ppermute | solution.py:346
  24.3 4.2 %collective-permute-start.10 = (bf16[64,128]{1,0:T(8,128)(2,1)S(1)}, bf16[64,128]{1,0:T(8,128)(2,1)S(1)}, u32[]{:S(2)}, u32[]{:S(2)}) collective-permute-start(bf16[64,128]{1,0:T(8,128)(2,1)S(1)} %get-tuple-element.73), channel_id=1, source_target_pairs={{0,1},{1,0},{2,3},{3,2},{4,5},{5,4},{6,7},{7,6},{8,9},{9,8},{10,11... | collective-permute-start | bytes 49160 | tf_op jit(solution)/shard_map/ppermute | solution.py:346
